TPU v7x, 32 devices: a whole 2x2x4 slice. The times are simulated.
32 devices in a mesh: section: 2 (over y), expert: 8 (over z, x), dp: 2 (over core).
Axes of the slice: x: 2, y: 2, z: 4, core: 2. Of those that a mesh axis runs over, the one named last changes fastest.
Arguments:
- tokens: bfloat16 [256, 3072], P(('expert', 'dp')), may hold values from -6 to 6
- grad_out: bfloat16 [256, 3072], P(('expert', 'dp')), may hold values from -6 to 6
- expert_ids: int32 [256, 2], P(('expert', 'dp')), may hold values from 0 to 3, as said below
- gate_probs: float32 [256, 2], P(('expert', 'dp')), may hold values from 0.1 to 0.9
- gate_weight: bfloat16 [3072, 32768], P('dp', ('expert', 'section')), may hold values from -0.109375 to 0.109375
- up_weight: bfloat16 [3072, 32768], P('dp', ('expert', 'section')), may hold values from -0.109375 to 0.109375
- down_weight: bfloat16 [3072, 32768], P('dp', ('expert', 'section')), may hold values from -0.0625 to 0.0625
Outputs:
- moe_out: bfloat16 [256, 3072], P(('expert', 'dp'), 'section')
- grad_tokens: bfloat16 [256, 3072], P(('expert', 'dp'), 'section')
- grad_gate: bfloat16 [3072, 32768], P('dp', ('expert', 'section'))
- grad_up: bfloat16 [3072, 32768], P('dp', ('expert', 'section'))
- grad_down: bfloat16 [3072, 32768], P('dp', ('expert', 'section'))
Inputs may be any that keep to these rules, and one draw needn't show every extreme that they name: `expert_ids`: each token names two different experts. Among the 16 tokens of one index of expert and dp (aligned blocks of 16 rows) no expert is named more than 12 times. For each index of dp one expert, drawn from the seed, is named exactly 12 times in every block of that index; block b has dp index b % 2.
All inputs are finite; a program needn't handle non-finite values.
Results may differ from a plain program's by a relative error of at most 0.015.
Values may be sent and summed in bfloat16 or wider, within the bound.
No kernel may reach another device: no remote copies, remote signals or barrier semaphores. Data moves between devices by JAX's collectives and lax.ppermute only.
A program may use at most 256 MiB of HBM per device.

v0:
```python
import jax
import jax.numpy as jnp
from jax import lax
from jax.sharding import PartitionSpec as P

EXP = 4
CAP = 12


def slot_tables(id_match, gates, capacity):
    chosen = jnp.any(id_match, axis=2)
    gate_share = jnp.sum(jnp.where(id_match, gates, 0.0), axis=2)
    slot_rank = jnp.cumsum(chosen.astype(jnp.int32), axis=1) - 1
    slot_index = jnp.arange(capacity, dtype=jnp.int32)
    pick_table = jnp.logical_and(
        chosen[:, None, :], slot_rank[:, None, :] == slot_index[None, :, None]
    )
    return (pick_table.astype(jnp.float32), gate_share)


def contract_rows(left, right):
    return lax.dot_general(
        left, right, (((0,), (0,)), ((), ())), preferred_element_type=jnp.float32
    )


def contract_cols(left, right):
    return lax.dot_general(
        left, right, (((1,), (1,)), ((), ())), preferred_element_type=jnp.float32
    )


def local(tokens, grad_out, expert_ids, gate_probs, gate_weight, up_weight, down_weight):
    expert_devices = lax.axis_size("expert")
    tok_count, model_width = tokens.shape
    capacity = CAP
    group_size = expert_devices // EXP
    gate_full, up_full, down_full = (
        lax.all_gather(gate_weight, "dp", axis=0, tiled=True),
        lax.all_gather(up_weight, "dp", axis=0, tiled=True),
        lax.all_gather(down_weight, "dp", axis=0, tiled=True),
    )
    own_match = expert_ids[None, :, :] == jnp.arange(EXP, dtype=jnp.int32)[:, None, None]
    own_picks, own_share = slot_tables(own_match, gate_probs[None, :, :], capacity)
    own_scaled = (own_share[:, :, None] * grad_out[None].astype(jnp.float32)).astype(jnp.bfloat16)
    pick_bf = own_picks.astype(jnp.bfloat16)
    send_tokens = jnp.einsum(
        "ect,td->ecd", pick_bf, tokens, preferred_element_type=jnp.float32
    ).astype(jnp.bfloat16)
    send_grads = jnp.einsum(
        "ect,etd->ecd", pick_bf, own_scaled, preferred_element_type=jnp.float32
    ).astype(jnp.bfloat16)
    send_tokens = jnp.repeat(send_tokens, group_size, axis=0)
    send_grads = jnp.repeat(send_grads, group_size, axis=0)
    recv_tokens, recv_grads = (
        lax.all_to_all(send_tokens, "expert", split_axis=0, concat_axis=0, tiled=True),
        lax.all_to_all(send_grads, "expert", split_axis=0, concat_axis=0, tiled=True),
    )
    slot_tokens = recv_tokens.reshape(-1, model_width)
    slot_grads = recv_grads.reshape(-1, model_width)
    gate_pre = jnp.dot(slot_tokens, gate_full, preferred_element_type=jnp.float32)
    up_pre = jnp.dot(slot_tokens, up_full, preferred_element_type=jnp.float32)
    sigmoid_gate = jax.nn.sigmoid(gate_pre)
    silu_value = gate_pre * sigmoid_gate
    activation = (silu_value * up_pre).astype(jnp.bfloat16)
    partial_out = contract_cols(activation, down_full)
    act_grad = jnp.dot(slot_grads, down_full, preferred_element_type=jnp.float32)
    up_grad = (act_grad * silu_value).astype(jnp.bfloat16)
    gate_grad = (act_grad * up_pre * sigmoid_gate * (1.0 + gate_pre * (1.0 - sigmoid_gate))).astype(
        jnp.bfloat16
    )
    partial_in = contract_cols(gate_grad, gate_full) + contract_cols(up_grad, up_full)
    summed_grads = lax.psum_scatter(
        jnp.concatenate(
            [
                contract_rows(slot_tokens, gate_grad),
                contract_rows(slot_tokens, up_grad),
                contract_rows(slot_grads, activation),
            ],
            axis=1,
        ).astype(jnp.bfloat16),
        "dp",
        scatter_dimension=0,
        tiled=True,
    ).astype(jnp.float32)
    hidden_dev = gate_weight.shape[1]
    grad_gate = summed_grads[:, :hidden_dev].astype(jnp.bfloat16)
    grad_up = summed_grads[:, hidden_dev : 2 * hidden_dev].astype(jnp.bfloat16)
    grad_down = summed_grads[:, 2 * hidden_dev :].astype(jnp.bfloat16)
    weighted_picks = own_picks * own_share[:, None, :]
    back_out, back_in = (
        lax.all_to_all(
            partial_out.reshape(expert_devices, capacity, model_width).astype(jnp.bfloat16),
            "expert",
            split_axis=0,
            concat_axis=0,
            tiled=True,
        ).astype(jnp.float32),
        lax.all_to_all(
            partial_in.reshape(expert_devices, capacity, model_width).astype(jnp.bfloat16),
            "expert",
            split_axis=0,
            concat_axis=0,
            tiled=True,
        ).astype(jnp.float32),
    )
    sum_out = back_out.reshape(EXP, group_size, capacity, model_width).sum(axis=1)
    sum_in = back_in.reshape(EXP, group_size, capacity, model_width).sum(axis=1)
    token_out = jnp.einsum("ect,ecd->td", weighted_picks, sum_out, precision=lax.Precision.HIGHEST)
    token_in = jnp.einsum("ect,ecd->td", own_picks, sum_in, precision=lax.Precision.HIGHEST)
    final_out, final_in = (
        lax.psum_scatter(
            token_out.astype(jnp.bfloat16), "section", scatter_dimension=1, tiled=True
        ).astype(jnp.float32),
        lax.psum_scatter(
            token_in.astype(jnp.bfloat16), "section", scatter_dimension=1, tiled=True
        ).astype(jnp.float32),
    )
    return (
        final_out.astype(jnp.bfloat16),
        final_in.astype(jnp.bfloat16),
        grad_gate,
        grad_up,
        grad_down,
    )


def solution(mesh):
    return jax.shard_map(
        local,
        mesh=mesh,
        in_specs=(
            P(("expert", "dp"), None),
            P(("expert", "dp"), None),
            P(("expert", "dp"), None),
            P(("expert", "dp"), None),
            P("dp", ("expert", "section")),
            P("dp", ("expert", "section")),
            P("dp", ("expert", "section")),
        ),
        out_specs=(
            P(("expert", "dp"), "section"),
            P(("expert", "dp"), "section"),
            P("dp", ("expert", "section")),
            P("dp", ("expert", "section")),
            P("dp", ("expert", "section")),
        ),
        check_vma=False,
    )
```

profile of v0, /device:TPU:1, one launch (start us, length us, event | category | flops | bytes accessed | tf_op | source)
XLA Modules:
  0.0 263.6 jit_solution(12528469794259314242)
XLA Ops:
  7.2 0.0 copy-start
  7.2 0.0 copy-start.4
  7.2 0.0 copy-start.2
  7.2 0.0 copy-start.3
  7.2 0.0 all-gather.6.cloned.1.call-start
  7.3 0.7 all-gather.6.cloned.1.call-update
  7.9 0.0 all-gather.4.cloned.1.call-start
  8.0 0.7 all-gather.4.cloned.1.call-update
  8.7 0.0 all-gather.8.cloned.1.call-start
  8.7 0.7 all-gather.8.cloned.1.call-update
  9.4 0.0 copy-done.4
  9.5 0.0 copy-done.2
  9.5 0.2 reduce_window_sum.11
  9.7 0.0 copy-done.3
  9.7 0.4 convolution_convert_fusion.4
  10.1 1.0 broadcast_in_dim.30
  11.1 6.4 %all-to-all-start.2 = ((bf16[8,12,3072]{2,1,0:T(8,128)(2,1)}), bf16[8,12,3072]{2,1,0:T(8,128)(2,1)S(1)}, u32[]{:S(2)}, u32[]{:S(2)}) async-start(bf16[8,12,3072]{2,1,0:T(8,128)(2,1)} %bitcast.4), calls=%async_computation.3 | async-start | bytes 1572864 | tf_op jit(solution)/shard_map/all_to_all | solution.py:57
  17.4 0.0 copy-done
  17.4 0.3 convolution_convert_fusion.5
  17.8 18.7 %all-to-all-done.2 = bf16[8,12,3072]{2,1,0:T(8,128)(2,1)S(1)} async-done(((bf16[8,12,3072]{2,1,0:T(8,128)(2,1)}), bf16[8,12,3072]{2,1,0:T(8,128)(2,1)S(1)}, u32[]{:S(2)}, u32[]{:S(2)}) %all-to-all-start.2) | async-done | bytes 589856 | tf_op jit(solution)/shard_map/all_to_all | solution.py:57
  36.5 1.0 broadcast_in_dim.18
  37.4 4.9 %all-to-all-start = ((bf16[8,12,3072]{2,1,0:T(8,128)(2,1)}), bf16[8,12,3072]{2,1,0:T(8,128)(2,1)S(1)}, u32[]{:S(2)}, u32[]{:S(2)}) async-start(bf16[8,12,3072]{2,1,0:T(8,128)(2,1)} %bitcast.1), calls=%async_computation | async-start | bytes 1572864 | tf_op jit(solution)/shard_map/all_to_all | solution.py:56
  42.3 0.0 reduce-scatter.8.cloned.1.call-start
  42.3 0.1 reshape.59
  42.5 19.1 %all-to-all-done = bf16[8,12,3072]{2,1,0:T(8,128)(2,1)S(1)} async-done(((bf16[8,12,3072]{2,1,0:T(8,128)(2,1)}), bf16[8,12,3072]{2,1,0:T(8,128)(2,1)S(1)}, u32[]{:S(2)}, u32[]{:S(2)}) %all-to-all-start) | async-done | bytes 589856 | tf_op jit(solution)/shard_map/all_to_all | solution.py:56
  61.6 0.1 reshape.55
  61.7 0.0 all-gather.6.cloned.1.call-done
  61.8 6.7 %fusion.25 = f32[96,2048]{1,0:T(8,128)S(1)} fusion(bf16[96,3072]{1,0:T(8,128)(2,1)S(1)} %reshape.55, bf16[3072,2048]{1,0:T(8,128)(2,1)} %all-gather.6.cloned.1.call-done), kind=kOutput, calls=%fused_computation.45 | convolution fusion | flops 1207959552 | bytes 13959168 | tf_op jit(solution)/shard_map/dot_general | solution.py:62
  68.4 0.0 all-gather.4.cloned.1.call-done
  68.5 7.6 %fusion.24 = f32[96,2048]{1,0:T(8,128)} fusion(bf16[96,3072]{1,0:T(8,128)(2,1)S(1)} %reshape.55, bf16[3072,2048]{1,0:T(8,128)(2,1)} %all-gather.4.cloned.1.call-done), kind=kOutput, calls=%fused_computation.44 | convolution fusion | flops 1207959552 | bytes 13959168 | tf_op jit(solution)/shard_map/dot_general | solution.py:61
  76.0 16.3 %all-gather.8.cloned.1.call-done = bf16[3072,2048]{1,0:T(8,128)(2,1)} async-done(((bf16[1536,2048]{1,0:T(8,128)(2,1)}), bf16[3072,2048]{1,0:T(8,128)(2,1)}) %all-gather.8.cloned.1.call-update) | async-done | bytes 12582928 | tf_op jit(solution)/shard_map/all_gather | solution.py:41
  92.3 7.2 %multiply_convert_fusion = (bf16[96,2048]{1,0:T(8,128)(2,1)S(1)}, bf16[96,2048]{1,0:T(8,128)(2,1)S(1)}, bf16[96,2048]{1,0:T(8,128)(2,1)S(1)}) fusion(f32[96,2048]{1,0:T(8,128)} %fusion.24, f32[96,2048]{1,0:T(8,128)S(1)} %fusion.25, bf16[96,3072]{1,0:T(8,128)(2,1)S(1)} %reshape.59, bf16[3072,2048]{1,0:T(8,128)(2,1)} %all-gather.8.cloned.1.call-done), kind=kOutput, calls=%fused_computation.15 | convolution fusion | flops 1210908672 | bytes 15925248 | tf_op jit(solution)/shard_map/dot_general | solution.py:67
  99.5 6.6 %convolution_convert_fusion = bf16[3072,2048]{0,1:T(8,128)(2,1)} fusion(bf16[96,3072]{1,0:T(8,128)(2,1)S(1)} %reshape.59, bf16[96,2048]{1,0:T(8,128)(2,1)S(1)} %get-tuple-element.25), kind=kOutput, calls=%fused_computation.1 | convolution fusion | flops 1214251008 | bytes 13565952 | tf_op jit(solution)/shard_map/dot_general | solution.py:22
  106.1 6.4 %convolution_convert_fusion.1 = bf16[3072,2048]{0,1:T(8,128)(2,1)} fusion(bf16[96,3072]{1,0:T(8,128)(2,1)S(1)} %reshape.55, bf16[96,2048]{1,0:T(8,128)(2,1)S(1)} %get-tuple-element.23), kind=kOutput, calls=%fused_computation.2 | convolution fusion | flops 1214251008 | bytes 13565952 | tf_op jit(solution)/shard_map/dot_general | solution.py:22
  112.5 6.3 %convolution_convert_fusion.2 = bf16[3072,2048]{0,1:T(8,128)(2,1)} fusion(bf16[96,3072]{1,0:T(8,128)(2,1)S(1)} %reshape.55, bf16[96,2048]{1,0:T(8,128)(2,1)S(1)} %get-tuple-element.24), kind=kOutput, calls=%fused_computation.3 | convolution fusion | flops 1214251008 | bytes 13565952 | tf_op jit(solution)/shard_map/dot_general | solution.py:22
  118.8 26.2 %pad_maximum_fusion = bf16[3072,6144]{0,1:T(8,128)(2,1)} fusion(bf16[3072,2048]{0,1:T(8,128)(2,1)} %convolution_convert_fusion, bf16[3072,2048]{0,1:T(8,128)(2,1)} %convolution_convert_fusion.1, bf16[3072,2048]{0,1:T(8,128)(2,1)} %convolution_convert_fusion.2), kind=kLoop, calls=%fused_computation | loop fusion | flops 113246208 | bytes 75497472 | tf_op jit(solution)/shard_map/concatenate | solution.py:74
  145.0 0.0 reduce-scatter.8.cloned.1.call-update
  145.0 8.5 %fusion.26 = f32[96,3072]{1,0:T(8,128)S(1)} fusion(bf16[96,2048]{1,0:T(8,128)(2,1)S(1)} %get-tuple-element.24, bf16[3072,2048]{1,0:T(8,128)(2,1)} %all-gather.4.cloned.1.call-done), kind=kOutput, calls=%fused_computation.46 | convolution fusion | flops 1207959552 | bytes 14155776 | tf_op jit(solution)/shard_map/dot_general | solution.py:28
  153.6 11.3 %fusion = bf16[96,3072]{1,0:T(8,128)(2,1)S(1)} fusion(f32[96,3072]{1,0:T(8,128)S(1)} %fusion.26, bf16[96,2048]{1,0:T(8,128)(2,1)S(1)} %get-tuple-element.23, bf16[3072,2048]{1,0:T(8,128)(2,1)} %all-gather.6.cloned.1.call-done), kind=kOutput, calls=%fused_computation.6 | convolution fusion | flops 1208549376 | bytes 14745600 | tf_op jit(solution)/shard_map/dot_general | solution.py:28
  164.9 1.0 convert_element_type.78
  165.9 5.7 %all-to-all-start.3 = ((bf16[8,12,3072]{2,1,0:T(8,128)(2,1)}), bf16[8,12,3072]{2,1,0:T(8,128)(2,1)S(1)}, u32[]{:S(2)}, u32[]{:S(2)}) async-start(bf16[8,12,3072]{2,1,0:T(8,128)(2,1)} %convert_element_type.78), calls=%async_computation.4 | async-start | bytes 1572864 | tf_op jit(solution)/shard_map/all_to_all | solution.py:99
  171.6 11.5 %convolution_convert_fusion.3 = bf16[96,3072]{1,0:T(8,128)(2,1)S(1)} fusion(bf16[96,2048]{1,0:T(8,128)(2,1)S(1)} %get-tuple-element.25, bf16[3072,2048]{1,0:T(8,128)(2,1)} %all-gather.8.cloned.1.call-done), kind=kOutput, calls=%fused_computation.5 | convolution fusion | flops 1208254464 | bytes 13565952 | tf_op jit(solution)/shard_map/dot_general | solution.py:28
  183.1 1.0 convert_element_type.70
  184.1 7.3 %all-to-all-done.3 = bf16[8,12,3072]{2,1,0:T(8,128)(2,1)S(1)} async-done(((bf16[8,12,3072]{2,1,0:T(8,128)(2,1)}), bf16[8,12,3072]{2,1,0:T(8,128)(2,1)S(1)}, u32[]{:S(2)}, u32[]{:S(2)}) %all-to-all-start.3) | async-done | bytes 589856 | tf_op jit(solution)/shard_map/all_to_all | solution.py:99
  191.4 4.2 %all-to-all-start.1 = ((bf16[8,12,3072]{2,1,0:T(8,128)(2,1)}), bf16[8,12,3072]{2,1,0:T(8,128)(2,1)S(1)}, u32[]{:S(2)}, u32[]{:S(2)}) async-start(bf16[8,12,3072]{2,1,0:T(8,128)(2,1)} %convert_element_type.70), calls=%async_computation.1 | async-start | bytes 1572864 | tf_op jit(solution)/shard_map/all_to_all | solution.py:92
  195.6 0.0 reduce-scatter.6.cloned.1.call-start
  195.6 0.1 convert_reduce_fusion
  195.8 1.2 fusion.2
  197.0 0.0 reduce-scatter.6.cloned.1.call-update
  197.0 0.0 reduce-scatter.4.cloned.1.call-start
  197.1 17.8 %all-to-all-done.1 = bf16[8,12,3072]{2,1,0:T(8,128)(2,1)S(1)} async-done(((bf16[8,12,3072]{2,1,0:T(8,128)(2,1)}), bf16[8,12,3072]{2,1,0:T(8,128)(2,1)S(1)}, u32[]{:S(2)}, u32[]{:S(2)}) %all-to-all-start.1) | async-done | bytes 589856 | tf_op jit(solution)/shard_map/all_to_all | solution.py:92
  214.9 0.1 convert_reduce_fusion.1
  215.0 1.7 fusion.1
  216.7 0.0 reduce-scatter.4.cloned.1.call-update
  216.7 0.0 reduce-scatter.8.cloned.1.call-done
  216.7 14.2 %fusion.23 = (bf16[1536,2048]{0,1:T(8,128)(2,1)}, bf16[1536,2048]{0,1:T(8,128)(2,1)}, bf16[1536,2048]{0,1:T(8,128)(2,1)}) fusion(bf16[1536,6144]{0,1:T(8,128)(2,1)} %reduce-scatter.8.cloned.1.call-done), kind=kLoop, calls=%fused_computation.43 | loop fusion | bytes 37748736 | tf_op jit(solution)/shard_map/slice | solution.py:89
  230.9 8.6 %copy.30 = bf16[1536,2048]{1,0:T(8,128)(2,1)} copy(bf16[1536,2048]{0,1:T(8,128)(2,1)} %get-tuple-element.20) | data formatting | bytes 12582912
  239.5 0.0 copy-start.1
  239.5 8.6 %copy.29 = bf16[1536,2048]{1,0:T(8,128)(2,1)} copy(bf16[1536,2048]{0,1:T(8,128)(2,1)} %get-tuple-element.21) | data formatting | bytes 12582912
  248.2 8.6 %copy.28 = bf16[1536,2048]{1,0:T(8,128)(2,1)} copy(bf16[1536,2048]{0,1:T(8,128)(2,1)} %get-tuple-element.22) | data formatting | bytes 12582912
  256.8 0.0 reduce-scatter.6.cloned.1.call-done
  256.8 0.0 reduce-scatter.4.cloned.1.call-done
  256.8 0.0 copy-done.1
  (5 shorter events, 0.1 us)
Async XLA Ops:
  7.2 10.3 %copy-start = (bf16[16,3072]{1,0:T(8,128)(2,1)S(1)}, bf16[16,3072]{1,0:T(8,128)(2,1)}, u32[]{:S(2)}) copy-start(bf16[16,3072]{1,0:T(8,128)(2,1)} %param.7) | copy-start | bytes 294916
  7.2 2.3 copy-start.4
  7.2 2.3 copy-start.2
  7.2 2.5 copy-start.3
  7.2 54.5 %all-gather.6.cloned.1.call-start = ((), (), s32[]{:S(2)}) async-start(), calls=%async_computation.8 | async-start | bytes 18874368 | tf_op jit(solution)/shard_map/all_gather | solution.py:40
  7.9 60.5 %all-gather.4.cloned.1.call-start = ((), (), s32[]{:S(2)}) async-start(), calls=%async_computation.7 | async-start | bytes 18874368 | tf_op jit(solution)/shard_map/all_gather | solution.py:39
  8.7 83.6 %all-gather.8.cloned.1.call-start = ((), (), s32[]{:S(2)}) async-start(), calls=%async_computation.9 | async-start | bytes 18874368 | tf_op jit(solution)/shard_map/all_gather | solution.py:41
  11.1 25.4 %all-to-all-start.2 = ((bf16[8,12,3072]{2,1,0:T(8,128)(2,1)}), bf16[8,12,3072]{2,1,0:T(8,128)(2,1)S(1)}, u32[]{:S(2)}, u32[]{:S(2)}) async-start(bf16[8,12,3072]{2,1,0:T(8,128)(2,1)} %bitcast.4), calls=%async_computation.3 | async-start | bytes 1572864 | tf_op jit(solution)/shard_map/all_to_all | solution.py:57
  37.4 24.2 %all-to-all-start = ((bf16[8,12,3072]{2,1,0:T(8,128)(2,1)}), bf16[8,12,3072]{2,1,0:T(8,128)(2,1)S(1)}, u32[]{:S(2)}, u32[]{:S(2)}) async-start(bf16[8,12,3072]{2,1,0:T(8,128)(2,1)} %bitcast.1), calls=%async_computation | async-start | bytes 1572864 | tf_op jit(solution)/shard_map/all_to_all | solution.py:56
  42.3 174.4 %reduce-scatter.8.cloned.1.call-start = ((), (), s32[]{:S(2)}) async-start(), calls=%async_computation.12 | async-start | bytes 56623104 | tf_op jit(solution)/shard_map/reduce_scatter | solution.py:73
  165.9 25.5 %all-to-all-start.3 = ((bf16[8,12,3072]{2,1,0:T(8,128)(2,1)}), bf16[8,12,3072]{2,1,0:T(8,128)(2,1)S(1)}, u32[]{:S(2)}, u32[]{:S(2)}) async-start(bf16[8,12,3072]{2,1,0:T(8,128)(2,1)} %convert_element_type.78), calls=%async_computation.4 | async-start | bytes 1572864 | tf_op jit(solution)/shard_map/all_to_all | solution.py:99
  191.4 23.5 %all-to-all-start.1 = ((bf16[8,12,3072]{2,1,0:T(8,128)(2,1)}), bf16[8,12,3072]{2,1,0:T(8,128)(2,1)S(1)}, u32[]{:S(2)}, u32[]{:S(2)}) async-start(bf16[8,12,3072]{2,1,0:T(8,128)(2,1)} %convert_element_type.70), calls=%async_computation.1 | async-start | bytes 1572864 | tf_op jit(solution)/shard_map/all_to_all | solution.py:92
  195.6 61.2 %reduce-scatter.6.cloned.1.call-start = ((), (), s32[]{:S(2)}) async-start(), calls=%async_computation.11 | async-start | bytes 147456 | tf_op jit(solution)/shard_map/reduce_scatter | solution.py:115
  197.0 59.7 %reduce-scatter.4.cloned.1.call-start = ((), (), s32[]{:S(2)}) async-start(), calls=%async_computation.10 | async-start | bytes 147456 | tf_op jit(solution)/shard_map/reduce_scatter | solution.py:112
  239.5 17.3 %copy-start.1 = (bf16[16,3072]{1,0:T(8,128)(2,1)S(1)}, bf16[16,3072]{1,0:T(8,128)(2,1)}, u32[]{:S(2)}) copy-start(bf16[16,3072]{1,0:T(8,128)(2,1)} %param.7) | copy-start | bytes 294916
Sparse Core Ops, SparseCore 0:
  9.6 27.3 all-gather.5
  38.6 26.0 all-gather.3
  66.2 26.0 all-gather.7
  145.1 50.5 reduce-scatter.7
  198.9 11.3 reduce-scatter.5
  216.8 9.9 reduce-scatter.3
where the time goes:
time: 267 us; the launch traced here: 264 us
  waiting for transfers between devices  81.4 us (30%)
  matrix products  75.8 us (28%)
  local copies, waits for them, and re-layouts  44.3 us (17%)
  other arithmetic  26.7 us (10%)
  starting transfers between devices  21.3 us (8%)
  between operations  14.3 us (5%)
    dot_general x3, matrix products, contract_cols(): lax.dot_general(left, right, (((1,), (1,)), ((), ())), preferred_element_...  31.4 us
    concatenate x1, other arithmetic, local(): jnp.concatenate([contract_rows(slot_tokens, gate_grad), contract_rows(slo...  26.2 us
    unnamed x13, local copies, waits for them, and re-layouts  25.9 us
    dot_general x3, matrix products, contract_rows(): lax.dot_general(left, right, (((0,), (0,)), ((), ())), preferred_element_...  19.3 us
    all_to_all x1, waiting for transfers between devices, local(): lax.all_to_all(send_tokens, 'expert', split_axis=0, concat_axis=0, tiled=...  19.1 us
    all_to_all x1, waiting for transfers between devices, local(): lax.all_to_all(send_grads, 'expert', split_axis=0, concat_axis=0, tiled=T...  18.7 us
    all_to_all x1, waiting for transfers between devices, local(): lax.all_to_all(partial_out.reshape(expert_devices, capacity, model_width)...  17.8 us
    all_gather x1, waiting for transfers between devices, local(): lax.all_gather(down_weight, 'dp', axis=0, tiled=True)  16.3 us
  transfers between devices with their start and end apart: 10, of which 5 were waited for; matrix products, arithmetic and copies ran while one was open for 36% of the time, Pallas kernels for 0%

commit v1 on v0

v1 whole, which is shorter than its diff:
```python
import jax
import jax.numpy as jnp
from jax import lax
from jax.sharding import PartitionSpec as P

EXP = 4
CAP = 12
BF = jnp.bfloat16
F32 = jnp.float32


def contract_rows(left, right):
    return lax.dot_general(left, right, (((0,), (0,)), ((), ())), preferred_element_type=F32)


def contract_cols(left, right):
    return lax.dot_general(left, right, (((1,), (1,)), ((), ())), preferred_element_type=F32)


def slot_tables(id_match, capacity):
    chosen = jnp.any(id_match, axis=2)
    slot_rank = jnp.cumsum(chosen.astype(jnp.int32), axis=1) - 1
    slot_index = jnp.arange(capacity, dtype=jnp.int32)
    return jnp.logical_and(
        chosen[:, None, :], slot_rank[:, None, :] == slot_index[None, :, None]
    )


def general(tokens, grad_out, expert_ids, gate_probs, gate_weight, up_weight, down_weight):
    expert_devices = lax.axis_size("expert")
    model_width = tokens.shape[1]
    group_size = expert_devices // EXP
    gate_full, up_full, down_full = (
        lax.all_gather(weight, "dp", axis=0, tiled=True)
        for weight in (gate_weight, up_weight, down_weight)
    )
    own_match = expert_ids[None, :, :] == jnp.arange(EXP, dtype=jnp.int32)[:, None, None]
    own_picks = slot_tables(own_match, CAP).astype(F32)
    own_share = jnp.sum(jnp.where(own_match, gate_probs[None, :, :], 0.0), axis=2)
    own_scaled = (own_share[:, :, None] * grad_out[None].astype(F32)).astype(BF)
    pick_bf = own_picks.astype(BF)
    send_tokens = jnp.einsum("ect,td->ecd", pick_bf, tokens, preferred_element_type=F32).astype(BF)
    send_grads = jnp.einsum("ect,etd->ecd", pick_bf, own_scaled, preferred_element_type=F32).astype(BF)

    def swap(rows):
        return lax.all_to_all(rows, "expert", split_axis=0, concat_axis=0, tiled=True)

    slot_tokens = swap(jnp.repeat(send_tokens, group_size, axis=0)).reshape(-1, model_width)
    slot_grads = swap(jnp.repeat(send_grads, group_size, axis=0)).reshape(-1, model_width)
    gate_pre = jnp.dot(slot_tokens, gate_full, preferred_element_type=F32)
    up_pre = jnp.dot(slot_tokens, up_full, preferred_element_type=F32)
    act_grad = jnp.dot(slot_grads, down_full, preferred_element_type=F32)
    activation, up_grad, gate_grad = pointwise(gate_pre, up_pre, act_grad)
    partial_out = contract_cols(activation, down_full)
    partial_in = contract_cols(gate_grad, gate_full) + contract_cols(up_grad, up_full)
    summed_grads = lax.psum_scatter(
        jnp.concatenate(
            [
                contract_rows(slot_tokens, gate_grad),
                contract_rows(slot_tokens, up_grad),
                contract_rows(slot_grads, activation),
            ],
            axis=1,
        ).astype(BF),
        "dp",
        scatter_dimension=0,
        tiled=True,
    )
    hidden = gate_weight.shape[1]
    weighted_picks = own_picks * own_share[:, None, :]
    back_out = swap(partial_out.reshape(expert_devices, CAP, model_width).astype(BF)).astype(F32)
    back_in = swap(partial_in.reshape(expert_devices, CAP, model_width).astype(BF)).astype(F32)
    sum_out = back_out.reshape(EXP, group_size, CAP, model_width).sum(axis=1)
    sum_in = back_in.reshape(EXP, group_size, CAP, model_width).sum(axis=1)
    token_out = jnp.einsum("ect,ecd->td", weighted_picks, sum_out, precision=lax.Precision.HIGHEST)
    token_in = jnp.einsum("ect,ecd->td", own_picks, sum_in, precision=lax.Precision.HIGHEST)
    return (
        lax.psum_scatter(token_out.astype(BF), "section", scatter_dimension=1, tiled=True),
        lax.psum_scatter(token_in.astype(BF), "section", scatter_dimension=1, tiled=True),
        summed_grads[:, :hidden],
        summed_grads[:, hidden : 2 * hidden],
        summed_grads[:, 2 * hidden :],
    )


def pointwise(gate_pre, up_pre, act_grad):
    sigmoid_gate = jax.nn.sigmoid(gate_pre)
    silu_value = gate_pre * sigmoid_gate
    activation = (silu_value * up_pre).astype(BF)
    up_grad = (act_grad * silu_value).astype(BF)
    gate_grad = (act_grad * up_pre * sigmoid_gate * (1.0 + gate_pre * (1.0 - sigmoid_gate))).astype(BF)
    return activation, up_grad, gate_grad


def swap_expert(rows):
    size = lax.axis_size("expert")
    return lax.ppermute(rows, "expert", [(i, i ^ 1) for i in range(size)])


def swap_section(rows):
    return lax.ppermute(rows, "section", [(0, 1), (1, 0)])


def swap_dp(rows):
    return lax.ppermute(rows, "dp", [(0, 1), (1, 0)])


def turn(rows, shift):
    size = lax.axis_size("expert")
    pairs = []
    for s in range(2):
        for i in range(size):
            for d in range(2):
                j = (i + 2 * shift) % size
                pairs.append(((s * size + i) * 2 + d, (d * size + j) * 2 + s))
    return lax.ppermute(rows, ("section", "expert", "dp"), pairs)


def paired(tokens, grad_out, expert_ids, gate_probs, gate_weight, up_weight, down_weight):
    half = gate_weight.shape[0]
    count = tokens.shape[0]
    section = lax.axis_index("section")
    plane = lax.axis_index("expert") // 2
    experts = (plane + jnp.arange(EXP, dtype=jnp.int32)) % EXP
    match = expert_ids[None, :, :] == experts[:, None, None]
    picks = slot_tables(match, CAP)
    share = jnp.sum(jnp.where(match, gate_probs[None, :, :], 0.0), axis=2)
    slot_gate = jnp.sum(jnp.where(picks, share[:, None, :], 0.0), axis=2)
    none = jnp.zeros_like(picks)
    pick_both = jnp.concatenate(
        [jnp.concatenate([picks, none], axis=2), jnp.concatenate([none, picks], axis=2)], axis=1
    ).reshape(EXP * 2 * CAP, 2 * count).astype(BF)
    scale = jnp.concatenate([jnp.ones_like(slot_gate), slot_gate], axis=1).reshape(-1, 1)
    rows = jnp.concatenate([tokens, grad_out], axis=0)
    rows = lax.dynamic_slice_in_dim(rows, section * half, half, axis=1)
    payload = (jnp.dot(pick_both, rows, preferred_element_type=F32) * scale).astype(BF)
    got = [turn(payload[k * 2 * CAP : (k + 1) * 2 * CAP], k) for k in range(EXP)]
    own_t = jnp.concatenate([g[:CAP] for g in got], axis=0)
    own_g = jnp.concatenate([g[CAP:] for g in got], axis=0)
    n = EXP * CAP
    xt = swap_expert(own_t)
    yg = swap_section(own_g)
    yt = swap_section(jnp.concatenate([own_t, xt], axis=0))
    two_g = jnp.concatenate([own_g, yg], axis=0)
    xg = swap_expert(two_g)
    slot_t = jnp.concatenate([own_t, yt[:n], xt, yt[n:]], axis=0)
    slot_g = jnp.concatenate([two_g, xg], axis=0)

    gate_p = jnp.dot(slot_t, gate_weight, preferred_element_type=F32)
    up_p = jnp.dot(slot_t, up_weight, preferred_element_type=F32)
    act_p = jnp.dot(slot_g, down_weight, preferred_element_type=F32)
    gate_pre = gate_p + swap_dp(gate_p.astype(BF)).astype(F32)
    up_pre = up_p + swap_dp(up_p.astype(BF)).astype(F32)
    act_grad = act_p + swap_dp(act_p.astype(BF)).astype(F32)
    activation, up_grad, gate_grad = pointwise(gate_pre, up_pre, act_grad)

    part_out = contract_cols(activation, down_weight).astype(BF)
    part_in = (contract_cols(gate_grad, gate_weight) + contract_cols(up_grad, up_weight)).astype(BF)
    grad_gate = contract_rows(slot_t, gate_grad).astype(BF)
    grad_up = contract_rows(slot_t, up_grad).astype(BF)
    grad_down = contract_rows(slot_g, activation).astype(BF)

    def add(a, b):
        return (a.astype(F32) + b.astype(F32)).astype(BF)

    two_out = add(part_out[: 2 * n], swap_expert(part_out[2 * n :]))
    one_out = add(two_out[:n], swap_section(two_out[n:]))
    two_in = add(
        jnp.concatenate([part_in[:n], part_in[2 * n : 3 * n]], axis=0),
        swap_section(jnp.concatenate([part_in[n : 2 * n], part_in[3 * n :]], axis=0)),
    )
    one_in = add(two_in[:n], swap_expert(two_in[n:]))
    back = [
        turn(
            jnp.concatenate(
                [one_out[k * CAP : (k + 1) * CAP], one_in[k * CAP : (k + 1) * CAP]], axis=0
            ),
            -k,
        )
        for k in range(EXP)
    ]
    back = jnp.concatenate(back, axis=0)
    per_choice = [
        jnp.logical_and(picks, match[:, None, :, j]) for j in range(2)
    ]
    blank = jnp.zeros_like(picks)
    spread = jnp.concatenate(
        [
            jnp.concatenate([per_choice[0], per_choice[1], blank], axis=2),
            jnp.concatenate([blank, blank, picks], axis=2),
        ],
        axis=1,
    ).reshape(EXP * 2 * CAP, 3 * count).astype(BF)
    found = contract_rows(spread, back)
    moe_out = (
        gate_probs[:, 0:1] * found[:count] + gate_probs[:, 1:2] * found[count : 2 * count]
    ).astype(BF)
    grad_tokens = found[2 * count :].astype(BF)
    return moe_out, grad_tokens, grad_gate, grad_up, grad_down


def solution(mesh):
    sizes = mesh.shape
    pairs = sizes["section"] == 2 and sizes["dp"] == 2 and sizes["expert"] == 2 * EXP
    return jax.shard_map(
        paired if pairs else general,
        mesh=mesh,
        in_specs=(
            P(("expert", "dp"), None),
            P(("expert", "dp"), None),
            P(("expert", "dp"), None),
            P(("expert", "dp"), None),
            P("dp", ("expert", "section")),
            P("dp", ("expert", "section")),
            P("dp", ("expert", "section")),
        ),
        out_specs=(
            P(("expert", "dp"), "section"),
            P(("expert", "dp"), "section"),
            P("dp", ("expert", "section")),
            P("dp", ("expert", "section")),
            P("dp", ("expert", "section")),
        ),
        check_vma=False,
    )
```

time: 267 us -> 112 us (0.42)
  waiting for transfers between devices: 81.4 us -> 25.6 us
  matrix products: 75.8 us -> 34.5 us
  local copies, waits for them, and re-layouts: 44.3 us -> 15.4 us
  other arithmetic: 26.7 us -> 5.37 us
  between operations: 14.3 us -> 1.2 us
  starting transfers between devices: 21.3 us -> 28.7 us
    all_to_all x4 -> x0, waiting for transfers between devices: 62.9 us -> none  [the longest x1 19.1 us: local(): lax.all_to_all(send_tokens, 'expert', split_axis=0, concat_axis=0, tiled=...]
    ppermute x0 -> x19, starting transfers between devices: none -> 28.7 us  [the longest x8 18.8 us: turn(): return lax.ppermute(rows, ('section', 'expert', 'dp'), pairs)]
    concatenate x1 -> x9, other arithmetic: 26.2 us -> 0.4 us  [the longest x1 0.1 us: paired(): jnp.concatenate([jnp.concatenate([per_choice[0], per_choice[1], blank], a...]
    unnamed x13 -> x27, local copies, waits for them, and re-layouts: 25.9 us -> 0.17 us
    ppermute x0 -> x19, waiting for transfers between devices: none -> 25.6 us  [the longest x4 10 us: swap_expert(): return lax.ppermute(rows, 'expert', [(i, i ^ 1) for i in range(size)])]
    dot_general x3, matrix products: 31.4 us -> 6.64 us  [contract_cols(): lax.dot_general(left, right, (((1,), (1,)), ((), ())), preferred_element_...]
    all_to_all x4 -> x0, starting transfers between devices: 21 us -> none  [the longest x1 6.35 us: local(): lax.all_to_all(send_grads, 'expert', split_axis=0, concat_axis=0, tiled=T...]
    all_gather x3 -> x0, waiting for transfers between devices: 16.3 us -> none  [the longest x1 16.3 us: local(): lax.all_gather(down_weight, 'dp', axis=0, tiled=True)]
  transfers between devices with their start and end apart: 10 -> 19, of which waited for: 5 -> 9; matrix products, arithmetic and copies ran while one was open for 36% -> 37% of each run, Pallas kernels for 0% -> 0%
where the time goes in v1:
time: 112 us; the launch traced here: 111 us
  matrix products  34.5 us (31%)
  starting transfers between devices  28.7 us (26%)
  waiting for transfers between devices  25.6 us (23%)
  local copies, waits for them, and re-layouts  15.4 us (14%)
  other arithmetic  5.37 us (5%)
  between operations  1.2 us (1%)
    ppermute x8, starting transfers between devices, turn(): return lax.ppermute(rows, ('section', 'expert', 'dp'), pairs)  18.8 us
    dot_general x4, matrix products, contract_rows(): lax.dot_general(left, right, (((0,), (0,)), ((), ())), preferred_element_...  14.1 us
    ppermute x4, waiting for transfers between devices, swap_expert(): return lax.ppermute(rows, 'expert', [(i, i ^ 1) for i in range(size)])  10 us
    ppermute x4, waiting for transfers between devices, swap_section(): return lax.ppermute(rows, 'section', [(0, 1), (1, 0)])  9.91 us
    dot_general x3, matrix products, contract_cols(): lax.dot_general(left, right, (((1,), (1,)), ((), ())), preferred_element_...  6.64 us
    concatenate x1, local copies, waits for them, and re-layouts, paired(): slot_t = jnp.concatenate([own_t, yt[:n], xt, yt[n:]], axis=0)  6.36 us
    ppermute x3, starting transfers between devices, swap_dp(): return lax.ppermute(rows, 'dp', [(0, 1), (1, 0)])  5.08 us
    concatenate x1, local copies, waits for them, and re-layouts, paired(): yt = swap_section(jnp.concatenate([own_t, xt], axis=0))  4.89 us
  transfers between devices with their start and end apart: 19, of which 9 were waited for; matrix products, arithmetic and copies ran while one was open for 37% of the time, Pallas kernels for 0%

profile of v1, /device:TPU:1, one launch (start us, length us, event | category | flops | bytes accessed | tf_op | source)
XLA Modules:
  0.0 110.8 jit_solution(6864673289220548185)
XLA Ops:
  0.7 0.8 select_reduce_fusion.1
  1.5 0.2 reduce_window_sum.11
  1.7 0.1 select_reduce_fusion
  1.8 0.1 copy.23
  1.9 0.1 concatenate.75.clone
  1.9 0.1 mul.57
  2.0 0.6 broadcast_and_fusion.1
  2.6 0.1 pad_add_fusion
  2.7 0.1 copy.21
  2.8 0.1 reshape.49
  2.9 1.1 fusion.1
  4.1 5.7 %collective-permute-start.3 = (bf16[24,1536]{1,0:T(8,128)(2,1)S(1)}, bf16[24,1536]{1,0:T(8,128)(2,1)S(1)}, u32[]{:S(2)}, u32[]{:S(2)}) collective-permute-start(bf16[24,1536]{1,0:T(8,128)(2,1)S(1)} %get-tuple-element.16), channel_id=1, source_target_pairs={{0,12},{1,28},{2,14},{3,30},{4,0},{5,16},{6,2},{7,18},{8,4},{9,20}... | collective-permute-start | bytes 221192 | tf_op jit(solution)/shard_map/ppermute | solution.py:116
  9.8 1.6 %collective-permute-start.1 = (bf16[24,1536]{1,0:T(8,128)(2,1)S(1)}, bf16[24,1536]{1,0:T(8,128)(2,1)S(1)}, u32[]{:S(2)}, u32[]{:S(2)}) collective-permute-start(bf16[24,1536]{1,0:T(8,128)(2,1)S(1)} %get-tuple-element.18), channel_id=1, source_target_pairs={{0,4},{1,20},{2,6},{3,22},{4,8},{5,24},{6,10},{7,26},{8,12},{9,28}... | collective-permute-start | bytes 221192 | tf_op jit(solution)/shard_map/ppermute | solution.py:116
  11.4 2.1 %collective-permute-start = (bf16[24,1536]{1,0:T(8,128)(2,1)S(1)}, bf16[24,1536]{1,0:T(8,128)(2,1)S(1)}, u32[]{:S(2)}, u32[]{:S(2)}) collective-permute-start(bf16[24,1536]{1,0:T(8,128)(2,1)S(1)} %get-tuple-element.19), channel_id=1, source_target_pairs={{0,0},{1,16},{2,2},{3,18},{4,4},{5,20},{6,6},{7,22},{8,8},{9,24},{... | collective-permute-start | bytes 221192 | tf_op jit(solution)/shard_map/ppermute | solution.py:116
  13.6 3.1 %collective-permute-done.2 = bf16[24,1536]{1,0:T(8,128)(2,1)S(1)} collective-permute-done((bf16[24,1536]{1,0:T(8,128)(2,1)S(1)}, bf16[24,1536]{1,0:T(8,128)(2,1)S(1)}, u32[]{:S(2)}, u32[]{:S(2)}) %collective-permute-start.2) | collective-permute-done | bytes 73760 | tf_op jit(solution)/shard_map/ppermute | solution.py:116
  16.8 0.7 collective-permute-done
  17.5 0.1 collective-permute-start.10
  17.6 5.3 %collective-permute-done.10 = bf16[48,1536]{1,0:T(8,128)(2,1)S(1)} collective-permute-done((bf16[48,1536]{1,0:T(8,128)(2,1)S(1)}, bf16[48,1536]{1,0:T(8,128)(2,1)S(1)}, u32[]{:S(2)}, u32[]{:S(2)}) %collective-permute-start.10) | collective-permute-done | bytes 147488 | tf_op jit(solution)/shard_map/ppermute | solution.py:101
  22.9 0.4 concatenate.80
  23.3 1.3 %collective-permute-start.11 = (bf16[96,1536]{1,0:T(8,128)(2,1)S(1)}, bf16[96,1536]{1,0:T(8,128)(2,1)S(1)}, u32[]{:S(2)}, u32[]{:S(2)}) collective-permute-start(bf16[96,1536]{1,0:T(8,128)(2,1)S(1)} %concatenate.80), channel_id=1, source_target_pairs={{0,2},{2,0},{4,6},{6,4},{8,10},{10,8},{12,14},{14,12},{1,3},{3,1},... | collective-permute-start | bytes 884744 | tf_op jit(solution)/shard_map/ppermute | solution.py:97
  24.6 0.3 collective-permute-start.4
  24.9 9.1 %collective-permute-done.4 = bf16[48,1536]{1,0:T(8,128)(2,1)S(1)} collective-permute-done((bf16[48,1536]{1,0:T(8,128)(2,1)S(1)}, bf16[48,1536]{1,0:T(8,128)(2,1)S(1)}, u32[]{:S(2)}, u32[]{:S(2)}) %collective-permute-start.4) | collective-permute-done | bytes 147488 | tf_op jit(solution)/shard_map/ppermute | solution.py:97
  34.0 4.9 %concatenate.77 = bf16[96,1536]{1,0:T(8,128)(2,1)} concatenate(bf16[12,1536]{1,0:T(8,128)(2,1)S(1)} %get-tuple-element.35, bf16[12,1536]{1,0:T(8,128)(2,1)S(1)} %get-tuple-element.33, bf16[12,1536]{1,0:T(8,128)(2,1)S(1)} %get-tuple-element.31, bf16[12,1536]{1,0:T(8,128)(2,1)S(1)} %get-tuple-element.29, bf16[48,1536]{1,0:T(8,128)(2,1)S(1)} %collective-permute-done.4), dimensions={0} | concatenate | bytes 589824 | tf_op jit(solution)/shard_map/concatenate | solution.py:143
  38.9 0.5 concatenate.81
  39.5 4.2 %fusion.31 = (bf16[192,2048]{1,0:T(8,128)(2,1)S(1)}, f32[192,2048]{1,0:T(8,128)S(1)}) fusion(bf16[192,1536]{1,0:T(8,128)(2,1)S(1)} %concatenate.81, bf16[1536,2048]{1,0:T(8,128)(2,1)} %param.13), kind=kOutput, calls=%fused_computation.75 | convolution fusion | flops 1208352768 | bytes 9240576 | tf_op jit(solution)/shard_map/dot_general | solution.py:151
  43.7 2.0 %collective-permute-start.12 = (bf16[192,2048]{1,0:T(8,128)(2,1)S(1)}, bf16[192,2048]{1,0:T(8,128)(2,1)}, u32[]{:S(2)}, u32[]{:S(2)}) collective-permute-start(bf16[192,2048]{1,0:T(8,128)(2,1)S(1)} %get-tuple-element.47), channel_id=1, source_target_pairs={{0,1},{1,0},{2,3},{3,2},{4,5},{5,4},{6,7},{7,6},{8,9},{9,8},{10,11... | collective-permute-start | bytes 2359304 | tf_op jit(solution)/shard_map/ppermute | solution.py:105
  45.7 0.2 collective-permute-done.5
  45.8 1.7 %fusion.21 = (bf16[48,1536]{1,0:T(8,128)(2,1)}, bf16[48,1536]{1,0:T(8,128)(2,1)}) fusion(bf16[96,1536]{1,0:T(8,128)(2,1)} %collective-permute-done.5), kind=kLoop, calls=%fused_computation.65 | loop fusion | bytes 589824 | tf_op jit(solution)/shard_map/slice | solution.py:146
  47.5 6.4 %concatenate.78 = bf16[192,1536]{1,0:T(8,128)(2,1)S(1)} concatenate(bf16[12,1536]{1,0:T(8,128)(2,1)} %copy-done.3, bf16[12,1536]{1,0:T(8,128)(2,1)} %copy-done.2, bf16[12,1536]{1,0:T(8,128)(2,1)} %copy-done.1, bf16[12,1536]{1,0:T(8,128)(2,1)} %copy-done, bf16[48,1536]{1,0:T(8,128)(2,1)} %get-tuple-element.15, bf16[48,1536]{1,0:T(8,128)(2,1)} %copy-done.4, ...), dimensions={0} | concatenate | bytes 1179648 | tf_op jit(solution)/shard_map/concatenate | solution.py:146
  53.9 0.0 slice-start
  53.9 4.3 %fusion.30 = (bf16[192,2048]{1,0:T(8,128)(2,1)S(1)}, f32[192,2048]{1,0:T(8,128)S(1)}) fusion(bf16[192,1536]{1,0:T(8,128)(2,1)S(1)} %concatenate.78, bf16[1536,2048]{1,0:T(8,128)(2,1)} %param.11), kind=kOutput, calls=%fused_computation.74 | convolution fusion | flops 1208352768 | bytes 9240576 | tf_op jit(solution)/shard_map/dot_general | solution.py:149
  58.3 0.0 slice-start.1
  58.3 2.9 %collective-permute-start.6 = (bf16[192,2048]{1,0:T(8,128)(2,1)S(1)}, bf16[192,2048]{1,0:T(8,128)(2,1)S(1)}, u32[]{:S(2)}, u32[]{:S(2)}) collective-permute-start(bf16[192,2048]{1,0:T(8,128)(2,1)S(1)} %get-tuple-element.45), channel_id=1, source_target_pairs={{0,1},{1,0},{2,3},{3,2},{4,5},{5,4},{6,7},{7,6},{8,9},{9,8},{10,11... | collective-permute-start | bytes 2359304 | tf_op jit(solution)/shard_map/ppermute | solution.py:105
  61.2 4.2 %fusion.29 = (bf16[192,2048]{1,0:T(8,128)(2,1)S(1)}, f32[192,2048]{1,0:T(8,128)S(1)}) fusion(bf16[192,1536]{1,0:T(8,128)(2,1)S(1)} %concatenate.78, bf16[1536,2048]{1,0:T(8,128)(2,1)} %param.12), kind=kOutput, calls=%fused_computation.73 | convolution fusion | flops 1208352768 | bytes 9240576 | tf_op jit(solution)/shard_map/dot_general | solution.py:150
  65.4 0.2 collective-permute-start.7
  65.6 0.1 pad.34.clone
  65.7 0.1 pad_add_fusion.1
  65.8 1.9 %collective-permute-done.7 = bf16[192,2048]{1,0:T(8,128)(2,1)S(1)} collective-permute-done((bf16[192,2048]{1,0:T(8,128)(2,1)S(1)}, bf16[192,2048]{1,0:T(8,128)(2,1)S(1)}, u32[]{:S(2)}, u32[]{:S(2)}) %collective-permute-start.7) | collective-permute-done | bytes 786464 | tf_op jit(solution)/shard_map/ppermute | solution.py:105
  67.7 2.3 %multiply_convert_fusion.2 = (bf16[192,2048]{1,0:T(8,128)(2,1)S(1)}, bf16[192,2048]{1,0:T(8,128)(2,1)S(1)}, bf16[192,2048]{1,0:T(8,128)(2,1)S(1)}) fusion(f32[192,2048]{1,0:T(8,128)S(1)} %get-tuple-element.44, bf16[192,2048]{1,0:T(8,128)(2,1)S(1)} %collective-permute-done.7, f32[192,2048]{1,0:T(8,128)S(1)} %get-tuple-element.46, ...), kind=kLoop, calls=%fused_computation.11 | loop fusion | flops 8257536 | bytes 9437184 | tf_op jit(solution)/shard_map/convert_element_type | solution.py:89
  70.1 0.0 slice-start.2
  70.1 0.0 slice-start.4
  70.1 2.2 %convolution_convert_fusion.3 = bf16[192,1536]{1,0:T(8,128)(2,1)S(1)} fusion(bf16[192,2048]{1,0:T(8,128)(2,1)S(1)} %get-tuple-element.7, bf16[1536,2048]{1,0:T(8,128)(2,1)S(1)} %bitcast.32), kind=kOutput, calls=%fused_computation.5 | convolution fusion | flops 1208254464 | bytes 7667712 | tf_op jit(solution)/shard_map/dot_general | solution.py:17
  72.4 0.0 slice-start.5
  72.4 4.5 %convolution_convert_fusion = bf16[1536,2048]{1,0:T(8,128)(2,1)} fusion(bf16[192,1536]{1,0:T(8,128)(2,1)S(1)} %concatenate.81, bf16[192,2048]{1,0:T(8,128)(2,1)S(1)} %get-tuple-element.7), kind=kOutput, calls=%fused_computation | convolution fusion | flops 1211105280 | bytes 7667712 | tf_op jit(solution)/shard_map/dot_general | solution.py:13
  76.9 1.3 %collective-permute-start.8 = (bf16[96,1536]{1,0:T(8,128)(2,1)S(1)}, bf16[96,1536]{1,0:T(8,128)(2,1)S(1)}, u32[]{:S(2)}, u32[]{:S(2)}) collective-permute-start(bf16[96,1536]{1,0:T(8,128)(2,1)S(1)} %slice.170), channel_id=1, source_target_pairs={{0,2},{2,0},{4,6},{6,4},{8,10},{10,8},{12,14},{14,12},{1,3},{3,1},... | collective-permute-start | bytes 884744 | tf_op jit(solution)/shard_map/ppermute | solution.py:97
  78.2 2.2 %fusion.32 = f32[192,1536]{1,0:T(8,128)S(1)} fusion(bf16[192,2048]{1,0:T(8,128)(2,1)S(1)} %get-tuple-element.8, bf16[1536,2048]{1,0:T(8,128)(2,1)S(1)} %bitcast.34), kind=kOutput, calls=%fused_computation.76 | convolution fusion | flops 1207959552 | bytes 8257536 | tf_op jit(solution)/shard_map/dot_general | solution.py:17
  80.5 2.2 %fusion = bf16[192,1536]{1,0:T(8,128)(2,1)S(1)} fusion(f32[192,1536]{1,0:T(8,128)S(1)} %fusion.32, bf16[192,2048]{1,0:T(8,128)(2,1)S(1)} %get-tuple-element.9, bf16[1536,2048]{1,0:T(8,128)(2,1)S(1)} %bitcast.36), kind=kOutput, calls=%fused_computation.4 | convolution fusion | flops 1208549376 | bytes 8847360 | tf_op jit(solution)/shard_map/dot_general | solution.py:17
  82.8 0.1 collective-permute-start.13
  82.8 4.8 %convolution_convert_fusion.1 = bf16[1536,2048]{1,0:T(8,128)(2,1)} fusion(bf16[192,1536]{1,0:T(8,128)(2,1)S(1)} %concatenate.78, bf16[192,2048]{1,0:T(8,128)(2,1)S(1)} %get-tuple-element.9), kind=kOutput, calls=%fused_computation.1 | convolution fusion | flops 1211105280 | bytes 7667712 | tf_op jit(solution)/shard_map/dot_general | solution.py:13
  87.6 0.1 add_convert_fusion.1
  87.7 1.5 %collective-permute-start.9 = (bf16[48,1536]{1,0:T(8,128)(2,1)S(1)}, bf16[48,1536]{1,0:T(8,128)(2,1)S(1)}, u32[]{:S(2)}, u32[]{:S(2)}) collective-permute-start(bf16[48,1536]{1,0:T(8,128)(2,1)S(1)} %slice.172), channel_id=1, source_target_pairs={{0,16},{16,0},{1,17},{17,1},{2,18},{18,2},{3,19},{19,3},{4,20},{20... | collective-permute-start | bytes 442376 | tf_op jit(solution)/shard_map/ppermute | solution.py:101
  89.2 1.8 %collective-permute-done.13 = bf16[96,1536]{1,0:T(8,128)(2,1)S(1)} collective-permute-done((bf16[96,1536]{1,0:T(8,128)(2,1)S(1)}, bf16[96,1536]{1,0:T(8,128)(2,1)S(1)}, u32[]{:S(2)}, u32[]{:S(2)}) %collective-permute-start.13) | collective-permute-done | bytes 294944 | tf_op jit(solution)/shard_map/ppermute | solution.py:101
  91.0 0.1 add_convert_fusion
  91.1 0.3 collective-permute-start.14
  91.4 2.7 %collective-permute-done.9 = bf16[48,1536]{1,0:T(8,128)(2,1)S(1)} collective-permute-done((bf16[48,1536]{1,0:T(8,128)(2,1)S(1)}, bf16[48,1536]{1,0:T(8,128)(2,1)S(1)}, u32[]{:S(2)}, u32[]{:S(2)}) %collective-permute-start.9) | collective-permute-done | bytes 147488 | tf_op jit(solution)/shard_map/ppermute | solution.py:101
  94.2 0.9 collective-permute-done.14
  95.2 4.9 %collective-permute-start.16 = (bf16[24,1536]{1,0:T(8,128)(2,1)S(1)}, bf16[24,1536]{1,0:T(8,128)(2,1)S(1)}, u32[]{:S(2)}, u32[]{:S(2)}) collective-permute-start(bf16[24,1536]{1,0:T(8,128)(2,1)S(1)} %pad_maximum_fusion.4), channel_id=1, source_target_pairs={{0,12},{1,28},{2,14},{3,30},{4,0},{5,16},{6,2},{7,18},{8,4},{9,20}... | collective-permute-start | bytes 221192 | tf_op jit(solution)/shard_map/ppermute | solution.py:116
  100.1 0.1 collective-permute-start.17
  100.2 0.1 collective-permute-start.18
  100.4 4.3 %collective-permute-start.15 = (bf16[24,1536]{1,0:T(8,128)(2,1)S(1)}, bf16[24,1536]{1,0:T(8,128)(2,1)S(1)}, u32[]{:S(2)}, u32[]{:S(2)}) collective-permute-start(bf16[24,1536]{1,0:T(8,128)(2,1)S(1)} %pad_maximum_fusion.3), channel_id=1, source_target_pairs={{0,0},{1,16},{2,2},{3,18},{4,4},{5,20},{6,6},{7,22},{8,8},{9,24},{... | collective-permute-start | bytes 221192 | tf_op jit(solution)/shard_map/ppermute | solution.py:116
  104.6 4.5 %convolution_convert_fusion.2 = bf16[1536,2048]{1,0:T(8,128)(2,1)} fusion(bf16[192,1536]{1,0:T(8,128)(2,1)S(1)} %concatenate.78, bf16[192,2048]{1,0:T(8,128)(2,1)S(1)} %get-tuple-element.8), kind=kOutput, calls=%fused_computation.2 | convolution fusion | flops 1211105280 | bytes 7667712 | tf_op jit(solution)/shard_map/dot_general | solution.py:13
  109.2 0.2 fusion.3
  109.4 0.6 slice.210
  110.1 0.7 fusion.14
  (64 shorter events, 0.7 us)
Async XLA Ops:
  4.1 9.5 %collective-permute-start.3 = (bf16[24,1536]{1,0:T(8,128)(2,1)S(1)}, bf16[24,1536]{1,0:T(8,128)(2,1)S(1)}, u32[]{:S(2)}, u32[]{:S(2)}) collective-permute-start(bf16[24,1536]{1,0:T(8,128)(2,1)S(1)} %get-tuple-element.16), channel_id=1, source_target_pairs={{0,12},{1,28},{2,14},{3,30},{4,0},{5,16},{6,2},{7,18},{8,4},{9,20}... | collective-permute-start | bytes 221192 | tf_op jit(solution)/shard_map/ppermute | solution.py:116
  9.8 6.9 %collective-permute-start.2 = (bf16[24,1536]{1,0:T(8,128)(2,1)S(1)}, bf16[24,1536]{1,0:T(8,128)(2,1)S(1)}, u32[]{:S(2)}, u32[]{:S(2)}) collective-permute-start(bf16[24,1536]{1,0:T(8,128)(2,1)S(1)} %get-tuple-element.17), channel_id=1, source_target_pairs={{0,8},{1,24},{2,10},{3,26},{4,12},{5,28},{6,14},{7,30},{8,0},{9,16... | collective-permute-start | bytes 221192 | tf_op jit(solution)/shard_map/ppermute | solution.py:116
  9.8 6.9 %collective-permute-start.1 = (bf16[24,1536]{1,0:T(8,128)(2,1)S(1)}, bf16[24,1536]{1,0:T(8,128)(2,1)S(1)}, u32[]{:S(2)}, u32[]{:S(2)}) collective-permute-start(bf16[24,1536]{1,0:T(8,128)(2,1)S(1)} %get-tuple-element.18), channel_id=1, source_target_pairs={{0,4},{1,20},{2,6},{3,22},{4,8},{5,24},{6,10},{7,26},{8,12},{9,28}... | collective-permute-start | bytes 221192 | tf_op jit(solution)/shard_map/ppermute | solution.py:116
  11.4 6.0 %collective-permute-start = (bf16[24,1536]{1,0:T(8,128)(2,1)S(1)}, bf16[24,1536]{1,0:T(8,128)(2,1)S(1)}, u32[]{:S(2)}, u32[]{:S(2)}) collective-permute-start(bf16[24,1536]{1,0:T(8,128)(2,1)S(1)} %get-tuple-element.19), channel_id=1, source_target_pairs={{0,0},{1,16},{2,2},{3,18},{4,4},{5,20},{6,6},{7,22},{8,8},{9,24},{... | collective-permute-start | bytes 221192 | tf_op jit(solution)/shard_map/ppermute | solution.py:116
  13.6 25.9 %copy-start = (bf16[12,1536]{1,0:T(8,128)(2,1)}, bf16[12,1536]{1,0:T(8,128)(2,1)S(1)}, u32[]{:S(2)}) copy-start(bf16[12,1536]{1,0:T(8,128)(2,1)S(1)} %get-tuple-element.29) | copy-start | bytes 110596
  16.7 22.7 %copy-start.1 = (bf16[12,1536]{1,0:T(8,128)(2,1)}, bf16[12,1536]{1,0:T(8,128)(2,1)S(1)}, u32[]{:S(2)}) copy-start(bf16[12,1536]{1,0:T(8,128)(2,1)S(1)} %get-tuple-element.31) | copy-start | bytes 110596
  16.8 22.7 %copy-start.2 = (bf16[12,1536]{1,0:T(8,128)(2,1)}, bf16[12,1536]{1,0:T(8,128)(2,1)S(1)}, u32[]{:S(2)}) copy-start(bf16[12,1536]{1,0:T(8,128)(2,1)S(1)} %get-tuple-element.33) | copy-start | bytes 110596
  17.5 22.0 %copy-start.3 = (bf16[12,1536]{1,0:T(8,128)(2,1)}, bf16[12,1536]{1,0:T(8,128)(2,1)S(1)}, u32[]{:S(2)}) copy-start(bf16[12,1536]{1,0:T(8,128)(2,1)S(1)} %get-tuple-element.35) | copy-start | bytes 110596
  17.5 5.3 %collective-permute-start.10 = (bf16[48,1536]{1,0:T(8,128)(2,1)S(1)}, bf16[48,1536]{1,0:T(8,128)(2,1)S(1)}, u32[]{:S(2)}, u32[]{:S(2)}) collective-permute-start(bf16[48,1536]{1,0:T(8,128)(2,1)S(1)} %pad_maximum_fusion.2), channel_id=1, source_target_pairs={{0,16},{16,0},{1,17},{17,1},{2,18},{18,2},{3,19},{19,3},{4,20},{20... | collective-permute-start | bytes 442376 | tf_op jit(solution)/shard_map/ppermute | solution.py:101
  23.3 15.6 %collective-permute-start.11 = (bf16[96,1536]{1,0:T(8,128)(2,1)S(1)}, bf16[96,1536]{1,0:T(8,128)(2,1)S(1)}, u32[]{:S(2)}, u32[]{:S(2)}) collective-permute-start(bf16[96,1536]{1,0:T(8,128)(2,1)S(1)} %concatenate.80), channel_id=1, source_target_pairs={{0,2},{2,0},{4,6},{6,4},{8,10},{10,8},{12,14},{14,12},{1,3},{3,1},... | collective-permute-start | bytes 884744 | tf_op jit(solution)/shard_map/ppermute | solution.py:97
  24.6 9.4 %collective-permute-start.4 = (bf16[48,1536]{1,0:T(8,128)(2,1)S(1)}, bf16[48,1536]{1,0:T(8,128)(2,1)S(1)}, u32[]{:S(2)}, u32[]{:S(2)}) collective-permute-start(bf16[48,1536]{1,0:T(8,128)(2,1)S(1)} %pad_maximum_fusion.1), channel_id=1, source_target_pairs={{0,2},{2,0},{4,6},{6,4},{8,10},{10,8},{12,14},{14,12},{1,3},{3,1},... | collective-permute-start | bytes 442376 | tf_op jit(solution)/shard_map/ppermute | solution.py:97
  34.0 9.7 %copy-start.4 = (bf16[48,1536]{1,0:T(8,128)(2,1)}, bf16[48,1536]{1,0:T(8,128)(2,1)S(1)}, u32[]{:S(2)}) copy-start(bf16[48,1536]{1,0:T(8,128)(2,1)S(1)} %collective-permute-done.4) | copy-start | bytes 442372
  38.9 6.9 %collective-permute-start.5 = (bf16[96,1536]{1,0:T(8,128)(2,1)}, bf16[96,1536]{1,0:T(8,128)(2,1)}, u32[]{:S(2)}, u32[]{:S(2)}) collective-permute-start(bf16[96,1536]{1,0:T(8,128)(2,1)} %concatenate.77), channel_id=1, source_target_pairs={{0,16},{16,0},{1,17},{17,1},{2,18},{18,2},{3,19},{19,3},{4,20},{20... | collective-permute-start | bytes 884744 | tf_op jit(solution)/shard_map/ppermute | solution.py:101
  43.7 22.1 %collective-permute-start.12 = (bf16[192,2048]{1,0:T(8,128)(2,1)S(1)}, bf16[192,2048]{1,0:T(8,128)(2,1)}, u32[]{:S(2)}, u32[]{:S(2)}) collective-permute-start(bf16[192,2048]{1,0:T(8,128)(2,1)S(1)} %get-tuple-element.47), channel_id=1, source_target_pairs={{0,1},{1,0},{2,3},{3,2},{4,5},{5,4},{6,7},{7,6},{8,9},{9,8},{10,11... | collective-permute-start | bytes 2359304 | tf_op jit(solution)/shard_map/ppermute | solution.py:105
  53.9 16.2 %slice-start = ((s8[6291456]{0:T(1024)(128)(4,1)}), s8[4194304]{0:T(1024)(128)(4,1)S(1)}, s32[]{:S(2)}) async-start(s8[6291456]{0:T(1024)(128)(4,1)} %bitcast.31), calls=%async_computation | async-start | bytes 8388608
  58.3 7.4 %copy-start.5 = (pred[4,12,16]{2,0,1:T(4,128)(4,1)S(1)}, pred[4,12,16]{2,0,1:T(4,128)(4,1)}, u32[]{:S(2)}) copy-start(pred[4,12,16]{2,0,1:T(4,128)(4,1)} %get-tuple-element.37) | copy-start | bytes 2308
  58.3 7.5 %copy-start.6 = (f32[16,2]{0,1:T(2,128)S(1)}, f32[16,2]{0,1:T(2,128)}, u32[]{:S(2)}) copy-start(f32[16,2]{0,1:T(2,128)} %param.10) | copy-start | bytes 388
  58.3 11.8 %slice-start.1 = ((s8[6291456]{0:T(1024)(128)(4,1)}), s8[2097152]{0:T(1024)(128)(4,1)S(1)}, s32[]{:S(2)}) async-start(s8[6291456]{0:T(1024)(128)(4,1)} %bitcast.31), calls=%async_computation.1 | async-start | bytes 4194304
  58.3 7.5 %collective-permute-start.6 = (bf16[192,2048]{1,0:T(8,128)(2,1)S(1)}, bf16[192,2048]{1,0:T(8,128)(2,1)S(1)}, u32[]{:S(2)}, u32[]{:S(2)}) collective-permute-start(bf16[192,2048]{1,0:T(8,128)(2,1)S(1)} %get-tuple-element.45), channel_id=1, source_target_pairs={{0,1},{1,0},{2,3},{3,2},{4,5},{5,4},{6,7},{7,6},{8,9},{9,8},{10,11... | collective-permute-start | bytes 2359304 | tf_op jit(solution)/shard_map/ppermute | solution.py:105
  65.4 2.4 %collective-permute-start.7 = (bf16[192,2048]{1,0:T(8,128)(2,1)S(1)}, bf16[192,2048]{1,0:T(8,128)(2,1)S(1)}, u32[]{:S(2)}, u32[]{:S(2)}) collective-permute-start(bf16[192,2048]{1,0:T(8,128)(2,1)S(1)} %get-tuple-element.43), channel_id=1, source_target_pairs={{0,1},{1,0},{2,3},{3,2},{4,5},{5,4},{6,7},{7,6},{8,9},{9,8},{10,11... | collective-permute-start | bytes 2359304 | tf_op jit(solution)/shard_map/ppermute | solution.py:105
  70.1 8.1 %slice-start.2 = ((s8[6291456]{0:T(1024)(128)(4,1)}), s8[2097152]{0:T(1024)(128)(4,1)S(1)}, s32[]{:S(2)}) async-start(s8[6291456]{0:T(1024)(128)(4,1)} %bitcast.33), calls=%async_computation.2 | async-start | bytes 4194304
  70.1 10.3 %slice-start.4 = ((s8[6291456]{0:T(1024)(128)(4,1)}), s8[4194304]{0:T(1024)(128)(4,1)S(1)}, s32[]{:S(2)}) async-start(s8[6291456]{0:T(1024)(128)(4,1)} %bitcast.35), calls=%async_computation.4 | async-start | bytes 8388608
  72.3 5.9 %slice-start.3 = ((s8[6291456]{0:T(1024)(128)(4,1)}), s8[4194304]{0:T(1024)(128)(4,1)S(1)}, s32[]{:S(2)}) async-start(s8[6291456]{0:T(1024)(128)(4,1)} %bitcast.33), calls=%async_computation.3 | async-start | bytes 8388608
  72.4 8.1 %slice-start.5 = ((s8[6291456]{0:T(1024)(128)(4,1)}), s8[2097152]{0:T(1024)(128)(4,1)S(1)}, s32[]{:S(2)}) async-start(s8[6291456]{0:T(1024)(128)(4,1)} %bitcast.35), calls=%async_computation.5 | async-start | bytes 4194304
  76.9 10.7 %collective-permute-start.8 = (bf16[96,1536]{1,0:T(8,128)(2,1)S(1)}, bf16[96,1536]{1,0:T(8,128)(2,1)S(1)}, u32[]{:S(2)}, u32[]{:S(2)}) collective-permute-start(bf16[96,1536]{1,0:T(8,128)(2,1)S(1)} %slice.170), channel_id=1, source_target_pairs={{0,2},{2,0},{4,6},{6,4},{8,10},{10,8},{12,14},{14,12},{1,3},{3,1},... | collective-permute-start | bytes 884744 | tf_op jit(solution)/shard_map/ppermute | solution.py:97
  82.8 8.2 %collective-permute-start.13 = (bf16[96,1536]{1,0:T(8,128)(2,1)S(1)}, bf16[96,1536]{1,0:T(8,128)(2,1)S(1)}, u32[]{:S(2)}, u32[]{:S(2)}) collective-permute-start(bf16[96,1536]{1,0:T(8,128)(2,1)S(1)} %pad_maximum_fusion), channel_id=1, source_target_pairs={{0,16},{16,0},{1,17},{17,1},{2,18},{18,2},{3,19},{19,3},{4,20},{20... | collective-permute-start | bytes 884744 | tf_op jit(solution)/shard_map/ppermute | solution.py:101
  87.7 6.4 %collective-permute-start.9 = (bf16[48,1536]{1,0:T(8,128)(2,1)S(1)}, bf16[48,1536]{1,0:T(8,128)(2,1)S(1)}, u32[]{:S(2)}, u32[]{:S(2)}) collective-permute-start(bf16[48,1536]{1,0:T(8,128)(2,1)S(1)} %slice.172), channel_id=1, source_target_pairs={{0,16},{16,0},{1,17},{17,1},{2,18},{18,2},{3,19},{19,3},{4,20},{20... | collective-permute-start | bytes 442376 | tf_op jit(solution)/shard_map/ppermute | solution.py:101
  91.1 4.1 %collective-permute-start.14 = (bf16[48,1536]{1,0:T(8,128)(2,1)S(1)}, bf16[48,1536]{1,0:T(8,128)(2,1)S(1)}, u32[]{:S(2)}, u32[]{:S(2)}) collective-permute-start(bf16[48,1536]{1,0:T(8,128)(2,1)S(1)} %slice.183), channel_id=1, source_target_pairs={{0,2},{2,0},{4,6},{6,4},{8,10},{10,8},{12,14},{14,12},{1,3},{3,1},... | collective-permute-start | bytes 442376 | tf_op jit(solution)/shard_map/ppermute | solution.py:97
  95.2 14.0 %collective-permute-start.16 = (bf16[24,1536]{1,0:T(8,128)(2,1)S(1)}, bf16[24,1536]{1,0:T(8,128)(2,1)S(1)}, u32[]{:S(2)}, u32[]{:S(2)}) collective-permute-start(bf16[24,1536]{1,0:T(8,128)(2,1)S(1)} %pad_maximum_fusion.4), channel_id=1, source_target_pairs={{0,12},{1,28},{2,14},{3,30},{4,0},{5,16},{6,2},{7,18},{8,4},{9,20}... | collective-permute-start | bytes 221192 | tf_op jit(solution)/shard_map/ppermute | solution.py:116
  100.1 9.1 %collective-permute-start.17 = (bf16[24,1536]{1,0:T(8,128)(2,1)S(1)}, bf16[24,1536]{1,0:T(8,128)(2,1)S(1)}, u32[]{:S(2)}, u32[]{:S(2)}) collective-permute-start(bf16[24,1536]{1,0:T(8,128)(2,1)S(1)} %pad_maximum_fusion.5), channel_id=1, source_target_pairs={{0,8},{1,24},{2,10},{3,26},{4,12},{5,28},{6,14},{7,30},{8,0},{9,16... | collective-permute-start | bytes 221192 | tf_op jit(solution)/shard_map/ppermute | solution.py:116
  100.2 8.9 %collective-permute-start.18 = (bf16[24,1536]{1,0:T(8,128)(2,1)S(1)}, bf16[24,1536]{1,0:T(8,128)(2,1)S(1)}, u32[]{:S(2)}, u32[]{:S(2)}) collective-permute-start(bf16[24,1536]{1,0:T(8,128)(2,1)S(1)} %pad_maximum_fusion.6), channel_id=1, source_target_pairs={{0,4},{1,20},{2,6},{3,22},{4,8},{5,24},{6,10},{7,26},{8,12},{9,28}... | collective-permute-start | bytes 221192 | tf_op jit(solution)/shard_map/ppermute | solution.py:116
  100.4 8.8 %collective-permute-start.15 = (bf16[24,1536]{1,0:T(8,128)(2,1)S(1)}, bf16[24,1536]{1,0:T(8,128)(2,1)S(1)}, u32[]{:S(2)}, u32[]{:S(2)}) collective-permute-start(bf16[24,1536]{1,0:T(8,128)(2,1)S(1)} %pad_maximum_fusion.3), channel_id=1, source_target_pairs={{0,0},{1,16},{2,2},{3,18},{4,4},{5,20},{6,6},{7,22},{8,8},{9,24},{... | collective-permute-start | bytes 221192 | tf_op jit(solution)/shard_map/ppermute | solution.py:116

commit v2 on v1

--- a/solution.py
+++ b/solution.py
@@ -1,12 +1,17 @@
+import math
+
 import jax
 import jax.numpy as jnp
 from jax import lax
+from jax.experimental import pallas as pl
+from jax.experimental.pallas import tpu as pltpu
 from jax.sharding import PartitionSpec as P
 
 EXP = 4
 CAP = 12
 BF = jnp.bfloat16
 F32 = jnp.float32
+TILE = 512
 
 
 def contract_rows(left, right):
@@ -101,6 +106,342 @@
     return lax.ppermute(rows, "section", [(0, 1), (1, 0)])
 
 
+def swap_plane(pieces):
+    size = lax.axis_size("expert")
+    both = [(s * size + i, (1 - s) * size + (i ^ 1)) for s in range(2) for i in range(size)]
+    return [
+        swap_section(pieces[0]),
+        swap_expert(pieces[1]),
+        lax.ppermute(pieces[2], ("section", "expert"), both),
+    ]
+
+
+ANYWHERE = pl.BlockSpec(memory_space=pl.ANY)
+INSIDE = pl.BlockSpec(memory_space=pltpu.VMEM)
+
+
+def params(mib):
+    return pltpu.CompilerParams(vmem_limit_bytes=mib << 20)
+
+
+def cost(flops, *arrays):
+    moved = sum(a.size * a.dtype.itemsize for a in arrays)
+    return pl.CostEstimate(flops=flops, bytes_accessed=moved, transcendentals=0)
+
+
+def in_hbm(array):
+    return pltpu.with_memory_space_constraint(array, pltpu.HBM)
+
+
+def in_vmem(array):
+    return pltpu.with_memory_space_constraint(array, pltpu.VMEM)
+
+
+def pin_kernel(*refs):
+    count = len(refs) // 2 - 1
+    copies = [
+        pltpu.make_async_copy(refs[i], refs[count + 1 + i], refs[-1].at[i]) for i in range(count)
+    ]
+    for copy in copies:
+        copy.start()
+    for copy in copies:
+        copy.wait()
+
+
+def pin(weights, after):
+    count = len(weights)
+    return pl.pallas_call(
+        pin_kernel,
+        out_shape=[pltpu.VMEM(weight.shape, weight.dtype) for weight in weights],
+        in_specs=[ANYWHERE] * (count + 1),
+        out_specs=[ANYWHERE] * count,
+        scratch_shapes=[pltpu.SemaphoreType.DMA((count,))],
+        cost_estimate=cost(0, *weights),
+        compiler_params=params(1),
+    )(*(in_hbm(weight) for weight in weights), after)
+
+
+def gather_kernel(*refs):
+    pieces, (w_ref, x_ref, out_ref) = refs[:-3], refs[-3:]
+    rows = pieces[0].shape[0]
+    for i, piece in enumerate(pieces):
+        x_ref[i * rows : (i + 1) * rows] = piece[...]
+    out_ref[...] = jnp.dot(x_ref[...], w_ref[...], preferred_element_type=F32).astype(BF)
+
+
+def gather_project(pieces, weight):
+    rows, (depth, hidden) = sum(piece.shape[0] for piece in pieces), weight.shape
+    outs = [jax.ShapeDtypeStruct((rows, depth), BF), jax.ShapeDtypeStruct((rows, hidden), BF)]
+    return pl.pallas_call(
+        gather_kernel,
+        out_shape=outs,
+        in_specs=[INSIDE] * (len(pieces) + 1),
+        out_specs=[INSIDE] * 2,
+        cost_estimate=cost(2 * rows * depth * hidden, *pieces, *outs),
+        compiler_params=params(14),
+    )(*pieces, in_vmem(weight))
+
+
+def project_kernel(x_ref, w_ref, out_ref):
+    out_ref[...] = jnp.dot(x_ref[...], w_ref[...], preferred_element_type=F32).astype(BF)
+
+
+def project(x, weight):
+    rows, (depth, hidden) = x.shape[0], weight.shape
+    out = jax.ShapeDtypeStruct((rows, hidden), BF)
+    return pl.pallas_call(
+        project_kernel,
+        out_shape=out,
+        in_specs=[INSIDE] * 2,
+        out_specs=INSIDE,
+        cost_estimate=cost(2 * rows * depth * hidden, x, out),
+        compiler_params=params(12),
+    )(x, in_vmem(weight))
+
+
+def iota(shape, dim):
+    return lax.broadcasted_iota(jnp.int32, shape, dim)
+
+
+def slot_rows(ids_ref, plane):
+    count = ids_ref.shape[1]
+    shape = (EXP * 2 * CAP, count)
+    row = iota(shape, 0)
+    place = row % (2 * CAP)
+    expert = (plane + row // (2 * CAP)) % EXP
+    match = [ids_ref[j : j + 1, :] == expert for j in range(2)]
+    chosen = jnp.logical_or(*match)
+    before = (iota((count, count), 0) < iota((count, count), 1)).astype(F32)
+    rank = jnp.dot(chosen.astype(F32), before, preferred_element_type=F32)
+    picks = jnp.logical_and(chosen, rank == (place % CAP).astype(F32))
+    return match, picks, place
+
+
+def pack_kernel(tok_ref, grad_ref, ids_ref, probs_ref, *out_refs):
+    half = out_refs[0].shape[1]
+    start = pl.multiple_of(lax.axis_index("section") * half, half)
+    match, picks, place = slot_rows(ids_ref, lax.axis_index("expert") // 2)
+    share = jnp.where(match[0], probs_ref[0:1, :], 0.0) + jnp.where(match[1], probs_ref[1:2, :], 0.0)
+    scale = jnp.sum(jnp.where(picks, share, 0.0), axis=1, keepdims=True)
+    picks = picks.astype(BF)
+    tok = jnp.dot(picks, tok_ref[:, pl.ds(start, half)], preferred_element_type=F32)
+    grad = jnp.dot(picks, grad_ref[:, pl.ds(start, half)], preferred_element_type=F32)
+    payload = jnp.where(place[:, 0:1] < CAP, tok, grad * scale)
+    for k, out_ref in enumerate(out_refs):
+        out_ref[...] = payload[k * 2 * CAP : (k + 1) * 2 * CAP].astype(BF)
+
+
+def pack(tokens, grad_out, expert_ids, gate_probs, half):
+    outs = [jax.ShapeDtypeStruct((2 * CAP, half), BF)] * EXP
+    return pl.pallas_call(
+        pack_kernel,
+        out_shape=outs,
+        in_specs=[INSIDE] * 4,
+        out_specs=[INSIDE] * EXP,
+        cost_estimate=cost(0, tokens, grad_out, *outs),
+        compiler_params=params(8),
+    )(tokens, grad_out, expert_ids.T, gate_probs.T)
+
+
+def sorting():
+    n = EXP * CAP
+    sorted_row, row = iota((2 * n, 2 * n), 0), iota((2 * n, 2 * n), 1)
+    k, j = row // (2 * CAP), row % (2 * CAP)
+    place = jnp.where(j < CAP, k * CAP + j, n + k * CAP + j - CAP)
+    return (sorted_row == place).astype(BF)
+
+
+def stack(refs, held_ref):
+    rows = refs[0].shape[0]
+    for i, ref in enumerate(refs):
+        held_ref[i * rows : (i + 1) * rows] = ref[...].astype(F32)
+    return held_ref[...].astype(BF)
+
+
+def part_kernel(*refs):
+    refs, (tok_ref, grad_ref, held_ref) = refs[:EXP], refs[EXP:]
+    rows = jnp.dot(sorting(), stack(refs, held_ref), preferred_element_type=F32).astype(BF)
+    n = EXP * CAP
+    tok_ref[...] = rows[:n]
+    grad_ref[...] = rows[n:]
+
+
+def part(got):
+    width = got[0].shape[1]
+    outs = [jax.ShapeDtypeStruct((EXP * CAP, width), BF)] * 2
+    return pl.pallas_call(
+        part_kernel,
+        out_shape=outs,
+        in_specs=[INSIDE] * EXP,
+        out_specs=[INSIDE] * 2,
+        scratch_shapes=[pltpu.VMEM((2 * EXP * CAP, width), F32)],
+        cost_estimate=cost(0, *got, *outs),
+        compiler_params=params(8),
+    )(*got)
+
+
+def join_kernel(*refs):
+    outs, ins, sent = refs[:4], refs[4:8], refs[8:]
+
+    def total(pieces):
+        return sum(p[...].astype(F32) for p in pieces).astype(BF)
+
+    rows = jnp.concatenate([total(outs), total(ins)], axis=0)
+    rows = lax.dot_general(
+        sorting(), rows, (((0,), (0,)), ((), ())), preferred_element_type=F32
+    )
+    for k, ref in enumerate(sent):
+        ref[...] = rows[k * 2 * CAP : (k + 1) * 2 * CAP].astype(BF)
+
+
+def join(outs, ins):
+    width = outs[0].shape[1]
+    sent = [jax.ShapeDtypeStruct((2 * CAP, width), BF)] * EXP
+    return pl.pallas_call(
+        join_kernel,
+        out_shape=sent,
+        in_specs=[INSIDE] * 8,
+        out_specs=[INSIDE] * EXP,
+        cost_estimate=cost(0, *outs, *ins, *sent),
+        compiler_params=params(10),
+    )(*outs, *ins)
+
+
+def unpack_kernel(*refs):
+    refs, (ids_ref, probs_ref, out_ref, in_ref, held_ref) = refs[:EXP], refs[EXP:]
+    match, picks, place = slot_rows(ids_ref, lax.axis_index("expert") // 2)
+    rows = stack(refs, held_ref)
+    count = ids_ref.shape[1]
+    same = iota((count, count), 0) == iota((count, count), 1)
+    probs = [
+        jnp.sum(jnp.where(same, probs_ref[j : j + 1, :], 0.0), axis=1, keepdims=True)
+        for j in range(2)
+    ]
+
+    def found(where):
+        return contract_rows(jnp.logical_and(picks, where).astype(BF), rows)
+
+    first = place < CAP
+    out_ref[...] = (
+        probs[0] * found(jnp.logical_and(first, match[0]))
+        + probs[1] * found(jnp.logical_and(first, match[1]))
+    ).astype(BF)
+    in_ref[...] = found(jnp.logical_not(first)).astype(BF)
+
+
+def unpack(back, expert_ids, gate_probs):
+    width = back[0].shape[1]
+    outs = [jax.ShapeDtypeStruct((expert_ids.shape[0], width), BF)] * 2
+    return pl.pallas_call(
+        unpack_kernel,
+        out_shape=outs,
+        in_specs=[INSIDE] * (EXP + 2),
+        out_specs=[INSIDE] * 2,
+        scratch_shapes=[pltpu.VMEM((2 * EXP * CAP, width), F32)],
+        cost_estimate=cost(0, *back, *outs),
+        compiler_params=params(8),
+    )(*back, expert_ids.T, gate_probs.T)
+
+
+def spread(rows, refs):
+    count = refs[0].shape[0]
+    for i, ref in enumerate(refs):
+        ref[...] = rows[i * count : (i + 1) * count].astype(BF)
+
+
+def forward_kernel(g0_ref, g1_ref, u0_ref, u1_ref, w_ref, act_ref, *out_refs):
+    hidden = act_ref.shape[1]
+    tile = math.gcd(hidden, TILE)
+    for at in range(0, hidden, tile):
+        cut = slice(at, at + tile)
+        gate_pre = g0_ref[:, cut].astype(F32) + g1_ref[:, cut].astype(F32)
+        up_pre = u0_ref[:, cut].astype(F32) + u1_ref[:, cut].astype(F32)
+        act_ref[:, cut] = (gate_pre * jax.nn.sigmoid(gate_pre) * up_pre).astype(BF)
+    spread(contract_cols(act_ref[...], w_ref[...]), out_refs)
+
+
+def forward(gates, ups, weight):
+    rows, (depth, hidden) = gates[0].shape[0], weight.shape
+    outs = [jax.ShapeDtypeStruct((rows, hidden), BF)]
+    outs += [jax.ShapeDtypeStruct((rows // 4, depth), BF)] * 4
+    return pl.pallas_call(
+        forward_kernel,
+        out_shape=outs,
+        in_specs=[INSIDE] * 5,
+        out_specs=[INSIDE] * 5,
+        cost_estimate=cost(2 * rows * depth * hidden, *gates, *ups, *outs),
+        compiler_params=params(16),
+    )(*gates, *ups, in_vmem(weight))
+
+
+def backward_kernel(
+    g0_ref, g1_ref, u0_ref, u1_ref, a0_ref, a1_ref, wg_ref, wu_ref, dg_ref, du_ref, *out_refs
+):
+    hidden = dg_ref.shape[1]
+    tile = math.gcd(hidden, TILE)
+    for at in range(0, hidden, tile):
+        cut = slice(at, at + tile)
+        gate_pre = g0_ref[:, cut].astype(F32) + g1_ref[:, cut].astype(F32)
+        up_pre = u0_ref[:, cut].astype(F32) + u1_ref[:, cut].astype(F32)
+        act_grad = a0_ref[:, cut].astype(F32) + a1_ref[:, cut].astype(F32)
+        _, up_grad, gate_grad = pointwise(gate_pre, up_pre, act_grad)
+        dg_ref[:, cut] = gate_grad
+        du_ref[:, cut] = up_grad
+    spread(
+        contract_cols(dg_ref[...], wg_ref[...]) + contract_cols(du_ref[...], wu_ref[...]), out_refs
+    )
+
+
+def backward(gates, ups, acts, gate_weight, up_weight):
+    rows, (depth, hidden) = gates[0].shape[0], gate_weight.shape
+    outs = [
+        jax.ShapeDtypeStruct((rows, hidden), BF),
+        jax.ShapeDtypeStruct((rows, hidden), BF),
+    ] + [jax.ShapeDtypeStruct((rows // 4, depth), BF)] * 4
+    return pl.pallas_call(
+        backward_kernel,
+        out_shape=outs,
+        in_specs=[INSIDE] * 8,
+        out_specs=[INSIDE] * 6,
+        cost_estimate=cost(4 * rows * depth * hidden, *gates, *ups, *acts, *outs),
+        compiler_params=params(20),
+    )(*gates, *ups, *acts, in_vmem(gate_weight), in_vmem(up_weight))
+
+
+def outer_kernel(x_ref, y_ref, out_ref, turned_ref, held_ref, sem):
+    depth = held_ref.shape[0]
+    tile = math.gcd(depth, 256)
+    turned_ref[...] = x_ref[...].T
+    copies = []
+    for i, at in enumerate(range(0, depth, tile)):
+        cut = slice(at, at + tile)
+        held_ref[cut] = jnp.dot(
+            turned_ref[cut], y_ref[...], preferred_element_type=F32
+        ).astype(BF)
+        copies.append(pltpu.make_async_copy(held_ref.at[cut], out_ref.at[cut], sem.at[i]))
+        copies[-1].start()
+    for copy in copies:
+        copy.wait()
+
+
+def outer(x, y):
+    (rows, depth), hidden = x.shape, y.shape[1]
+    out = jax.ShapeDtypeStruct((depth, hidden), BF)
+    return pl.pallas_call(
+        outer_kernel,
+        out_shape=out,
+        in_specs=[INSIDE] * 2,
+        out_specs=ANYWHERE,
+        scratch_shapes=[
+            pltpu.VMEM((depth, rows), BF),
+            pltpu.VMEM((depth, hidden), BF),
+            pltpu.SemaphoreType.DMA((depth // math.gcd(depth, 256),)),
+        ],
+        cost_estimate=cost(2 * rows * depth * hidden, x, y, out),
+        compiler_params=params(24),
+    )(x, y)
+
+
 def swap_dp(rows):
     return lax.ppermute(rows, "dp", [(0, 1), (1, 0)])
 
@@ -117,85 +458,28 @@
 
 
 def paired(tokens, grad_out, expert_ids, gate_probs, gate_weight, up_weight, down_weight):
-    half = gate_weight.shape[0]
-    count = tokens.shape[0]
-    section = lax.axis_index("section")
-    plane = lax.axis_index("expert") // 2
-    experts = (plane + jnp.arange(EXP, dtype=jnp.int32)) % EXP
-    match = expert_ids[None, :, :] == experts[:, None, None]
-    picks = slot_tables(match, CAP)
-    share = jnp.sum(jnp.where(match, gate_probs[None, :, :], 0.0), axis=2)
-    slot_gate = jnp.sum(jnp.where(picks, share[:, None, :], 0.0), axis=2)
-    none = jnp.zeros_like(picks)
-    pick_both = jnp.concatenate(
-        [jnp.concatenate([picks, none], axis=2), jnp.concatenate([none, picks], axis=2)], axis=1
-    ).reshape(EXP * 2 * CAP, 2 * count).astype(BF)
-    scale = jnp.concatenate([jnp.ones_like(slot_gate), slot_gate], axis=1).reshape(-1, 1)
-    rows = jnp.concatenate([tokens, grad_out], axis=0)
-    rows = lax.dynamic_slice_in_dim(rows, section * half, half, axis=1)
-    payload = (jnp.dot(pick_both, rows, preferred_element_type=F32) * scale).astype(BF)
-    got = [turn(payload[k * 2 * CAP : (k + 1) * 2 * CAP], k) for k in range(EXP)]
-    own_t = jnp.concatenate([g[:CAP] for g in got], axis=0)
-    own_g = jnp.concatenate([g[CAP:] for g in got], axis=0)
-    n = EXP * CAP
-    xt = swap_expert(own_t)
-    yg = swap_section(own_g)
-    yt = swap_section(jnp.concatenate([own_t, xt], axis=0))
-    two_g = jnp.concatenate([own_g, yg], axis=0)
-    xg = swap_expert(two_g)
-    slot_t = jnp.concatenate([own_t, yt[:n], xt, yt[n:]], axis=0)
-    slot_g = jnp.concatenate([two_g, xg], axis=0)
-
-    gate_p = jnp.dot(slot_t, gate_weight, preferred_element_type=F32)
-    up_p = jnp.dot(slot_t, up_weight, preferred_element_type=F32)
-    act_p = jnp.dot(slot_g, down_weight, preferred_element_type=F32)
-    gate_pre = gate_p + swap_dp(gate_p.astype(BF)).astype(F32)
-    up_pre = up_p + swap_dp(up_p.astype(BF)).astype(F32)
-    act_grad = act_p + swap_dp(act_p.astype(BF)).astype(F32)
-    activation, up_grad, gate_grad = pointwise(gate_pre, up_pre, act_grad)
-
-    part_out = contract_cols(activation, down_weight).astype(BF)
-    part_in = (contract_cols(gate_grad, gate_weight) + contract_cols(up_grad, up_weight)).astype(BF)
-    grad_gate = contract_rows(slot_t, gate_grad).astype(BF)
-    grad_up = contract_rows(slot_t, up_grad).astype(BF)
-    grad_down = contract_rows(slot_g, activation).astype(BF)
-
-    def add(a, b):
-        return (a.astype(F32) + b.astype(F32)).astype(BF)
-
-    two_out = add(part_out[: 2 * n], swap_expert(part_out[2 * n :]))
-    one_out = add(two_out[:n], swap_section(two_out[n:]))
-    two_in = add(
-        jnp.concatenate([part_in[:n], part_in[2 * n : 3 * n]], axis=0),
-        swap_section(jnp.concatenate([part_in[n : 2 * n], part_in[3 * n :]], axis=0)),
-    )
-    one_in = add(two_in[:n], swap_expert(two_in[n:]))
-    back = [
-        turn(
-            jnp.concatenate(
-                [one_out[k * CAP : (k + 1) * CAP], one_in[k * CAP : (k + 1) * CAP]], axis=0
-            ),
-            -k,
-        )
-        for k in range(EXP)
-    ]
-    back = jnp.concatenate(back, axis=0)
-    per_choice = [
-        jnp.logical_and(picks, match[:, None, :, j]) for j in range(2)
-    ]
-    blank = jnp.zeros_like(picks)
-    spread = jnp.concatenate(
-        [
-            jnp.concatenate([per_choice[0], per_choice[1], blank], axis=2),
-            jnp.concatenate([blank, blank, picks], axis=2),
-        ],
-        axis=1,
-    ).reshape(EXP * 2 * CAP, 3 * count).astype(BF)
-    found = contract_rows(spread, back)
-    moe_out = (
-        gate_probs[:, 0:1] * found[:count] + gate_probs[:, 1:2] * found[count : 2 * count]
-    ).astype(BF)
-    grad_tokens = found[2 * count :].astype(BF)
+    payload = pack(tokens, grad_out, expert_ids, gate_probs, gate_weight.shape[0])
+    got = [turn(rows, k) for k, rows in enumerate(payload)]
+    gate_weight, up_weight = pin((gate_weight, up_weight), payload[0])
+    own_t, own_g = part(got)
+    (down_weight,) = pin((down_weight,), own_t)
+    slot_t, gate_part = gather_project([own_t] + swap_plane([own_t] * 3), gate_weight)
+    gates = [gate_part, swap_dp(gate_part)]
+    up_part = project(slot_t, up_weight)
+    ups = [up_part, swap_dp(up_part)]
+    slot_g, act_part = gather_project([own_g] + swap_plane([own_g] * 3), down_weight)
+    acts = [act_part, swap_dp(act_part)]
+    activation, *part_out = forward(gates, ups, down_weight)
+    gate_grad, up_grad, *part_in = backward(gates, ups, acts, gate_weight, up_weight)
+    grad_down = outer(slot_g, activation)
+    grad_gate = outer(slot_t, gate_grad)
+    grad_up = outer(slot_t, up_grad)
+    sent = join(
+        part_out[:1] + swap_plane(part_out[1:]), part_in[:1] + swap_plane(part_in[1:])
+    )
+    moe_out, grad_tokens = unpack(
+        [turn(rows, -k) for k, rows in enumerate(sent)], expert_ids, gate_probs
+    )
     return moe_out, grad_tokens, grad_gate, grad_up, grad_down
 
 

time: 112 us -> 72 us (0.64)
  matrix products: 34.5 us -> 0 us
  Pallas kernels: 0 us -> 29.8 us
  waiting for transfers between devices: 25.6 us -> 7.28 us
  local copies, waits for them, and re-layouts: 15.4 us -> 3.15 us
  other arithmetic: 5.37 us -> 0 us
  starting transfers between devices: 28.7 us -> 30.7 us
    dot_general x11 -> x0, matrix products: 34.5 us -> none  [the longest x4 14.1 us: contract_rows(): lax.dot_general(left, right, (((0,), (0,)), ((), ())), preferred_element_...]
    pallas_call x0 -> x14, Pallas kernels: none -> 29.8 us  [the longest x3 9.58 us: outer(): pl.pallas_call(outer_kernel, out_shape=out, in_specs=[INSIDE] * 2, out_sp...]
    concatenate x8 -> x0, local copies, waits for them, and re-layouts: 12.5 us -> none  [the longest x1 6.36 us: paired(): slot_t = jnp.concatenate([own_t, yt[:n], xt, yt[n:]], axis=0)]
    ppermute x4, waiting for transfers between devices: 10 us -> 0.01 us  [swap_expert(): return lax.ppermute(rows, 'expert', [(i, i ^ 1) for i in range(size)])]
    ppermute x4, waiting for transfers between devices: 9.91 us -> 0.01 us  [swap_section(): return lax.ppermute(rows, 'section', [(0, 1), (1, 0)])]
    ppermute x0 -> x4, starting transfers between devices: none -> 4.79 us  [swap_plane(): lax.ppermute(pieces[2], ('section', 'expert'), both)]
    ppermute x3, starting transfers between devices: 5.08 us -> 1.4 us  [swap_dp(): return lax.ppermute(rows, 'dp', [(0, 1), (1, 0)])]
    convert_element_type x7 -> x0, other arithmetic: 3.26 us -> none  [the longest x1 2.33 us: pointwise(): activation = (silu_value * up_pre).astype(BF)]
  transfers between devices with their start and end apart: 19 -> 23, of which waited for: 9 -> 6; matrix products, arithmetic and copies ran while one was open for 37% -> 0% of each run, Pallas kernels for 0% -> 39%
where the time goes in v2:
time: 72 us; the launch traced here: 71.8 us
  starting transfers between devices  30.7 us (43%)
  Pallas kernels  29.8 us (41%)
  waiting for transfers between devices  7.28 us (10%)
  local copies, waits for them, and re-layouts  3.15 us (4%)
  between operations  0.87 us (1%)
    ppermute x8, starting transfers between devices, turn(): return lax.ppermute(rows, ('section', 'expert', 'dp'), pairs)  18.4 us
    pallas_call x3, Pallas kernels, outer(): pl.pallas_call(outer_kernel, out_shape=out, in_specs=[INSIDE] * 2, out_sp...  9.58 us
    pallas_call x2, Pallas kernels, pin(): pl.pallas_call(pin_kernel, out_shape=[pltpu.VMEM(weight.shape, weight.dty...  7.41 us
    ppermute x8, waiting for transfers between devices, turn(): return lax.ppermute(rows, ('section', 'expert', 'dp'), pairs)  6.26 us
    ppermute x4, starting transfers between devices, swap_expert(): return lax.ppermute(rows, 'expert', [(i, i ^ 1) for i in range(size)])  4.92 us
    ppermute x4, starting transfers between devices, swap_plane(): lax.ppermute(pieces[2], ('section', 'expert'), both)  4.79 us
    pallas_call x1, Pallas kernels, backward(): pl.pallas_call(backward_kernel, out_shape=outs, in_specs=[INSIDE] * 8, ou...  4.42 us
    unnamed x12, local copies, waits for them, and re-layouts  3.15 us
  transfers between devices with their start and end apart: 23, of which 6 were waited for; matrix products, arithmetic and copies ran while one was open for 0% of the time, Pallas kernels for 39%

profile of v2, /device:TPU:1, one launch (start us, length us, event | category | flops | bytes accessed | tf_op | source)
XLA Modules:
  0.0 71.8 jit_solution(1296524477494264729)
XLA Ops:
  0.6 0.9 %copy-done = bf16[16,3072]{1,0:T(8,128)(2,1)S(1)} copy-done((bf16[16,3072]{1,0:T(8,128)(2,1)S(1)}, bf16[16,3072]{1,0:T(8,128)(2,1)}, u32[]{:S(2)}) %copy-start) | copy-done | bytes 98328
  1.5 0.9 %copy-done.1 = bf16[16,3072]{1,0:T(8,128)(2,1)S(1)} copy-done((bf16[16,3072]{1,0:T(8,128)(2,1)S(1)}, bf16[16,3072]{1,0:T(8,128)(2,1)}, u32[]{:S(2)}) %copy-start.1) | copy-done | bytes 98328
  2.4 0.7 copy-done.2
  3.1 0.7 copy-done.4
  3.8 0.4 shard_map.110
  4.2 4.5 %collective-permute-start = (bf16[24,1536]{1,0:T(8,128)(2,1)S(1)}, bf16[24,1536]{1,0:T(8,128)(2,1)S(1)}, u32[]{:S(2)}, u32[]{:S(2)}) collective-permute-start(bf16[24,1536]{1,0:T(8,128)(2,1)S(1)} %get-tuple-element.34.refs_2_), channel_id=1, source_target_pairs={{0,0},{1,16},{2,2},{3,18},{4,4},{5,20},{6,6},{7,22},{8,8},{9,24},{... | collective-permute-start | bytes 221192 | tf_op jit(solution)/shard_map/ppermute | solution.py:457
  8.8 1.1 %collective-permute-start.1 = (bf16[24,1536]{1,0:T(8,128)(2,1)S(1)}, bf16[24,1536]{1,0:T(8,128)(2,1)S(1)}, u32[]{:S(2)}, u32[]{:S(2)}) collective-permute-start(bf16[24,1536]{1,0:T(8,128)(2,1)S(1)} %get-tuple-element.35), channel_id=1, source_target_pairs={{0,4},{1,20},{2,6},{3,22},{4,8},{5,24},{6,10},{7,26},{8,12},{9,28}... | collective-permute-start | bytes 221192 | tf_op jit(solution)/shard_map/ppermute | solution.py:457
  9.8 3.8 %collective-permute-start.2 = (bf16[24,1536]{1,0:T(8,128)(2,1)S(1)}, bf16[24,1536]{1,0:T(8,128)(2,1)S(1)}, u32[]{:S(2)}, u32[]{:S(2)}) collective-permute-start(bf16[24,1536]{1,0:T(8,128)(2,1)S(1)} %get-tuple-element.36), channel_id=1, source_target_pairs={{0,8},{1,24},{2,10},{3,26},{4,12},{5,28},{6,14},{7,30},{8,0},{9,16... | collective-permute-start | bytes 221192 | tf_op jit(solution)/shard_map/ppermute | solution.py:457
  13.6 0.8 %collective-permute-start.3 = (bf16[24,1536]{1,0:T(8,128)(2,1)S(1)}, bf16[24,1536]{1,0:T(8,128)(2,1)S(1)}, u32[]{:S(2)}, u32[]{:S(2)}) collective-permute-start(bf16[24,1536]{1,0:T(8,128)(2,1)S(1)} %get-tuple-element.37), channel_id=1, source_target_pairs={{0,12},{1,28},{2,14},{3,30},{4,0},{5,16},{6,2},{7,18},{8,4},{9,20}... | collective-permute-start | bytes 221192 | tf_op jit(solution)/shard_map/ppermute | solution.py:457
  14.4 0.0 collective-permute-done.refs_0_
  14.4 0.9 %collective-permute-done.1.refs_1_ = bf16[24,1536]{1,0:T(8,128)(2,1)S(1)} collective-permute-done((bf16[24,1536]{1,0:T(8,128)(2,1)S(1)}, bf16[24,1536]{1,0:T(8,128)(2,1)S(1)}, u32[]{:S(2)}, u32[]{:S(2)}) %collective-permute-start.1) | collective-permute-done | bytes 73760 | tf_op jit(solution)/shard_map/ppermute | solution.py:457
  15.3 1.5 %collective-permute-done.2.refs_2_ = bf16[24,1536]{1,0:T(8,128)(2,1)S(1)} collective-permute-done((bf16[24,1536]{1,0:T(8,128)(2,1)S(1)}, bf16[24,1536]{1,0:T(8,128)(2,1)S(1)}, u32[]{:S(2)}, u32[]{:S(2)}) %collective-permute-start.2) | collective-permute-done | bytes 73760 | tf_op jit(solution)/shard_map/ppermute | solution.py:457
  16.9 1.4 %collective-permute-done.3.refs_3_ = bf16[24,1536]{1,0:T(8,128)(2,1)S(1)} collective-permute-done((bf16[24,1536]{1,0:T(8,128)(2,1)S(1)}, bf16[24,1536]{1,0:T(8,128)(2,1)S(1)}, u32[]{:S(2)}, u32[]{:S(2)}) %collective-permute-start.3) | collective-permute-done | bytes 73760 | tf_op jit(solution)/shard_map/ppermute | solution.py:457
  18.3 0.2 shard_map.111
  18.5 0.1 collective-permute-start.4
  18.6 1.3 %collective-permute-start.5 = (bf16[48,1536]{1,0:T(8,128)(2,1)S(1)}, bf16[48,1536]{1,0:T(8,128)(2,1)S(1)}, u32[]{:S(2)}, u32[]{:S(2)}) collective-permute-start(bf16[48,1536]{1,0:T(8,128)(2,1)S(1)} %get-tuple-element.38.refs_0_.refs_1_), channel_id=1, source_target_pairs={{0,2},{2,0},{4,6},{6,4},{8,10},{10,8},{12,14},{14,12},{1,3},{3,1},... | collective-permute-start | bytes 442376 | tf_op jit(solution)/shard_map/ppermute | solution.py:102
  19.9 1.4 %collective-permute-start.6 = (bf16[48,1536]{1,0:T(8,128)(2,1)S(1)}, bf16[48,1536]{1,0:T(8,128)(2,1)S(1)}, u32[]{:S(2)}, u32[]{:S(2)}) collective-permute-start(bf16[48,1536]{1,0:T(8,128)(2,1)S(1)} %get-tuple-element.38.refs_0_.refs_1_), channel_id=1, source_target_pairs={{0,18},{2,16},{4,22},{6,20},{8,26},{10,24},{12,30},{14,28},{16,2},... | collective-permute-start | bytes 442376 | tf_op jit(solution)/shard_map/ppermute | solution.py:115
  21.2 4.6 %shard_map.112 = (bf16[1536,2048]{1,0:T(8,128)(2,1)S(1)}, bf16[1536,2048]{1,0:T(8,128)(2,1)S(1)}) custom-call(bf16[1536,2048]{1,0:T(8,128)(2,1)} %refs_0_.2, bf16[1536,2048]{1,0:T(8,128)(2,1)} %refs_1_.1, bf16[24,1536]{1,0:T(8,128)(2,1)S(1)} %get-tuple-element.34.refs_2_), custom_call_target="tpu_custom_call" | custom-call | bytes 12582912 | tf_op jit(solution)/shard_map/pallas_call | solution.py:153
  25.8 0.1 collective-permute-start.12
  26.0 1.2 %collective-permute-start.13 = (bf16[48,1536]{1,0:T(8,128)(2,1)S(1)}, bf16[48,1536]{1,0:T(8,128)(2,1)S(1)}, u32[]{:S(2)}, u32[]{:S(2)}) collective-permute-start(bf16[48,1536]{1,0:T(8,128)(2,1)S(1)} %get-tuple-element.47.refs_0_), channel_id=1, source_target_pairs={{0,2},{2,0},{4,6},{6,4},{8,10},{10,8},{12,14},{14,12},{1,3},{3,1},... | collective-permute-start | bytes 442376 | tf_op jit(solution)/shard_map/ppermute | solution.py:102
  27.2 0.0 collective-permute-done.4.refs_1_
  27.2 1.4 %collective-permute-start.14 = (bf16[48,1536]{1,0:T(8,128)(2,1)S(1)}, bf16[48,1536]{1,0:T(8,128)(2,1)S(1)}, u32[]{:S(2)}, u32[]{:S(2)}) collective-permute-start(bf16[48,1536]{1,0:T(8,128)(2,1)S(1)} %get-tuple-element.47.refs_0_), channel_id=1, source_target_pairs={{0,18},{2,16},{4,22},{6,20},{8,26},{10,24},{12,30},{14,28},{16,2},... | collective-permute-start | bytes 442376 | tf_op jit(solution)/shard_map/ppermute | solution.py:115
  28.6 0.0 collective-permute-done.5.refs_2_
  28.6 0.0 collective-permute-done.6.refs_3_
  28.6 1.4 %shard_map.113 = (bf16[192,1536]{1,0:T(8,128)(2,1)S(1)}, bf16[192,2048]{1,0:T(8,128)(2,1)S(1)}) custom-call(bf16[48,1536]{1,0:T(8,128)(2,1)S(1)} %get-tuple-element.38.refs_0_.refs_1_, bf16[48,1536]{1,0:T(8,128)(2,1)S(1)} %collective-permute-done.4.refs_1_, bf16[48,1536]{1,0:T(8,128)(2,1)S(1)} %collective-permute-done.5.refs_2_, ...), custom_call_target="tpu_custom_call" | custom-call | flops 1207959552 | bytes 1966080 | tf_op jit(solution)/shard_map/pallas_call | solution.py:175
  30.0 0.5 collective-permute-start.7
  30.5 1.4 %shard_map.114.u0_ref = bf16[192,2048]{1,0:T(8,128)(2,1)S(1)} custom-call(bf16[192,1536]{1,0:T(8,128)(2,1)S(1)} %get-tuple-element.41.x_ref, bf16[1536,2048]{1,0:T(8,128)(2,1)S(1)} %get-tuple-element.42.w_ref.wu_ref), custom_call_target="tpu_custom_call" | custom-call | flops 1207959552 | bytes 1376256 | tf_op jit(solution)/shard_map/pallas_call | solution.py:192
  31.9 0.2 collective-permute-start.8
  32.0 2.8 %shard_map.115.w_ref.refs_4_ = bf16[1536,2048]{1,0:T(8,128)(2,1)S(1)} custom-call(bf16[1536,2048]{1,0:T(8,128)(2,1)} %refs_0_.3, bf16[48,1536]{1,0:T(8,128)(2,1)S(1)} %get-tuple-element.38.refs_0_.refs_1_), custom_call_target="tpu_custom_call" | custom-call | bytes 6291456 | tf_op jit(solution)/shard_map/pallas_call | solution.py:153
  34.8 0.0 collective-permute-done.12.refs_1_
  34.8 0.0 collective-permute-done.13.refs_2_
  34.8 1.0 %collective-permute-done.14.refs_3_ = bf16[48,1536]{1,0:T(8,128)(2,1)S(1)} collective-permute-done((bf16[48,1536]{1,0:T(8,128)(2,1)S(1)}, bf16[48,1536]{1,0:T(8,128)(2,1)S(1)}, u32[]{:S(2)}, u32[]{:S(2)}) %collective-permute-start.14) | collective-permute-done | bytes 147488 | tf_op jit(solution)/shard_map/ppermute | solution.py:115
  35.8 1.4 %shard_map.117 = (bf16[192,1536]{1,0:T(8,128)(2,1)S(1)}, bf16[192,2048]{1,0:T(8,128)(2,1)S(1)}) custom-call(bf16[48,1536]{1,0:T(8,128)(2,1)S(1)} %get-tuple-element.47.refs_0_, bf16[48,1536]{1,0:T(8,128)(2,1)S(1)} %collective-permute-done.12.refs_1_, bf16[48,1536]{1,0:T(8,128)(2,1)S(1)} %collective-permute-done.13.refs_2_, ...), custom_call_target="tpu_custom_call" | custom-call | flops 1207959552 | bytes 1966080 | tf_op jit(solution)/shard_map/pallas_call | solution.py:175
  37.2 0.8 %collective-permute-start.15 = (bf16[192,2048]{1,0:T(8,128)(2,1)S(1)}, bf16[192,2048]{1,0:T(8,128)(2,1)S(1)}, u32[]{:S(2)}, u32[]{:S(2)}) collective-permute-start(bf16[192,2048]{1,0:T(8,128)(2,1)S(1)} %get-tuple-element.48.a0_ref), channel_id=1, source_target_pairs={{0,1},{1,0},{2,3},{3,2},{4,5},{5,4},{6,7},{7,6},{8,9},{9,8},{10,11... | collective-permute-start | bytes 2359304 | tf_op jit(solution)/shard_map/ppermute | solution.py:446
  38.0 0.0 collective-permute-done.7.g1_ref
  38.0 0.0 collective-permute-done.8.u1_ref
  38.0 2.2 %shard_map.116 = (bf16[192,2048]{1,0:T(8,128)(2,1)S(1)}, bf16[48,1536]{1,0:T(8,128)(2,1)S(1)}, bf16[48,1536]{1,0:T(8,128)(2,1)S(1)}, bf16[48,1536]{1,0:T(8,128)(2,1)S(1)}, bf16[48,1536]{1,0:T(8,128)(2,1)S(1)}) custom-call(bf16[192,2048]{1,0:T(8,128)(2,1)S(1)} %get-tuple-element.40.g0_ref, bf16[192,2048]{1,0:T(8,128)(2,1)S(1)} %collective-permute-done.7.g1_ref, ...), custom_call_target="tpu_custom_call" | custom-call | flops 1207959552 | bytes 4521984 | tf_op jit(solution)/shard_map/pallas_call | solution.py:367
  40.2 0.5 collective-permute-start.9
  40.7 1.2 %collective-permute-start.10 = (bf16[48,1536]{1,0:T(8,128)(2,1)S(1)}, bf16[48,1536]{1,0:T(8,128)(2,1)S(1)}, u32[]{:S(2)}, u32[]{:S(2)}) collective-permute-start(bf16[48,1536]{1,0:T(8,128)(2,1)S(1)} %get-tuple-element.45), channel_id=1, source_target_pairs={{0,2},{2,0},{4,6},{6,4},{8,10},{10,8},{12,14},{14,12},{1,3},{3,1},... | collective-permute-start | bytes 442376 | tf_op jit(solution)/shard_map/ppermute | solution.py:102
  41.9 1.0 %collective-permute-start.11 = (bf16[48,1536]{1,0:T(8,128)(2,1)S(1)}, bf16[48,1536]{1,0:T(8,128)(2,1)S(1)}, u32[]{:S(2)}, u32[]{:S(2)}) collective-permute-start(bf16[48,1536]{1,0:T(8,128)(2,1)S(1)} %get-tuple-element.46), channel_id=1, source_target_pairs={{0,18},{2,16},{4,22},{6,20},{8,26},{10,24},{12,30},{14,28},{16,2},... | collective-permute-start | bytes 442376 | tf_op jit(solution)/shard_map/ppermute | solution.py:115
  42.9 0.0 collective-permute-done.15.a1_ref
  42.9 4.4 %shard_map.118 = (bf16[192,2048]{1,0:T(8,128)(2,1)S(1)}, bf16[192,2048]{1,0:T(8,128)(2,1)S(1)}, bf16[48,1536]{1,0:T(8,128)(2,1)S(1)}, bf16[48,1536]{1,0:T(8,128)...) custom-call(bf16[192,2048]{1,0:T(8,128)(2,1)S(1)} %get-tuple-element.40.g0_ref, ...), custom_call_target="tpu_custom_call" | custom-call | flops 2415919104 | bytes 6881280 | tf_op jit(solution)/shard_map/pallas_call | solution.py:401
  47.3 0.5 collective-permute-start.16
  47.8 1.2 %collective-permute-start.17 = (bf16[48,1536]{1,0:T(8,128)(2,1)S(1)}, bf16[48,1536]{1,0:T(8,128)(2,1)S(1)}, u32[]{:S(2)}, u32[]{:S(2)}) collective-permute-start(bf16[48,1536]{1,0:T(8,128)(2,1)S(1)} %get-tuple-element.51), channel_id=1, source_target_pairs={{0,2},{2,0},{4,6},{6,4},{8,10},{10,8},{12,14},{14,12},{1,3},{3,1},... | collective-permute-start | bytes 442376 | tf_op jit(solution)/shard_map/ppermute | solution.py:102
  49.0 0.0 collective-permute-done.9.refs_1_
  49.0 1.0 %collective-permute-start.18 = (bf16[48,1536]{1,0:T(8,128)(2,1)S(1)}, bf16[48,1536]{1,0:T(8,128)(2,1)S(1)}, u32[]{:S(2)}, u32[]{:S(2)}) collective-permute-start(bf16[48,1536]{1,0:T(8,128)(2,1)S(1)} %get-tuple-element.52), channel_id=1, source_target_pairs={{0,18},{2,16},{4,22},{6,20},{8,26},{10,24},{12,30},{14,28},{16,2},... | collective-permute-start | bytes 442376 | tf_op jit(solution)/shard_map/ppermute | solution.py:115
  50.1 3.2 %shard_map.121 = bf16[1536,2048]{1,0:T(8,128)(2,1)} custom-call(bf16[192,1536]{1,0:T(8,128)(2,1)S(1)} %get-tuple-element.41.x_ref, bf16[192,2048]{1,0:T(8,128)(2,1)S(1)} %get-tuple-element.59.y_ref), custom_call_target="tpu_custom_call" | custom-call | flops 1207959552 | bytes 7667712 | tf_op jit(solution)/shard_map/pallas_call | solution.py:430
  53.3 3.2 %shard_map.122 = bf16[1536,2048]{1,0:T(8,128)(2,1)} custom-call(bf16[192,1536]{1,0:T(8,128)(2,1)S(1)} %get-tuple-element.41.x_ref, bf16[192,2048]{1,0:T(8,128)(2,1)S(1)} %get-tuple-element.60.y_ref), custom_call_target="tpu_custom_call" | custom-call | flops 1207959552 | bytes 7667712 | tf_op jit(solution)/shard_map/pallas_call | solution.py:430
  56.5 0.0 copy-start.3
  56.5 0.0 copy-start.5
  56.5 0.0 collective-permute-done.10.refs_2_
  56.5 0.0 collective-permute-done.11.refs_3_
  56.5 0.0 collective-permute-done.16.refs_5_
  56.5 0.0 collective-permute-done.17.refs_6_
  56.5 0.3 shard_map.119
  56.9 3.9 %collective-permute-start.19 = (bf16[24,1536]{1,0:T(8,128)(2,1)S(1)}, bf16[24,1536]{1,0:T(8,128)(2,1)S(1)}, u32[]{:S(2)}, u32[]{:S(2)}) collective-permute-start(bf16[24,1536]{1,0:T(8,128)(2,1)S(1)} %get-tuple-element.53), channel_id=1, source_target_pairs={{0,0},{1,16},{2,2},{3,18},{4,4},{5,20},{6,6},{7,22},{8,8},{9,24},{... | collective-permute-start | bytes 221192 | tf_op jit(solution)/shard_map/ppermute | solution.py:457
  60.8 2.5 %collective-permute-start.20 = (bf16[24,1536]{1,0:T(8,128)(2,1)S(1)}, bf16[24,1536]{1,0:T(8,128)(2,1)S(1)}, u32[]{:S(2)}, u32[]{:S(2)}) collective-permute-start(bf16[24,1536]{1,0:T(8,128)(2,1)S(1)} %get-tuple-element.54), channel_id=1, source_target_pairs={{0,12},{1,28},{2,14},{3,30},{4,0},{5,16},{6,2},{7,18},{8,4},{9,20}... | collective-permute-start | bytes 221192 | tf_op jit(solution)/shard_map/ppermute | solution.py:457
  63.3 0.9 %collective-permute-start.21 = (bf16[24,1536]{1,0:T(8,128)(2,1)S(1)}, bf16[24,1536]{1,0:T(8,128)(2,1)S(1)}, u32[]{:S(2)}, u32[]{:S(2)}) collective-permute-start(bf16[24,1536]{1,0:T(8,128)(2,1)S(1)} %get-tuple-element.55), channel_id=1, source_target_pairs={{0,8},{1,24},{2,10},{3,26},{4,12},{5,28},{6,14},{7,30},{8,0},{9,16... | collective-permute-start | bytes 221192 | tf_op jit(solution)/shard_map/ppermute | solution.py:457
  64.2 0.9 %collective-permute-start.22 = (bf16[24,1536]{1,0:T(8,128)(2,1)S(1)}, bf16[24,1536]{1,0:T(8,128)(2,1)S(1)}, u32[]{:S(2)}, u32[]{:S(2)}) collective-permute-start(bf16[24,1536]{1,0:T(8,128)(2,1)S(1)} %get-tuple-element.56), channel_id=1, source_target_pairs={{0,4},{1,20},{2,6},{3,22},{4,8},{5,24},{6,10},{7,26},{8,12},{9,28}... | collective-permute-start | bytes 221192 | tf_op jit(solution)/shard_map/ppermute | solution.py:457
  65.1 3.2 %shard_map.123 = bf16[1536,2048]{1,0:T(8,128)(2,1)} custom-call(bf16[192,1536]{1,0:T(8,128)(2,1)S(1)} %get-tuple-element.61.x_ref, bf16[192,2048]{1,0:T(8,128)(2,1)S(1)} %get-tuple-element.62.y_ref), custom_call_target="tpu_custom_call" | custom-call | flops 1207959552 | bytes 7667712 | tf_op jit(solution)/shard_map/pallas_call | solution.py:430
  68.3 0.0 collective-permute-done.19.refs_0_
  68.3 0.5 collective-permute-done.21.refs_2_
  68.9 1.8 %collective-permute-done.22.refs_3_ = bf16[24,1536]{1,0:T(8,128)(2,1)S(1)} collective-permute-done((bf16[24,1536]{1,0:T(8,128)(2,1)S(1)}, bf16[24,1536]{1,0:T(8,128)(2,1)S(1)}, u32[]{:S(2)}, u32[]{:S(2)}) %collective-permute-start.22) | collective-permute-done | bytes 73760 | tf_op jit(solution)/shard_map/ppermute | solution.py:457
  70.7 1.0 %shard_map.120 = (bf16[16,1536]{1,0:T(8,128)(2,1)}, bf16[16,1536]{1,0:T(8,128)(2,1)}) custom-call(bf16[24,1536]{1,0:T(8,128)(2,1)S(1)} %collective-permute-done.19.refs_0_, bf16[24,1536]{1,0:T(8,128)(2,1)S(1)} %collective-permute-done.20.refs_1_, bf16[24,1536]{1,0:T(8,128)(2,1)S(1)} %collective-permute-done.21.refs_2_, ...), custom_call_target="tpu_custom_call" | custom-call | bytes 393216 | tf_op jit(solution)/shard_map/pallas_call | solution.py:335
  (8 shorter events, 0.0 us)
Async XLA Ops:
  0.6 0.9 %copy-start = (bf16[16,3072]{1,0:T(8,128)(2,1)S(1)}, bf16[16,3072]{1,0:T(8,128)(2,1)}, u32[]{:S(2)}) copy-start(bf16[16,3072]{1,0:T(8,128)(2,1)} %tok_ref.1) | copy-start | bytes 294916
  1.5 0.9 %copy-start.1 = (bf16[16,3072]{1,0:T(8,128)(2,1)S(1)}, bf16[16,3072]{1,0:T(8,128)(2,1)}, u32[]{:S(2)}) copy-start(bf16[16,3072]{1,0:T(8,128)(2,1)} %grad_ref.1) | copy-start | bytes 294916
  2.4 0.7 copy-start.2
  3.1 0.7 copy-start.4
  4.2 10.2 %collective-permute-start = (bf16[24,1536]{1,0:T(8,128)(2,1)S(1)}, bf16[24,1536]{1,0:T(8,128)(2,1)S(1)}, u32[]{:S(2)}, u32[]{:S(2)}) collective-permute-start(bf16[24,1536]{1,0:T(8,128)(2,1)S(1)} %get-tuple-element.34.refs_2_), channel_id=1, source_target_pairs={{0,0},{1,16},{2,2},{3,18},{4,4},{5,20},{6,6},{7,22},{8,8},{9,24},{... | collective-permute-start | bytes 221192 | tf_op jit(solution)/shard_map/ppermute | solution.py:457
  8.8 6.6 %collective-permute-start.1 = (bf16[24,1536]{1,0:T(8,128)(2,1)S(1)}, bf16[24,1536]{1,0:T(8,128)(2,1)S(1)}, u32[]{:S(2)}, u32[]{:S(2)}) collective-permute-start(bf16[24,1536]{1,0:T(8,128)(2,1)S(1)} %get-tuple-element.35), channel_id=1, source_target_pairs={{0,4},{1,20},{2,6},{3,22},{4,8},{5,24},{6,10},{7,26},{8,12},{9,28}... | collective-permute-start | bytes 221192 | tf_op jit(solution)/shard_map/ppermute | solution.py:457
  9.8 7.0 %collective-permute-start.2 = (bf16[24,1536]{1,0:T(8,128)(2,1)S(1)}, bf16[24,1536]{1,0:T(8,128)(2,1)S(1)}, u32[]{:S(2)}, u32[]{:S(2)}) collective-permute-start(bf16[24,1536]{1,0:T(8,128)(2,1)S(1)} %get-tuple-element.36), channel_id=1, source_target_pairs={{0,8},{1,24},{2,10},{3,26},{4,12},{5,28},{6,14},{7,30},{8,0},{9,16... | collective-permute-start | bytes 221192 | tf_op jit(solution)/shard_map/ppermute | solution.py:457
  13.6 4.7 %collective-permute-start.3 = (bf16[24,1536]{1,0:T(8,128)(2,1)S(1)}, bf16[24,1536]{1,0:T(8,128)(2,1)S(1)}, u32[]{:S(2)}, u32[]{:S(2)}) collective-permute-start(bf16[24,1536]{1,0:T(8,128)(2,1)S(1)} %get-tuple-element.37), channel_id=1, source_target_pairs={{0,12},{1,28},{2,14},{3,30},{4,0},{5,16},{6,2},{7,18},{8,4},{9,20}... | collective-permute-start | bytes 221192 | tf_op jit(solution)/shard_map/ppermute | solution.py:457
  18.5 8.7 %collective-permute-start.4 = (bf16[48,1536]{1,0:T(8,128)(2,1)S(1)}, bf16[48,1536]{1,0:T(8,128)(2,1)S(1)}, u32[]{:S(2)}, u32[]{:S(2)}) collective-permute-start(bf16[48,1536]{1,0:T(8,128)(2,1)S(1)} %get-tuple-element.38.refs_0_.refs_1_), channel_id=1, source_target_pairs={{0,16},{16,0},{1,17},{17,1},{2,18},{18,2},{3,19},{19,3},{4,20},{20... | collective-permute-start | bytes 442376 | tf_op jit(solution)/shard_map/ppermute | solution.py:106
  18.6 10.0 %collective-permute-start.5 = (bf16[48,1536]{1,0:T(8,128)(2,1)S(1)}, bf16[48,1536]{1,0:T(8,128)(2,1)S(1)}, u32[]{:S(2)}, u32[]{:S(2)}) collective-permute-start(bf16[48,1536]{1,0:T(8,128)(2,1)S(1)} %get-tuple-element.38.refs_0_.refs_1_), channel_id=1, source_target_pairs={{0,2},{2,0},{4,6},{6,4},{8,10},{10,8},{12,14},{14,12},{1,3},{3,1},... | collective-permute-start | bytes 442376 | tf_op jit(solution)/shard_map/ppermute | solution.py:102
  19.9 8.7 %collective-permute-start.6 = (bf16[48,1536]{1,0:T(8,128)(2,1)S(1)}, bf16[48,1536]{1,0:T(8,128)(2,1)S(1)}, u32[]{:S(2)}, u32[]{:S(2)}) collective-permute-start(bf16[48,1536]{1,0:T(8,128)(2,1)S(1)} %get-tuple-element.38.refs_0_.refs_1_), channel_id=1, source_target_pairs={{0,18},{2,16},{4,22},{6,20},{8,26},{10,24},{12,30},{14,28},{16,2},... | collective-permute-start | bytes 442376 | tf_op jit(solution)/shard_map/ppermute | solution.py:115
  25.8 9.0 %collective-permute-start.12 = (bf16[48,1536]{1,0:T(8,128)(2,1)S(1)}, bf16[48,1536]{1,0:T(8,128)(2,1)S(1)}, u32[]{:S(2)}, u32[]{:S(2)}) collective-permute-start(bf16[48,1536]{1,0:T(8,128)(2,1)S(1)} %get-tuple-element.47.refs_0_), channel_id=1, source_target_pairs={{0,16},{16,0},{1,17},{17,1},{2,18},{18,2},{3,19},{19,3},{4,20},{20... | collective-permute-start | bytes 442376 | tf_op jit(solution)/shard_map/ppermute | solution.py:106
  26.0 8.8 %collective-permute-start.13 = (bf16[48,1536]{1,0:T(8,128)(2,1)S(1)}, bf16[48,1536]{1,0:T(8,128)(2,1)S(1)}, u32[]{:S(2)}, u32[]{:S(2)}) collective-permute-start(bf16[48,1536]{1,0:T(8,128)(2,1)S(1)} %get-tuple-element.47.refs_0_), channel_id=1, source_target_pairs={{0,2},{2,0},{4,6},{6,4},{8,10},{10,8},{12,14},{14,12},{1,3},{3,1},... | collective-permute-start | bytes 442376 | tf_op jit(solution)/shard_map/ppermute | solution.py:102
  27.2 8.6 %collective-permute-start.14 = (bf16[48,1536]{1,0:T(8,128)(2,1)S(1)}, bf16[48,1536]{1,0:T(8,128)(2,1)S(1)}, u32[]{:S(2)}, u32[]{:S(2)}) collective-permute-start(bf16[48,1536]{1,0:T(8,128)(2,1)S(1)} %get-tuple-element.47.refs_0_), channel_id=1, source_target_pairs={{0,18},{2,16},{4,22},{6,20},{8,26},{10,24},{12,30},{14,28},{16,2},... | collective-permute-start | bytes 442376 | tf_op jit(solution)/shard_map/ppermute | solution.py:115
  30.0 8.0 %collective-permute-start.7 = (bf16[192,2048]{1,0:T(8,128)(2,1)S(1)}, bf16[192,2048]{1,0:T(8,128)(2,1)S(1)}, u32[]{:S(2)}, u32[]{:S(2)}) collective-permute-start(bf16[192,2048]{1,0:T(8,128)(2,1)S(1)} %get-tuple-element.40.g0_ref), channel_id=1, source_target_pairs={{0,1},{1,0},{2,3},{3,2},{4,5},{5,4},{6,7},{7,6},{8,9},{9,8},{10,11... | collective-permute-start | bytes 2359304 | tf_op jit(solution)/shard_map/ppermute | solution.py:446
  31.9 6.1 %collective-permute-start.8 = (bf16[192,2048]{1,0:T(8,128)(2,1)S(1)}, bf16[192,2048]{1,0:T(8,128)(2,1)S(1)}, u32[]{:S(2)}, u32[]{:S(2)}) collective-permute-start(bf16[192,2048]{1,0:T(8,128)(2,1)S(1)} %shard_map.114.u0_ref), channel_id=1, source_target_pairs={{0,1},{1,0},{2,3},{3,2},{4,5},{5,4},{6,7},{7,6},{8,9},{9,8},{10,11... | collective-permute-start | bytes 2359304 | tf_op jit(solution)/shard_map/ppermute | solution.py:446
  37.2 5.7 %collective-permute-start.15 = (bf16[192,2048]{1,0:T(8,128)(2,1)S(1)}, bf16[192,2048]{1,0:T(8,128)(2,1)S(1)}, u32[]{:S(2)}, u32[]{:S(2)}) collective-permute-start(bf16[192,2048]{1,0:T(8,128)(2,1)S(1)} %get-tuple-element.48.a0_ref), channel_id=1, source_target_pairs={{0,1},{1,0},{2,3},{3,2},{4,5},{5,4},{6,7},{7,6},{8,9},{9,8},{10,11... | collective-permute-start | bytes 2359304 | tf_op jit(solution)/shard_map/ppermute | solution.py:446
  40.2 8.8 %collective-permute-start.9 = (bf16[48,1536]{1,0:T(8,128)(2,1)S(1)}, bf16[48,1536]{1,0:T(8,128)(2,1)S(1)}, u32[]{:S(2)}, u32[]{:S(2)}) collective-permute-start(bf16[48,1536]{1,0:T(8,128)(2,1)S(1)} %get-tuple-element.44), channel_id=1, source_target_pairs={{0,16},{16,0},{1,17},{17,1},{2,18},{18,2},{3,19},{19,3},{4,20},{20... | collective-permute-start | bytes 442376 | tf_op jit(solution)/shard_map/ppermute | solution.py:106
  40.7 15.8 %collective-permute-start.10 = (bf16[48,1536]{1,0:T(8,128)(2,1)S(1)}, bf16[48,1536]{1,0:T(8,128)(2,1)S(1)}, u32[]{:S(2)}, u32[]{:S(2)}) collective-permute-start(bf16[48,1536]{1,0:T(8,128)(2,1)S(1)} %get-tuple-element.45), channel_id=1, source_target_pairs={{0,2},{2,0},{4,6},{6,4},{8,10},{10,8},{12,14},{14,12},{1,3},{3,1},... | collective-permute-start | bytes 442376 | tf_op jit(solution)/shard_map/ppermute | solution.py:102
  41.9 14.6 %collective-permute-start.11 = (bf16[48,1536]{1,0:T(8,128)(2,1)S(1)}, bf16[48,1536]{1,0:T(8,128)(2,1)S(1)}, u32[]{:S(2)}, u32[]{:S(2)}) collective-permute-start(bf16[48,1536]{1,0:T(8,128)(2,1)S(1)} %get-tuple-element.46), channel_id=1, source_target_pairs={{0,18},{2,16},{4,22},{6,20},{8,26},{10,24},{12,30},{14,28},{16,2},... | collective-permute-start | bytes 442376 | tf_op jit(solution)/shard_map/ppermute | solution.py:115
  47.3 9.2 %collective-permute-start.16 = (bf16[48,1536]{1,0:T(8,128)(2,1)S(1)}, bf16[48,1536]{1,0:T(8,128)(2,1)S(1)}, u32[]{:S(2)}, u32[]{:S(2)}) collective-permute-start(bf16[48,1536]{1,0:T(8,128)(2,1)S(1)} %get-tuple-element.50), channel_id=1, source_target_pairs={{0,16},{16,0},{1,17},{17,1},{2,18},{18,2},{3,19},{19,3},{4,20},{20... | collective-permute-start | bytes 442376 | tf_op jit(solution)/shard_map/ppermute | solution.py:106
  47.8 8.7 %collective-permute-start.17 = (bf16[48,1536]{1,0:T(8,128)(2,1)S(1)}, bf16[48,1536]{1,0:T(8,128)(2,1)S(1)}, u32[]{:S(2)}, u32[]{:S(2)}) collective-permute-start(bf16[48,1536]{1,0:T(8,128)(2,1)S(1)} %get-tuple-element.51), channel_id=1, source_target_pairs={{0,2},{2,0},{4,6},{6,4},{8,10},{10,8},{12,14},{14,12},{1,3},{3,1},... | collective-permute-start | bytes 442376 | tf_op jit(solution)/shard_map/ppermute | solution.py:102
  49.0 7.5 %collective-permute-start.18 = (bf16[48,1536]{1,0:T(8,128)(2,1)S(1)}, bf16[48,1536]{1,0:T(8,128)(2,1)S(1)}, u32[]{:S(2)}, u32[]{:S(2)}) collective-permute-start(bf16[48,1536]{1,0:T(8,128)(2,1)S(1)} %get-tuple-element.52), channel_id=1, source_target_pairs={{0,18},{2,16},{4,22},{6,20},{8,26},{10,24},{12,30},{14,28},{16,2},... | collective-permute-start | bytes 442376 | tf_op jit(solution)/shard_map/ppermute | solution.py:115
  56.5 14.3 %copy-start.3 = (s32[16,2]{0,1:T(2,128)S(1)}, s32[16,2]{0,1:T(2,128)}, u32[]{:S(2)}) copy-start(s32[16,2]{0,1:T(2,128)} %param.9) | copy-start | bytes 388
  56.5 14.3 %copy-start.5 = (f32[16,2]{0,1:T(2,128)S(1)}, f32[16,2]{0,1:T(2,128)}, u32[]{:S(2)}) copy-start(f32[16,2]{0,1:T(2,128)} %param.10) | copy-start | bytes 388
  56.9 11.5 %collective-permute-start.19 = (bf16[24,1536]{1,0:T(8,128)(2,1)S(1)}, bf16[24,1536]{1,0:T(8,128)(2,1)S(1)}, u32[]{:S(2)}, u32[]{:S(2)}) collective-permute-start(bf16[24,1536]{1,0:T(8,128)(2,1)S(1)} %get-tuple-element.53), channel_id=1, source_target_pairs={{0,0},{1,16},{2,2},{3,18},{4,4},{5,20},{6,6},{7,22},{8,8},{9,24},{... | collective-permute-start | bytes 221192 | tf_op jit(solution)/shard_map/ppermute | solution.py:457
  60.8 7.6 %collective-permute-start.20 = (bf16[24,1536]{1,0:T(8,128)(2,1)S(1)}, bf16[24,1536]{1,0:T(8,128)(2,1)S(1)}, u32[]{:S(2)}, u32[]{:S(2)}) collective-permute-start(bf16[24,1536]{1,0:T(8,128)(2,1)S(1)} %get-tuple-element.54), channel_id=1, source_target_pairs={{0,12},{1,28},{2,14},{3,30},{4,0},{5,16},{6,2},{7,18},{8,4},{9,20}... | collective-permute-start | bytes 221192 | tf_op jit(solution)/shard_map/ppermute | solution.py:457
  63.3 5.6 %collective-permute-start.21 = (bf16[24,1536]{1,0:T(8,128)(2,1)S(1)}, bf16[24,1536]{1,0:T(8,128)(2,1)S(1)}, u32[]{:S(2)}, u32[]{:S(2)}) collective-permute-start(bf16[24,1536]{1,0:T(8,128)(2,1)S(1)} %get-tuple-element.55), channel_id=1, source_target_pairs={{0,8},{1,24},{2,10},{3,26},{4,12},{5,28},{6,14},{7,30},{8,0},{9,16... | collective-permute-start | bytes 221192 | tf_op jit(solution)/shard_map/ppermute | solution.py:457
  64.2 6.5 %collective-permute-start.22 = (bf16[24,1536]{1,0:T(8,128)(2,1)S(1)}, bf16[24,1536]{1,0:T(8,128)(2,1)S(1)}, u32[]{:S(2)}, u32[]{:S(2)}) collective-permute-start(bf16[24,1536]{1,0:T(8,128)(2,1)S(1)} %get-tuple-element.56), channel_id=1, source_target_pairs={{0,4},{1,20},{2,6},{3,22},{4,8},{5,24},{6,10},{7,26},{8,12},{9,28}... | collective-permute-start | bytes 221192 | tf_op jit(solution)/shard_map/ppermute | solution.py:457

commit v3 on v2

--- a/solution.py
+++ b/solution.py
@@ -109,11 +109,8 @@
 def swap_plane(pieces):
     size = lax.axis_size("expert")
     both = [(s * size + i, (1 - s) * size + (i ^ 1)) for s in range(2) for i in range(size)]
-    return [
-        swap_section(pieces[0]),
-        swap_expert(pieces[1]),
-        lax.ppermute(pieces[2], ("section", "expert"), both),
-    ]
+    far = lax.ppermute(pieces[2], ("section", "expert"), both)
+    return [swap_section(pieces[0]), swap_expert(pieces[1]), far]
 
 
 ANYWHERE = pl.BlockSpec(memory_space=pl.ANY)
@@ -156,30 +153,30 @@
         in_specs=[ANYWHERE] * (count + 1),
         out_specs=[ANYWHERE] * count,
         scratch_shapes=[pltpu.SemaphoreType.DMA((count,))],
-        cost_estimate=cost(0, *weights),
+        cost_estimate=cost(0),
         compiler_params=params(1),
     )(*(in_hbm(weight) for weight in weights), after)
 
 
 def gather_kernel(*refs):
-    pieces, (w_ref, x_ref, out_ref) = refs[:-3], refs[-3:]
+    pieces, (w_ref, _, x_ref, out_ref) = refs[:-4][::-1], refs[-4:]
     rows = pieces[0].shape[0]
     for i, piece in enumerate(pieces):
         x_ref[i * rows : (i + 1) * rows] = piece[...]
     out_ref[...] = jnp.dot(x_ref[...], w_ref[...], preferred_element_type=F32).astype(BF)
 
 
-def gather_project(pieces, weight):
+def gather_project(pieces, weight, after):
     rows, (depth, hidden) = sum(piece.shape[0] for piece in pieces), weight.shape
     outs = [jax.ShapeDtypeStruct((rows, depth), BF), jax.ShapeDtypeStruct((rows, hidden), BF)]
     return pl.pallas_call(
         gather_kernel,
         out_shape=outs,
-        in_specs=[INSIDE] * (len(pieces) + 1),
+        in_specs=[INSIDE] * (len(pieces) + 1) + [ANYWHERE],
         out_specs=[INSIDE] * 2,
-        cost_estimate=cost(2 * rows * depth * hidden, *pieces, *outs),
+        cost_estimate=cost(0),
         compiler_params=params(14),
-    )(*pieces, in_vmem(weight))
+    )(*pieces[::-1], in_vmem(weight), after)
 
 
 def project_kernel(x_ref, w_ref, out_ref):
@@ -194,7 +191,7 @@
         out_shape=out,
         in_specs=[INSIDE] * 2,
         out_specs=INSIDE,
-        cost_estimate=cost(2 * rows * depth * hidden, x, out),
+        cost_estimate=cost(0),
         compiler_params=params(12),
     )(x, in_vmem(weight))
 
@@ -208,7 +205,7 @@
     shape = (EXP * 2 * CAP, count)
     row = iota(shape, 0)
     place = row % (2 * CAP)
-    expert = (plane + row // (2 * CAP)) % EXP
+    expert = plane ^ (row // (2 * CAP))
     match = [ids_ref[j : j + 1, :] == expert for j in range(2)]
     chosen = jnp.logical_or(*match)
     before = (iota((count, count), 0) < iota((count, count), 1)).astype(F32)
@@ -217,15 +214,23 @@
     return match, picks, place
 
 
-def pack_kernel(tok_ref, grad_ref, ids_ref, probs_ref, *out_refs):
+def pack_kernel(*refs):
+    hbm, out_refs, held, sem = refs[:4], refs[4 : 4 + EXP], refs[4 + EXP : 8 + EXP], refs[-1]
     half = out_refs[0].shape[1]
-    start = pl.multiple_of(lax.axis_index("section") * half, half)
+    cut = pl.ds(pl.multiple_of(lax.axis_index("section") * half, half), half)
+    sources = [hbm[0].at[:, cut], hbm[1].at[:, cut], hbm[2], hbm[3]]
+    copies = [pltpu.make_async_copy(a, b, sem.at[i]) for i, (a, b) in enumerate(zip(sources, held))]
+    for copy in copies:
+        copy.start()
+    for copy in copies:
+        copy.wait()
+    tok_ref, grad_ref, ids_ref, probs_ref = held
     match, picks, place = slot_rows(ids_ref, lax.axis_index("expert") // 2)
     share = jnp.where(match[0], probs_ref[0:1, :], 0.0) + jnp.where(match[1], probs_ref[1:2, :], 0.0)
     scale = jnp.sum(jnp.where(picks, share, 0.0), axis=1, keepdims=True)
     picks = picks.astype(BF)
-    tok = jnp.dot(picks, tok_ref[:, pl.ds(start, half)], preferred_element_type=F32)
-    grad = jnp.dot(picks, grad_ref[:, pl.ds(start, half)], preferred_element_type=F32)
+    tok = jnp.dot(picks, tok_ref[...], preferred_element_type=F32)
+    grad = jnp.dot(picks, grad_ref[...], preferred_element_type=F32)
     payload = jnp.where(place[:, 0:1] < CAP, tok, grad * scale)
     for k, out_ref in enumerate(out_refs):
         out_ref[...] = payload[k * 2 * CAP : (k + 1) * 2 * CAP].astype(BF)
@@ -233,14 +238,23 @@
 
 def pack(tokens, grad_out, expert_ids, gate_probs, half):
     outs = [jax.ShapeDtypeStruct((2 * CAP, half), BF)] * EXP
+    rows = tokens.shape[0]
+    given = (tokens, grad_out, expert_ids.T, gate_probs.T)
     return pl.pallas_call(
         pack_kernel,
         out_shape=outs,
-        in_specs=[INSIDE] * 4,
+        in_specs=[ANYWHERE] * 4,
         out_specs=[INSIDE] * EXP,
+        scratch_shapes=[
+            pltpu.VMEM((rows, half), BF),
+            pltpu.VMEM((rows, half), BF),
+            pltpu.VMEM((2, rows), jnp.int32),
+            pltpu.VMEM((2, rows), F32),
+            pltpu.SemaphoreType.DMA((4,)),
+        ],
         cost_estimate=cost(0, tokens, grad_out, *outs),
         compiler_params=params(8),
-    )(tokens, grad_out, expert_ids.T, gate_probs.T)
+    )(*(in_hbm(array) for array in given))
 
 
 def sorting():
@@ -259,25 +273,25 @@
 
 
 def part_kernel(*refs):
-    refs, (tok_ref, grad_ref, held_ref) = refs[:EXP], refs[EXP:]
+    refs, (_, tok_ref, grad_ref, held_ref) = refs[:EXP][::-1], refs[EXP:]
     rows = jnp.dot(sorting(), stack(refs, held_ref), preferred_element_type=F32).astype(BF)
     n = EXP * CAP
     tok_ref[...] = rows[:n]
     grad_ref[...] = rows[n:]
 
 
-def part(got):
+def part(got, after):
     width = got[0].shape[1]
     outs = [jax.ShapeDtypeStruct((EXP * CAP, width), BF)] * 2
     return pl.pallas_call(
         part_kernel,
         out_shape=outs,
-        in_specs=[INSIDE] * EXP,
+        in_specs=[INSIDE] * EXP + [ANYWHERE],
         out_specs=[INSIDE] * 2,
         scratch_shapes=[pltpu.VMEM((2 * EXP * CAP, width), F32)],
         cost_estimate=cost(0, *got, *outs),
         compiler_params=params(8),
-    )(*got)
+    )(*got[::-1], after)
 
 
 def join_kernel(*refs):
@@ -304,11 +318,11 @@
         out_specs=[INSIDE] * EXP,
         cost_estimate=cost(0, *outs, *ins, *sent),
         compiler_params=params(10),
-    )(*outs, *ins)
+    )(*outs[::-1], *ins[::-1])
 
 
 def unpack_kernel(*refs):
-    refs, (ids_ref, probs_ref, out_ref, in_ref, held_ref) = refs[:EXP], refs[EXP:]
+    refs, (ids_ref, probs_ref, out_ref, in_ref, held_ref) = refs[:EXP][::-1], refs[EXP:]
     match, picks, place = slot_rows(ids_ref, lax.axis_index("expert") // 2)
     rows = stack(refs, held_ref)
     count = ids_ref.shape[1]
@@ -340,7 +354,7 @@
         scratch_shapes=[pltpu.VMEM((2 * EXP * CAP, width), F32)],
         cost_estimate=cost(0, *back, *outs),
         compiler_params=params(8),
-    )(*back, expert_ids.T, gate_probs.T)
+    )(*back[::-1], expert_ids.T, gate_probs.T)
 
 
 def spread(rows, refs):
@@ -349,63 +363,88 @@
         ref[...] = rows[i * count : (i + 1) * count].astype(BF)
 
 
-def forward_kernel(g0_ref, g1_ref, u0_ref, u1_ref, w_ref, act_ref, *out_refs):
+def times_rows(lefts, weights, turned, refs):
+    depth = weights[0].shape[0]
+    tile = math.gcd(depth, TILE)
+    for left, held in zip(lefts, turned):
+        held[...] = left[...].T
+    for at in range(0, depth, tile):
+        cut = slice(at, at + tile)
+        spread(
+            sum(
+                jnp.dot(weight[cut], held[...], preferred_element_type=F32)
+                for weight, held in zip(weights, turned)
+            )
+            .astype(BF)
+            .T,
+            refs,
+            cut,
+        )
+
+
+def spread(rows, refs, cut):
+    count = refs[0].shape[0]
+    for i, ref in enumerate(refs):
+        ref[:, cut] = rows[i * count : (i + 1) * count]
+
+
+def forward_kernel(g0_ref, g1_ref, u0_ref, u1_ref, w_ref, act_ref, silu_ref, slope_ref, *refs):
     hidden = act_ref.shape[1]
     tile = math.gcd(hidden, TILE)
     for at in range(0, hidden, tile):
         cut = slice(at, at + tile)
         gate_pre = g0_ref[:, cut].astype(F32) + g1_ref[:, cut].astype(F32)
         up_pre = u0_ref[:, cut].astype(F32) + u1_ref[:, cut].astype(F32)
-        act_ref[:, cut] = (gate_pre * jax.nn.sigmoid(gate_pre) * up_pre).astype(BF)
-    spread(contract_cols(act_ref[...], w_ref[...]), out_refs)
+        sigmoid_gate = jax.nn.sigmoid(gate_pre)
+        silu_value = gate_pre * sigmoid_gate
+        act_ref[:, cut] = (silu_value * up_pre).astype(BF)
+        silu_ref[:, cut] = silu_value
+        slope_ref[:, cut] = up_pre * sigmoid_gate * (1.0 + gate_pre * (1.0 - sigmoid_gate))
+    times_rows([act_ref], [w_ref], refs[4:], refs[:4])
 
 
 def forward(gates, ups, weight):
     rows, (depth, hidden) = gates[0].shape[0], weight.shape
     outs = [jax.ShapeDtypeStruct((rows, hidden), BF)]
+    outs += [jax.ShapeDtypeStruct((rows, hidden), F32)] * 2
     outs += [jax.ShapeDtypeStruct((rows // 4, depth), BF)] * 4
     return pl.pallas_call(
         forward_kernel,
         out_shape=outs,
         in_specs=[INSIDE] * 5,
-        out_specs=[INSIDE] * 5,
-        cost_estimate=cost(2 * rows * depth * hidden, *gates, *ups, *outs),
-        compiler_params=params(16),
+        out_specs=[INSIDE] * 7,
+        scratch_shapes=[pltpu.VMEM((hidden, rows), BF)],
+        cost_estimate=cost(0),
+        compiler_params=params(18),
     )(*gates, *ups, in_vmem(weight))
 
 
 def backward_kernel(
-    g0_ref, g1_ref, u0_ref, u1_ref, a0_ref, a1_ref, wg_ref, wu_ref, dg_ref, du_ref, *out_refs
+    a0_ref, a1_ref, silu_ref, slope_ref, wg_ref, wu_ref, dg_ref, du_ref, *refs
 ):
     hidden = dg_ref.shape[1]
     tile = math.gcd(hidden, TILE)
     for at in range(0, hidden, tile):
         cut = slice(at, at + tile)
-        gate_pre = g0_ref[:, cut].astype(F32) + g1_ref[:, cut].astype(F32)
-        up_pre = u0_ref[:, cut].astype(F32) + u1_ref[:, cut].astype(F32)
         act_grad = a0_ref[:, cut].astype(F32) + a1_ref[:, cut].astype(F32)
-        _, up_grad, gate_grad = pointwise(gate_pre, up_pre, act_grad)
-        dg_ref[:, cut] = gate_grad
-        du_ref[:, cut] = up_grad
-    spread(
-        contract_cols(dg_ref[...], wg_ref[...]) + contract_cols(du_ref[...], wu_ref[...]), out_refs
-    )
-
-
-def backward(gates, ups, acts, gate_weight, up_weight):
-    rows, (depth, hidden) = gates[0].shape[0], gate_weight.shape
-    outs = [
-        jax.ShapeDtypeStruct((rows, hidden), BF),
-        jax.ShapeDtypeStruct((rows, hidden), BF),
-    ] + [jax.ShapeDtypeStruct((rows // 4, depth), BF)] * 4
+        dg_ref[:, cut] = (act_grad * slope_ref[:, cut]).astype(BF)
+        du_ref[:, cut] = (act_grad * silu_ref[:, cut]).astype(BF)
+    times_rows([dg_ref, du_ref], [wg_ref, wu_ref], refs[4:], refs[:4])
+
+
+def backward(acts, silu_value, slope, gate_weight, up_weight):
+    rows, (depth, hidden) = acts[0].shape[0], gate_weight.shape
+    outs = [jax.ShapeDtypeStruct((rows, hidden), BF)] * 2
+    outs += [jax.ShapeDtypeStruct((rows // 4, depth), BF)] * 4
     return pl.pallas_call(
         backward_kernel,
         out_shape=outs,
-        in_specs=[INSIDE] * 8,
+        in_specs=[INSIDE] * 6,
         out_specs=[INSIDE] * 6,
-        cost_estimate=cost(4 * rows * depth * hidden, *gates, *ups, *acts, *outs),
+        scratch_shapes=[pltpu.VMEM((hidden, rows), BF)] * 2,
+        cost_estimate=cost(4 * rows * depth * hidden, *acts, silu_value, slope, *outs),
         compiler_params=params(20),
-    )(*gates, *ups, *acts, in_vmem(gate_weight), in_vmem(up_weight))
+    )(*acts, silu_value, slope, in_vmem(gate_weight), in_vmem(up_weight))
 
 
 def outer_kernel(x_ref, y_ref, out_ref, turned_ref, held_ref, sem):
@@ -446,40 +485,44 @@
     return lax.ppermute(rows, "dp", [(0, 1), (1, 0)])
 
 
-def turn(rows, shift):
+def turn(pieces):
     size = lax.axis_size("expert")
-    pairs = []
-    for s in range(2):
-        for i in range(size):
-            for d in range(2):
-                j = (i + 2 * shift) % size
-                pairs.append(((s * size + i) * 2 + d, (d * size + j) * 2 + s))
-    return lax.ppermute(rows, ("section", "expert", "dp"), pairs)
+    got = {}
+    for k in reversed(range(EXP)):
+        pairs = [
+            ((s * size + i) * 2 + d, (d * size + (i ^ (2 * k))) * 2 + s)
+            for s in range(2)
+            for i in range(size)
+            for d in range(2)
+        ]
+        got[k] = lax.ppermute(pieces[k], ("section", "expert", "dp"), pairs)
+    return [got[k] for k in range(EXP)]
 
 
 def paired(tokens, grad_out, expert_ids, gate_probs, gate_weight, up_weight, down_weight):
     payload = pack(tokens, grad_out, expert_ids, gate_probs, gate_weight.shape[0])
-    got = [turn(rows, k) for k, rows in enumerate(payload)]
+    got = turn(payload)
     gate_weight, up_weight = pin((gate_weight, up_weight), payload[0])
-    own_t, own_g = part(got)
+    own_t, own_g = part(got, gate_weight)
     (down_weight,) = pin((down_weight,), own_t)
-    slot_t, gate_part = gather_project([own_t] + swap_plane([own_t] * 3), gate_weight)
+    slot_t, gate_part = gather_project([own_t] + swap_plane([own_t] * 3), gate_weight, down_weight)
     gates = [gate_part, swap_dp(gate_part)]
     up_part = project(slot_t, up_weight)
     ups = [up_part, swap_dp(up_part)]
-    slot_g, act_part = gather_project([own_g] + swap_plane([own_g] * 3), down_weight)
+    activation, silu_value, slope, *part_out = forward(gates, ups, down_weight)
+    slot_g, act_part = gather_project(
+        [own_g] + swap_plane([own_g] * 3), down_weight, up_part
+    )
     acts = [act_part, swap_dp(act_part)]
-    activation, *part_out = forward(gates, ups, down_weight)
-    gate_grad, up_grad, *part_in = backward(gates, ups, acts, gate_weight, up_weight)
+    part_out, _ = lax.optimization_barrier((part_out, act_part))
+    gate_grad, up_grad, *part_in = backward(acts, silu_value, slope, gate_weight, up_weight)
     grad_down = outer(slot_g, activation)
     grad_gate = outer(slot_t, gate_grad)
     grad_up = outer(slot_t, up_grad)
     sent = join(
         part_out[:1] + swap_plane(part_out[1:]), part_in[:1] + swap_plane(part_in[1:])
     )
-    moe_out, grad_tokens = unpack(
-        [turn(rows, -k) for k, rows in enumerate(sent)], expert_ids, gate_probs
-    )
+    moe_out, grad_tokens = unpack(turn(sent), expert_ids, gate_probs)
     return moe_out, grad_tokens, grad_gate, grad_up, grad_down
 
 

time: 72 us -> 66.7 us (0.926)
  local copies, waits for them, and re-layouts: 3.15 us -> 0.01 us
  waiting for transfers between devices: 7.28 us -> 4.51 us
  Pallas kernels: 29.8 us -> 30.6 us
    ppermute x12, waiting for transfers between devices: 7.25 us -> 3.02 us  [the longest x4 2.69 us: swap_plane(): far = lax.ppermute(pieces[2], ('section', 'expert'), both)]
    unnamed x12 -> x4, local copies, waits for them, and re-layouts: 3.15 us -> 0.01 us
    ppermute x4, starting transfers between devices: 1.14 us -> 3.59 us  [swap_section(): return lax.ppermute(rows, 'section', [(0, 1), (1, 0)])]
    ppermute x4, starting transfers between devices: 4.92 us -> 2.55 us  [swap_expert(): return lax.ppermute(rows, 'expert', [(i, i ^ 1) for i in range(size)])]
    ppermute x12, starting transfers between devices: 23.2 us -> 21 us  [the longest x8 17.7 us: turn(): got[k] = lax.ppermute(pieces[k], ('section', 'expert', 'dp'), pairs)]
    ppermute x3, starting transfers between devices: 1.4 us -> 3.28 us  [swap_dp(): return lax.ppermute(rows, 'dp', [(0, 1), (1, 0)])]
    ppermute x4, waiting for transfers between devices: 0.01 us -> 1.48 us  [swap_section(): return lax.ppermute(rows, 'section', [(0, 1), (1, 0)])]
  transfers between devices with their start and end apart: 23 -> 23, of which waited for: 6 -> 5; matrix products, arithmetic and copies ran while one was open for 0% -> 0% of each run, Pallas kernels for 39% -> 42%
where the time goes in v3:
time: 66.7 us; the launch traced here: 66.5 us
  Pallas kernels  30.6 us (46%)
  starting transfers between devices  30.5 us (46%)
  waiting for transfers between devices  4.51 us (7%)
  between operations  0.88 us (1%)
    ppermute x8, starting transfers between devices, turn(): got[k] = lax.ppermute(pieces[k], ('section', 'expert', 'dp'), pairs)  17.7 us
    pallas_call x3, Pallas kernels, outer(): pl.pallas_call(outer_kernel, out_shape=out, in_specs=[INSIDE] * 2, out_sp...  9.65 us
    pallas_call x2, Pallas kernels, pin(): pl.pallas_call(pin_kernel, out_shape=[pltpu.VMEM(weight.shape, weight.dty...  7.42 us
    pallas_call x1, Pallas kernels, backward(): pl.pallas_call(backward_kernel, out_shape=outs, in_specs=[INSIDE] * 6, ou...  3.81 us
    ppermute x4, starting transfers between devices, swap_section(): return lax.ppermute(rows, 'section', [(0, 1), (1, 0)])  3.59 us
    ppermute x4, starting transfers between devices, swap_plane(): far = lax.ppermute(pieces[2], ('section', 'expert'), both)  3.28 us
    ppermute x3, starting transfers between devices, swap_dp(): return lax.ppermute(rows, 'dp', [(0, 1), (1, 0)])  3.28 us
    pallas_call x2, Pallas kernels, gather_project(): pl.pallas_call(gather_kernel, out_shape=outs, in_specs=[INSIDE] * (len(pi...  2.79 us
  transfers between devices with their start and end apart: 23, of which 5 were waited for; matrix products, arithmetic and copies ran while one was open for 0% of the time, Pallas kernels for 42%

profile of v3, /device:TPU:1, one launch (start us, length us, event | category | flops | bytes accessed | tf_op | source)
XLA Modules:
  0.0 66.5 jit_solution(14988351089694786277)
XLA Ops:
  0.6 1.3 %shard_map.110 = (bf16[24,1536]{1,0:T(8,128)(2,1)S(1)}, bf16[24,1536]{1,0:T(8,128)(2,1)S(1)}, bf16[24,1536]{1,0:T(8,128)(2,1)S(1)}, bf16[24,1536]{1,0:T(8,128)(2,1)S(1)}) custom-call(bf16[16,3072]{1,0:T(8,128)(2,1)} %refs_0_.3, bf16[16,3072]{1,0:T(8,128)(2,1)} %refs_1_.2, s32[2,16]{1,0:T(2,128)} %bitcast.2, f32[2,16]{1,0:T(2,128)} %bitcast.4), custom_call_target="tpu_custom_call" | custom-call | bytes 491520 | tf_op jit(solution)/shard_map/pallas_call | solution.py:243
  1.9 5.7 %collective-permute-start = (bf16[24,1536]{1,0:T(8,128)(2,1)S(1)}, bf16[24,1536]{1,0:T(8,128)(2,1)S(1)}, u32[]{:S(2)}, u32[]{:S(2)}) collective-permute-start(bf16[24,1536]{1,0:T(8,128)(2,1)S(1)} %get-tuple-element.40), channel_id=1, source_target_pairs={{0,12},{1,28},{2,14},{3,30},{4,8},{5,24},{6,10},{7,26},{8,4},{9,20... | collective-permute-start | bytes 221192 | tf_op jit(solution)/shard_map/ppermute | solution.py:498
  7.7 0.0 collective-permute-start.1
  7.7 1.4 %collective-permute-start.2 = (bf16[24,1536]{1,0:T(8,128)(2,1)S(1)}, bf16[24,1536]{1,0:T(8,128)(2,1)S(1)}, u32[]{:S(2)}, u32[]{:S(2)}) collective-permute-start(bf16[24,1536]{1,0:T(8,128)(2,1)S(1)} %get-tuple-element.42), channel_id=1, source_target_pairs={{0,4},{1,20},{2,6},{3,22},{4,0},{5,16},{6,2},{7,18},{8,12},{9,28},... | collective-permute-start | bytes 221192 | tf_op jit(solution)/shard_map/ppermute | solution.py:498
  9.1 2.3 %collective-permute-start.3 = (bf16[24,1536]{1,0:T(8,128)(2,1)S(1)}, bf16[24,1536]{1,0:T(8,128)(2,1)S(1)}, u32[]{:S(2)}, u32[]{:S(2)}) collective-permute-start(bf16[24,1536]{1,0:T(8,128)(2,1)S(1)} %get-tuple-element.43.refs_2_), channel_id=1, source_target_pairs={{0,0},{1,16},{2,2},{3,18},{4,4},{5,20},{6,6},{7,22},{8,8},{9,24},{... | collective-permute-start | bytes 221192 | tf_op jit(solution)/shard_map/ppermute | solution.py:498
  11.4 4.6 %shard_map.111 = (bf16[1536,2048]{1,0:T(8,128)(2,1)S(1)}, bf16[1536,2048]{1,0:T(8,128)(2,1)S(1)}) custom-call(bf16[1536,2048]{1,0:T(8,128)(2,1)} %refs_0_.4, bf16[1536,2048]{1,0:T(8,128)(2,1)} %refs_1_.3, bf16[24,1536]{1,0:T(8,128)(2,1)S(1)} %get-tuple-element.43.refs_2_), custom_call_target="tpu_custom_call" | custom-call | tf_op jit(solution)/shard_map/pallas_call | solution.py:150
  16.0 0.0 collective-permute-done.refs_0_
  16.0 0.0 collective-permute-done.1.refs_1_
  16.1 0.0 collective-permute-done.2.refs_2_
  16.1 0.0 collective-permute-done.3.refs_3_
  16.1 0.2 shard_map.112
  16.3 0.1 collective-permute-start.4
  16.4 1.3 %collective-permute-start.5 = (bf16[48,1536]{1,0:T(8,128)(2,1)S(1)}, bf16[48,1536]{1,0:T(8,128)(2,1)S(1)}, u32[]{:S(2)}, u32[]{:S(2)}) collective-permute-start(bf16[48,1536]{1,0:T(8,128)(2,1)S(1)} %get-tuple-element.45.refs_1_.refs_3_), channel_id=1, source_target_pairs={{0,2},{2,0},{4,6},{6,4},{8,10},{10,8},{12,14},{14,12},{1,3},{3,1},... | collective-permute-start | bytes 442376 | tf_op jit(solution)/shard_map/ppermute | solution.py:102
  17.7 1.4 %collective-permute-start.6 = (bf16[48,1536]{1,0:T(8,128)(2,1)S(1)}, bf16[48,1536]{1,0:T(8,128)(2,1)S(1)}, u32[]{:S(2)}, u32[]{:S(2)}) collective-permute-start(bf16[48,1536]{1,0:T(8,128)(2,1)S(1)} %get-tuple-element.45.refs_1_.refs_3_), channel_id=1, source_target_pairs={{0,16},{16,0},{1,17},{17,1},{2,18},{18,2},{3,19},{19,3},{4,20},{20... | collective-permute-start | bytes 442376 | tf_op jit(solution)/shard_map/ppermute | solution.py:106
  19.0 0.9 %collective-permute-start.9 = (bf16[48,1536]{1,0:T(8,128)(2,1)S(1)}, bf16[48,1536]{1,0:T(8,128)(2,1)S(1)}, u32[]{:S(2)}, u32[]{:S(2)}) collective-permute-start(bf16[48,1536]{1,0:T(8,128)(2,1)S(1)} %get-tuple-element.53.refs_3_), channel_id=1, source_target_pairs={{0,18},{2,16},{4,22},{6,20},{8,26},{10,24},{12,30},{14,28},{16,2},... | collective-permute-start | bytes 442376 | tf_op jit(solution)/shard_map/ppermute | solution.py:112
  19.9 0.4 collective-permute-start.10
  20.3 2.7 %collective-permute-done.4.refs_0_ = bf16[48,1536]{1,0:T(8,128)(2,1)S(1)} collective-permute-done((bf16[48,1536]{1,0:T(8,128)(2,1)S(1)}, bf16[48,1536]{1,0:T(8,128)(2,1)S(1)}, u32[]{:S(2)}, u32[]{:S(2)}) %collective-permute-start.4) | collective-permute-done | bytes 147488 | tf_op jit(solution)/shard_map/ppermute | solution.py:112
  23.0 0.0 collective-permute-start.11
  23.0 2.8 %shard_map.113.refs_5_.w_ref.refs_4_ = bf16[1536,2048]{1,0:T(8,128)(2,1)S(1)} custom-call(bf16[1536,2048]{1,0:T(8,128)(2,1)} %refs_0_.5, bf16[48,1536]{1,0:T(8,128)(2,1)S(1)} %get-tuple-element.45.refs_1_.refs_3_), custom_call_target="tpu_custom_call" | custom-call | tf_op jit(solution)/shard_map/pallas_call | solution.py:150
  25.8 0.0 collective-permute-done.5.refs_1_
  25.8 0.4 collective-permute-done.6.refs_2_
  26.2 1.4 %shard_map.114 = (bf16[192,1536]{1,0:T(8,128)(2,1)S(1)}, bf16[192,2048]{1,0:T(8,128)(2,1)S(1)}) custom-call(bf16[48,1536]{1,0:T(8,128)(2,1)S(1)} %collective-permute-done.4.refs_0_, bf16[48,1536]{1,0:T(8,128)(2,1)S(1)} %collective-permute-done.5.refs_1_, bf16[48,1536]{1,0:T(8,128)(2,1)S(1)} %collective-permute-done.6.refs_2_, ...), custom_call_target="tpu_custom_call" | custom-call | tf_op jit(solution)/shard_map/pallas_call | solution.py:172
  27.6 2.5 %collective-permute-start.7 = (bf16[192,2048]{1,0:T(8,128)(2,1)S(1)}, bf16[192,2048]{1,0:T(8,128)(2,1)S(1)}, u32[]{:S(2)}, u32[]{:S(2)}) collective-permute-start(bf16[192,2048]{1,0:T(8,128)(2,1)S(1)} %get-tuple-element.46.g0_ref), channel_id=1, source_target_pairs={{0,1},{1,0},{2,3},{3,2},{4,5},{5,4},{6,7},{7,6},{8,9},{9,8},{10,11... | collective-permute-start | bytes 2359304 | tf_op jit(solution)/shard_map/ppermute | solution.py:485
  30.2 1.4 %shard_map.115.u0_ref.refs_5_ = bf16[192,2048]{1,0:T(8,128)(2,1)S(1)} custom-call(bf16[192,1536]{1,0:T(8,128)(2,1)S(1)} %get-tuple-element.47.x_ref, bf16[1536,2048]{1,0:T(8,128)(2,1)S(1)} %get-tuple-element.48.w_ref.wu_ref), custom_call_target="tpu_custom_call" | custom-call | tf_op jit(solution)/shard_map/pallas_call | solution.py:189
  31.6 0.1 collective-permute-start.8
  31.7 0.0 collective-permute-done.9.refs_0_
  31.7 0.0 collective-permute-done.10.refs_1_
  31.7 0.7 %collective-permute-done.11.refs_2_ = bf16[48,1536]{1,0:T(8,128)(2,1)S(1)} collective-permute-done((bf16[48,1536]{1,0:T(8,128)(2,1)S(1)}, bf16[48,1536]{1,0:T(8,128)(2,1)S(1)}, u32[]{:S(2)}, u32[]{:S(2)}) %collective-permute-start.11) | collective-permute-done | bytes 147488 | tf_op jit(solution)/shard_map/ppermute | solution.py:106
  32.4 1.4 %shard_map.117 = (bf16[192,1536]{1,0:T(8,128)(2,1)S(1)}, bf16[192,2048]{1,0:T(8,128)(2,1)S(1)}) custom-call(bf16[48,1536]{1,0:T(8,128)(2,1)S(1)} %collective-permute-done.9.refs_0_, bf16[48,1536]{1,0:T(8,128)(2,1)S(1)} %collective-permute-done.10.refs_1_, bf16[48,1536]{1,0:T(8,128)(2,1)S(1)} %collective-permute-done.11.refs_2_, ...), custom_call_target="tpu_custom_call" | custom-call | tf_op jit(solution)/shard_map/pallas_call | solution.py:172
  33.8 0.7 %collective-permute-start.15 = (bf16[192,2048]{1,0:T(8,128)(2,1)S(1)}, bf16[192,2048]{1,0:T(8,128)(2,1)S(1)}, u32[]{:S(2)}, u32[]{:S(2)}) collective-permute-start(bf16[192,2048]{1,0:T(8,128)(2,1)S(1)} %get-tuple-element.54.a0_ref), channel_id=1, source_target_pairs={{0,1},{1,0},{2,3},{3,2},{4,5},{5,4},{6,7},{7,6},{8,9},{9,8},{10,11... | collective-permute-start | bytes 2359304 | tf_op jit(solution)/shard_map/ppermute | solution.py:485
  34.5 0.0 collective-permute-done.7.g1_ref
  34.5 0.0 collective-permute-done.8.u1_ref
  34.5 2.7 %shard_map.116 = (bf16[192,2048]{1,0:T(8,128)(2,1)S(1)}, f32[192,2048]{1,0:T(8,128)S(1)}, f32[192,2048]{1,0:T(8,128)S(1)}, bf16[48,1536]{1,0:T(8,128)(2,1)S(1)},...) custom-call(bf16[192,2048]{1,0:T(8,128)(2,1)S(1)} %get-tuple-element.46.g0_ref, ...), custom_call_target="tpu_custom_call" | custom-call | tf_op jit(solution)/shard_map/pallas_call | solution.py:411
  37.2 1.1 %collective-permute-start.12 = (bf16[48,1536]{1,0:T(8,128)(2,1)S(1)}, bf16[48,1536]{1,0:T(8,128)(2,1)S(1)}, u32[]{:S(2)}, u32[]{:S(2)}) collective-permute-start(bf16[48,1536]{1,0:T(8,128)(2,1)S(1)} %get-tuple-element.55), channel_id=1, source_target_pairs={{0,18},{2,16},{4,22},{6,20},{8,26},{10,24},{12,30},{14,28},{16,2},... | collective-permute-start | bytes 442376 | tf_op jit(solution)/shard_map/ppermute | solution.py:112
  38.3 0.5 collective-permute-start.13
  38.8 1.1 %collective-permute-start.14 = (bf16[48,1536]{1,0:T(8,128)(2,1)S(1)}, bf16[48,1536]{1,0:T(8,128)(2,1)S(1)}, u32[]{:S(2)}, u32[]{:S(2)}) collective-permute-start(bf16[48,1536]{1,0:T(8,128)(2,1)S(1)} %get-tuple-element.57), channel_id=1, source_target_pairs={{0,16},{16,0},{1,17},{17,1},{2,18},{18,2},{3,19},{19,3},{4,20},{20... | collective-permute-start | bytes 442376 | tf_op jit(solution)/shard_map/ppermute | solution.py:106
  39.9 0.0 collective-permute-done.15.a1_ref
  39.9 3.8 %shard_map.118 = (bf16[192,2048]{1,0:T(8,128)(2,1)S(1)}, bf16[192,2048]{1,0:T(8,128)(2,1)S(1)}, bf16[48,1536]{1,0:T(8,128)(2,1)S(1)}, bf16[48,1536]{1,0:T(8,128)...) custom-call(bf16[192,2048]{1,0:T(8,128)(2,1)S(1)} %get-tuple-element.54.a0_ref, ...), custom_call_target="tpu_custom_call" | custom-call | flops 2415919104 | bytes 6881280 | tf_op jit(solution)/shard_map/pallas_call | solution.py:439
  43.7 1.1 %collective-permute-start.16 = (bf16[48,1536]{1,0:T(8,128)(2,1)S(1)}, bf16[48,1536]{1,0:T(8,128)(2,1)S(1)}, u32[]{:S(2)}, u32[]{:S(2)}) collective-permute-start(bf16[48,1536]{1,0:T(8,128)(2,1)S(1)} %get-tuple-element.61), channel_id=1, source_target_pairs={{0,18},{2,16},{4,22},{6,20},{8,26},{10,24},{12,30},{14,28},{16,2},... | collective-permute-start | bytes 442376 | tf_op jit(solution)/shard_map/ppermute | solution.py:112
  44.8 0.5 collective-permute-start.17
  45.3 0.0 collective-permute-done.12.refs_0_
  45.3 1.1 %collective-permute-start.18 = (bf16[48,1536]{1,0:T(8,128)(2,1)S(1)}, bf16[48,1536]{1,0:T(8,128)(2,1)S(1)}, u32[]{:S(2)}, u32[]{:S(2)}) collective-permute-start(bf16[48,1536]{1,0:T(8,128)(2,1)S(1)} %get-tuple-element.63), channel_id=1, source_target_pairs={{0,16},{16,0},{1,17},{17,1},{2,18},{18,2},{3,19},{19,3},{4,20},{20... | collective-permute-start | bytes 442376 | tf_op jit(solution)/shard_map/ppermute | solution.py:106
  46.4 3.2 %shard_map.121 = bf16[1536,2048]{1,0:T(8,128)(2,1)} custom-call(bf16[192,1536]{1,0:T(8,128)(2,1)S(1)} %get-tuple-element.47.x_ref, bf16[192,2048]{1,0:T(8,128)(2,1)S(1)} %get-tuple-element.71.y_ref), custom_call_target="tpu_custom_call" | custom-call | flops 1207959552 | bytes 7667712 | tf_op jit(solution)/shard_map/pallas_call | solution.py:469
  49.6 3.3 %shard_map.122 = bf16[1536,2048]{1,0:T(8,128)(2,1)} custom-call(bf16[192,1536]{1,0:T(8,128)(2,1)S(1)} %get-tuple-element.47.x_ref, bf16[192,2048]{1,0:T(8,128)(2,1)S(1)} %get-tuple-element.72.y_ref), custom_call_target="tpu_custom_call" | custom-call | flops 1207959552 | bytes 7667712 | tf_op jit(solution)/shard_map/pallas_call | solution.py:469
  52.9 0.0 copy-start
  52.9 0.0 copy-start.1
  52.9 0.0 collective-permute-done.13.refs_1_
  52.9 0.0 collective-permute-done.14.refs_2_
  52.9 0.0 collective-permute-done.16.refs_4_
  52.9 0.0 collective-permute-done.17.refs_5_
  52.9 0.3 collective-permute-done.18.refs_6_
  53.2 0.3 shard_map.119
  53.6 4.6 %collective-permute-start.19 = (bf16[24,1536]{1,0:T(8,128)(2,1)S(1)}, bf16[24,1536]{1,0:T(8,128)(2,1)S(1)}, u32[]{:S(2)}, u32[]{:S(2)}) collective-permute-start(bf16[24,1536]{1,0:T(8,128)(2,1)S(1)} %get-tuple-element.65), channel_id=1, source_target_pairs={{0,12},{1,28},{2,14},{3,30},{4,8},{5,24},{6,10},{7,26},{8,4},{9,20... | collective-permute-start | bytes 221192 | tf_op jit(solution)/shard_map/ppermute | solution.py:498
  58.1 0.0 collective-permute-start.20
  58.1 1.6 %collective-permute-start.21 = (bf16[24,1536]{1,0:T(8,128)(2,1)S(1)}, bf16[24,1536]{1,0:T(8,128)(2,1)S(1)}, u32[]{:S(2)}, u32[]{:S(2)}) collective-permute-start(bf16[24,1536]{1,0:T(8,128)(2,1)S(1)} %get-tuple-element.67), channel_id=1, source_target_pairs={{0,4},{1,20},{2,6},{3,22},{4,0},{5,16},{6,2},{7,18},{8,12},{9,28},... | collective-permute-start | bytes 221192 | tf_op jit(solution)/shard_map/ppermute | solution.py:498
  59.8 2.1 %collective-permute-start.22 = (bf16[24,1536]{1,0:T(8,128)(2,1)S(1)}, bf16[24,1536]{1,0:T(8,128)(2,1)S(1)}, u32[]{:S(2)}, u32[]{:S(2)}) collective-permute-start(bf16[24,1536]{1,0:T(8,128)(2,1)S(1)} %get-tuple-element.68), channel_id=1, source_target_pairs={{0,0},{1,16},{2,2},{3,18},{4,4},{5,20},{6,6},{7,22},{8,8},{9,24},{... | collective-permute-start | bytes 221192 | tf_op jit(solution)/shard_map/ppermute | solution.py:498
  61.9 3.2 %shard_map.123 = bf16[1536,2048]{1,0:T(8,128)(2,1)} custom-call(bf16[192,1536]{1,0:T(8,128)(2,1)S(1)} %get-tuple-element.73.x_ref, bf16[192,2048]{1,0:T(8,128)(2,1)S(1)} %get-tuple-element.74.y_ref), custom_call_target="tpu_custom_call" | custom-call | flops 1207959552 | bytes 7667712 | tf_op jit(solution)/shard_map/pallas_call | solution.py:469
  65.1 0.0 collective-permute-done.19.refs_0_
  65.1 0.0 collective-permute-done.20.refs_1_
  65.1 0.0 collective-permute-done.21.refs_2_
  65.1 0.3 collective-permute-done.22.refs_3_
  65.4 0.0 copy-done
  65.4 0.0 copy-done.1
  65.4 1.0 %shard_map.120 = (bf16[16,1536]{1,0:T(8,128)(2,1)}, bf16[16,1536]{1,0:T(8,128)(2,1)}) custom-call(bf16[24,1536]{1,0:T(8,128)(2,1)S(1)} %collective-permute-done.19.refs_0_, bf16[24,1536]{1,0:T(8,128)(2,1)S(1)} %collective-permute-done.20.refs_1_, bf16[24,1536]{1,0:T(8,128)(2,1)S(1)} %collective-permute-done.21.refs_2_, ...), custom_call_target="tpu_custom_call" | custom-call | bytes 393216 | tf_op jit(solution)/shard_map/pallas_call | solution.py:349
Async XLA Ops:
  1.9 14.1 %collective-permute-start = (bf16[24,1536]{1,0:T(8,128)(2,1)S(1)}, bf16[24,1536]{1,0:T(8,128)(2,1)S(1)}, u32[]{:S(2)}, u32[]{:S(2)}) collective-permute-start(bf16[24,1536]{1,0:T(8,128)(2,1)S(1)} %get-tuple-element.40), channel_id=1, source_target_pairs={{0,12},{1,28},{2,14},{3,30},{4,8},{5,24},{6,10},{7,26},{8,4},{9,20... | collective-permute-start | bytes 221192 | tf_op jit(solution)/shard_map/ppermute | solution.py:498
  7.7 8.4 %collective-permute-start.1 = (bf16[24,1536]{1,0:T(8,128)(2,1)S(1)}, bf16[24,1536]{1,0:T(8,128)(2,1)S(1)}, u32[]{:S(2)}, u32[]{:S(2)}) collective-permute-start(bf16[24,1536]{1,0:T(8,128)(2,1)S(1)} %get-tuple-element.41), channel_id=1, source_target_pairs={{0,8},{1,24},{2,10},{3,26},{4,12},{5,28},{6,14},{7,30},{8,0},{9,16... | collective-permute-start | bytes 221192 | tf_op jit(solution)/shard_map/ppermute | solution.py:498
  7.7 8.4 %collective-permute-start.2 = (bf16[24,1536]{1,0:T(8,128)(2,1)S(1)}, bf16[24,1536]{1,0:T(8,128)(2,1)S(1)}, u32[]{:S(2)}, u32[]{:S(2)}) collective-permute-start(bf16[24,1536]{1,0:T(8,128)(2,1)S(1)} %get-tuple-element.42), channel_id=1, source_target_pairs={{0,4},{1,20},{2,6},{3,22},{4,0},{5,16},{6,2},{7,18},{8,12},{9,28},... | collective-permute-start | bytes 221192 | tf_op jit(solution)/shard_map/ppermute | solution.py:498
  9.1 7.0 %collective-permute-start.3 = (bf16[24,1536]{1,0:T(8,128)(2,1)S(1)}, bf16[24,1536]{1,0:T(8,128)(2,1)S(1)}, u32[]{:S(2)}, u32[]{:S(2)}) collective-permute-start(bf16[24,1536]{1,0:T(8,128)(2,1)S(1)} %get-tuple-element.43.refs_2_), channel_id=1, source_target_pairs={{0,0},{1,16},{2,2},{3,18},{4,4},{5,20},{6,6},{7,22},{8,8},{9,24},{... | collective-permute-start | bytes 221192 | tf_op jit(solution)/shard_map/ppermute | solution.py:498
  16.3 6.7 %collective-permute-start.4 = (bf16[48,1536]{1,0:T(8,128)(2,1)S(1)}, bf16[48,1536]{1,0:T(8,128)(2,1)S(1)}, u32[]{:S(2)}, u32[]{:S(2)}) collective-permute-start(bf16[48,1536]{1,0:T(8,128)(2,1)S(1)} %get-tuple-element.45.refs_1_.refs_3_), channel_id=1, source_target_pairs={{0,18},{2,16},{4,22},{6,20},{8,26},{10,24},{12,30},{14,28},{16,2},... | collective-permute-start | bytes 442376 | tf_op jit(solution)/shard_map/ppermute | solution.py:112
  16.4 9.4 %collective-permute-start.5 = (bf16[48,1536]{1,0:T(8,128)(2,1)S(1)}, bf16[48,1536]{1,0:T(8,128)(2,1)S(1)}, u32[]{:S(2)}, u32[]{:S(2)}) collective-permute-start(bf16[48,1536]{1,0:T(8,128)(2,1)S(1)} %get-tuple-element.45.refs_1_.refs_3_), channel_id=1, source_target_pairs={{0,2},{2,0},{4,6},{6,4},{8,10},{10,8},{12,14},{14,12},{1,3},{3,1},... | collective-permute-start | bytes 442376 | tf_op jit(solution)/shard_map/ppermute | solution.py:102
  17.7 8.6 %collective-permute-start.6 = (bf16[48,1536]{1,0:T(8,128)(2,1)S(1)}, bf16[48,1536]{1,0:T(8,128)(2,1)S(1)}, u32[]{:S(2)}, u32[]{:S(2)}) collective-permute-start(bf16[48,1536]{1,0:T(8,128)(2,1)S(1)} %get-tuple-element.45.refs_1_.refs_3_), channel_id=1, source_target_pairs={{0,16},{16,0},{1,17},{17,1},{2,18},{18,2},{3,19},{19,3},{4,20},{20... | collective-permute-start | bytes 442376 | tf_op jit(solution)/shard_map/ppermute | solution.py:106
  19.0 12.6 %collective-permute-start.9 = (bf16[48,1536]{1,0:T(8,128)(2,1)S(1)}, bf16[48,1536]{1,0:T(8,128)(2,1)S(1)}, u32[]{:S(2)}, u32[]{:S(2)}) collective-permute-start(bf16[48,1536]{1,0:T(8,128)(2,1)S(1)} %get-tuple-element.53.refs_3_), channel_id=1, source_target_pairs={{0,18},{2,16},{4,22},{6,20},{8,26},{10,24},{12,30},{14,28},{16,2},... | collective-permute-start | bytes 442376 | tf_op jit(solution)/shard_map/ppermute | solution.py:112
  19.9 11.7 %collective-permute-start.10 = (bf16[48,1536]{1,0:T(8,128)(2,1)S(1)}, bf16[48,1536]{1,0:T(8,128)(2,1)S(1)}, u32[]{:S(2)}, u32[]{:S(2)}) collective-permute-start(bf16[48,1536]{1,0:T(8,128)(2,1)S(1)} %get-tuple-element.53.refs_3_), channel_id=1, source_target_pairs={{0,2},{2,0},{4,6},{6,4},{8,10},{10,8},{12,14},{14,12},{1,3},{3,1},... | collective-permute-start | bytes 442376 | tf_op jit(solution)/shard_map/ppermute | solution.py:102
  23.0 9.4 %collective-permute-start.11 = (bf16[48,1536]{1,0:T(8,128)(2,1)S(1)}, bf16[48,1536]{1,0:T(8,128)(2,1)S(1)}, u32[]{:S(2)}, u32[]{:S(2)}) collective-permute-start(bf16[48,1536]{1,0:T(8,128)(2,1)S(1)} %get-tuple-element.53.refs_3_), channel_id=1, source_target_pairs={{0,16},{16,0},{1,17},{17,1},{2,18},{18,2},{3,19},{19,3},{4,20},{20... | collective-permute-start | bytes 442376 | tf_op jit(solution)/shard_map/ppermute | solution.py:106
  27.6 6.8 %collective-permute-start.7 = (bf16[192,2048]{1,0:T(8,128)(2,1)S(1)}, bf16[192,2048]{1,0:T(8,128)(2,1)S(1)}, u32[]{:S(2)}, u32[]{:S(2)}) collective-permute-start(bf16[192,2048]{1,0:T(8,128)(2,1)S(1)} %get-tuple-element.46.g0_ref), channel_id=1, source_target_pairs={{0,1},{1,0},{2,3},{3,2},{4,5},{5,4},{6,7},{7,6},{8,9},{9,8},{10,11... | collective-permute-start | bytes 2359304 | tf_op jit(solution)/shard_map/ppermute | solution.py:485
  31.6 2.9 %collective-permute-start.8 = (bf16[192,2048]{1,0:T(8,128)(2,1)S(1)}, bf16[192,2048]{1,0:T(8,128)(2,1)S(1)}, u32[]{:S(2)}, u32[]{:S(2)}) collective-permute-start(bf16[192,2048]{1,0:T(8,128)(2,1)S(1)} %shard_map.115.u0_ref.refs_5_), channel_id=1, source_target_pairs={{0,1},{1,0},{2,3},{3,2},{4,5},{5,4},{6,7},{7,6},{8,9},{9,8},{10,11... | collective-permute-start | bytes 2359304 | tf_op jit(solution)/shard_map/ppermute | solution.py:485
  33.8 6.1 %collective-permute-start.15 = (bf16[192,2048]{1,0:T(8,128)(2,1)S(1)}, bf16[192,2048]{1,0:T(8,128)(2,1)S(1)}, u32[]{:S(2)}, u32[]{:S(2)}) collective-permute-start(bf16[192,2048]{1,0:T(8,128)(2,1)S(1)} %get-tuple-element.54.a0_ref), channel_id=1, source_target_pairs={{0,1},{1,0},{2,3},{3,2},{4,5},{5,4},{6,7},{7,6},{8,9},{9,8},{10,11... | collective-permute-start | bytes 2359304 | tf_op jit(solution)/shard_map/ppermute | solution.py:485
  37.2 8.1 %collective-permute-start.12 = (bf16[48,1536]{1,0:T(8,128)(2,1)S(1)}, bf16[48,1536]{1,0:T(8,128)(2,1)S(1)}, u32[]{:S(2)}, u32[]{:S(2)}) collective-permute-start(bf16[48,1536]{1,0:T(8,128)(2,1)S(1)} %get-tuple-element.55), channel_id=1, source_target_pairs={{0,18},{2,16},{4,22},{6,20},{8,26},{10,24},{12,30},{14,28},{16,2},... | collective-permute-start | bytes 442376 | tf_op jit(solution)/shard_map/ppermute | solution.py:112
  38.3 14.6 %collective-permute-start.13 = (bf16[48,1536]{1,0:T(8,128)(2,1)S(1)}, bf16[48,1536]{1,0:T(8,128)(2,1)S(1)}, u32[]{:S(2)}, u32[]{:S(2)}) collective-permute-start(bf16[48,1536]{1,0:T(8,128)(2,1)S(1)} %get-tuple-element.56), channel_id=1, source_target_pairs={{0,2},{2,0},{4,6},{6,4},{8,10},{10,8},{12,14},{14,12},{1,3},{3,1},... | collective-permute-start | bytes 442376 | tf_op jit(solution)/shard_map/ppermute | solution.py:102
  38.8 14.2 %collective-permute-start.14 = (bf16[48,1536]{1,0:T(8,128)(2,1)S(1)}, bf16[48,1536]{1,0:T(8,128)(2,1)S(1)}, u32[]{:S(2)}, u32[]{:S(2)}) collective-permute-start(bf16[48,1536]{1,0:T(8,128)(2,1)S(1)} %get-tuple-element.57), channel_id=1, source_target_pairs={{0,16},{16,0},{1,17},{17,1},{2,18},{18,2},{3,19},{19,3},{4,20},{20... | collective-permute-start | bytes 442376 | tf_op jit(solution)/shard_map/ppermute | solution.py:106
  43.7 9.2 %collective-permute-start.16 = (bf16[48,1536]{1,0:T(8,128)(2,1)S(1)}, bf16[48,1536]{1,0:T(8,128)(2,1)S(1)}, u32[]{:S(2)}, u32[]{:S(2)}) collective-permute-start(bf16[48,1536]{1,0:T(8,128)(2,1)S(1)} %get-tuple-element.61), channel_id=1, source_target_pairs={{0,18},{2,16},{4,22},{6,20},{8,26},{10,24},{12,30},{14,28},{16,2},... | collective-permute-start | bytes 442376 | tf_op jit(solution)/shard_map/ppermute | solution.py:112
  44.8 8.1 %collective-permute-start.17 = (bf16[48,1536]{1,0:T(8,128)(2,1)S(1)}, bf16[48,1536]{1,0:T(8,128)(2,1)S(1)}, u32[]{:S(2)}, u32[]{:S(2)}) collective-permute-start(bf16[48,1536]{1,0:T(8,128)(2,1)S(1)} %get-tuple-element.62), channel_id=1, source_target_pairs={{0,2},{2,0},{4,6},{6,4},{8,10},{10,8},{12,14},{14,12},{1,3},{3,1},... | collective-permute-start | bytes 442376 | tf_op jit(solution)/shard_map/ppermute | solution.py:102
  45.3 7.9 %collective-permute-start.18 = (bf16[48,1536]{1,0:T(8,128)(2,1)S(1)}, bf16[48,1536]{1,0:T(8,128)(2,1)S(1)}, u32[]{:S(2)}, u32[]{:S(2)}) collective-permute-start(bf16[48,1536]{1,0:T(8,128)(2,1)S(1)} %get-tuple-element.63), channel_id=1, source_target_pairs={{0,16},{16,0},{1,17},{17,1},{2,18},{18,2},{3,19},{19,3},{4,20},{20... | collective-permute-start | bytes 442376 | tf_op jit(solution)/shard_map/ppermute | solution.py:106
  52.9 12.5 %copy-start = (s32[16,2]{0,1:T(2,128)S(1)}, s32[16,2]{0,1:T(2,128)}, u32[]{:S(2)}) copy-start(s32[16,2]{0,1:T(2,128)} %param.9) | copy-start | bytes 388
  52.9 12.5 %copy-start.1 = (f32[16,2]{0,1:T(2,128)S(1)}, f32[16,2]{0,1:T(2,128)}, u32[]{:S(2)}) copy-start(f32[16,2]{0,1:T(2,128)} %param.10) | copy-start | bytes 388
  53.6 11.5 %collective-permute-start.19 = (bf16[24,1536]{1,0:T(8,128)(2,1)S(1)}, bf16[24,1536]{1,0:T(8,128)(2,1)S(1)}, u32[]{:S(2)}, u32[]{:S(2)}) collective-permute-start(bf16[24,1536]{1,0:T(8,128)(2,1)S(1)} %get-tuple-element.65), channel_id=1, source_target_pairs={{0,12},{1,28},{2,14},{3,30},{4,8},{5,24},{6,10},{7,26},{8,4},{9,20... | collective-permute-start | bytes 221192 | tf_op jit(solution)/shard_map/ppermute | solution.py:498
  58.1 6.9 %collective-permute-start.20 = (bf16[24,1536]{1,0:T(8,128)(2,1)S(1)}, bf16[24,1536]{1,0:T(8,128)(2,1)S(1)}, u32[]{:S(2)}, u32[]{:S(2)}) collective-permute-start(bf16[24,1536]{1,0:T(8,128)(2,1)S(1)} %get-tuple-element.66), channel_id=1, source_target_pairs={{0,8},{1,24},{2,10},{3,26},{4,12},{5,28},{6,14},{7,30},{8,0},{9,16... | collective-permute-start | bytes 221192 | tf_op jit(solution)/shard_map/ppermute | solution.py:498
  58.1 6.9 %collective-permute-start.21 = (bf16[24,1536]{1,0:T(8,128)(2,1)S(1)}, bf16[24,1536]{1,0:T(8,128)(2,1)S(1)}, u32[]{:S(2)}, u32[]{:S(2)}) collective-permute-start(bf16[24,1536]{1,0:T(8,128)(2,1)S(1)} %get-tuple-element.67), channel_id=1, source_target_pairs={{0,4},{1,20},{2,6},{3,22},{4,0},{5,16},{6,2},{7,18},{8,12},{9,28},... | collective-permute-start | bytes 221192 | tf_op jit(solution)/shard_map/ppermute | solution.py:498
  59.8 5.7 %collective-permute-start.22 = (bf16[24,1536]{1,0:T(8,128)(2,1)S(1)}, bf16[24,1536]{1,0:T(8,128)(2,1)S(1)}, u32[]{:S(2)}, u32[]{:S(2)}) collective-permute-start(bf16[24,1536]{1,0:T(8,128)(2,1)S(1)} %get-tuple-element.68), channel_id=1, source_target_pairs={{0,0},{1,16},{2,2},{3,18},{4,4},{5,20},{6,6},{7,22},{8,8},{9,24},{... | collective-permute-start | bytes 221192 | tf_op jit(solution)/shard_map/ppermute | solution.py:498

commit v4 on v3

--- a/solution.py
+++ b/solution.py
@@ -11,7 +11,7 @@
 CAP = 12
 BF = jnp.bfloat16
 F32 = jnp.float32
-TILE = 512
+TILE = 256
 
 
 def contract_rows(left, right):
@@ -447,38 +447,44 @@
     )(*acts, silu_value, slope, in_vmem(gate_weight), in_vmem(up_weight))
 
 
-def outer_kernel(x_ref, y_ref, out_ref, turned_ref, held_ref, sem):
-    depth = held_ref.shape[0]
+def outer_kernel(*refs):
+    count = (len(refs) - 4) // 2
+    x_ref, y_refs, out_refs = refs[0], refs[1 : 1 + count], refs[1 + count : 1 + 2 * count]
+    turned_ref, held_ref, sem = refs[-3:]
+    depth = held_ref.shape[1]
     tile = math.gcd(depth, 256)
     turned_ref[...] = x_ref[...].T
     copies = []
-    for i, at in enumerate(range(0, depth, tile)):
-        cut = slice(at, at + tile)
-        held_ref[cut] = jnp.dot(
-            turned_ref[cut], y_ref[...], preferred_element_type=F32
-        ).astype(BF)
-        copies.append(pltpu.make_async_copy(held_ref.at[cut], out_ref.at[cut], sem.at[i]))
-        copies[-1].start()
+    for j in range(count):
+        for i, at in enumerate(range(0, depth, tile)):
+            cut = slice(at, at + tile)
+            held_ref[j, cut] = jnp.dot(
+                turned_ref[cut], y_refs[j][...], preferred_element_type=F32
+            ).astype(BF)
+            copies.append(
+                pltpu.make_async_copy(held_ref.at[j, cut], out_refs[j].at[cut], sem.at[j, i])
+            )
+            copies[-1].start()
     for copy in copies:
         copy.wait()
 
 
-def outer(x, y):
-    (rows, depth), hidden = x.shape, y.shape[1]
-    out = jax.ShapeDtypeStruct((depth, hidden), BF)
+def outer(x, *ys):
+    (rows, depth), hidden, count = x.shape, ys[0].shape[1], len(ys)
+    outs = [jax.ShapeDtypeStruct((depth, hidden), BF)] * count
     return pl.pallas_call(
         outer_kernel,
-        out_shape=out,
-        in_specs=[INSIDE] * 2,
-        out_specs=ANYWHERE,
+        out_shape=outs,
+        in_specs=[INSIDE] * (1 + count),
+        out_specs=[ANYWHERE] * count,
         scratch_shapes=[
             pltpu.VMEM((depth, rows), BF),
-            pltpu.VMEM((depth, hidden), BF),
-            pltpu.SemaphoreType.DMA((depth // math.gcd(depth, 256),)),
+            pltpu.VMEM((count, depth, hidden), BF),
+            pltpu.SemaphoreType.DMA((count, depth // math.gcd(depth, 256))),
         ],
-        cost_estimate=cost(2 * rows * depth * hidden, x, y, out),
-        compiler_params=params(24),
-    )(x, y)
+        cost_estimate=cost(2 * rows * depth * hidden * count, x, *ys, *outs),
+        compiler_params=params(20 + 8 * count),
+    )(x, *ys)
 
 
 def swap_dp(rows):
@@ -502,10 +508,10 @@
 def paired(tokens, grad_out, expert_ids, gate_probs, gate_weight, up_weight, down_weight):
     payload = pack(tokens, grad_out, expert_ids, gate_probs, gate_weight.shape[0])
     got = turn(payload)
-    gate_weight, up_weight = pin((gate_weight, up_weight), payload[0])
+    (gate_weight,) = pin((gate_weight,), payload[0])
     own_t, own_g = part(got, gate_weight)
-    (down_weight,) = pin((down_weight,), own_t)
-    slot_t, gate_part = gather_project([own_t] + swap_plane([own_t] * 3), gate_weight, down_weight)
+
+    slot_t, gate_part = gather_project([own_t] + swap_plane([own_t] * 3), gate_weight, own_t)
     gates = [gate_part, swap_dp(gate_part)]
     up_part = project(slot_t, up_weight)
     ups = [up_part, swap_dp(up_part)]
@@ -516,9 +522,8 @@
     acts = [act_part, swap_dp(act_part)]
     part_out, _ = lax.optimization_barrier((part_out, act_part))
     gate_grad, up_grad, *part_in = backward(acts, silu_value, slope, gate_weight, up_weight)
-    grad_down = outer(slot_g, activation)
-    grad_gate = outer(slot_t, gate_grad)
-    grad_up = outer(slot_t, up_grad)
+    (grad_down,) = outer(slot_g, activation)
+    grad_gate, grad_up = outer(slot_t, gate_grad, up_grad)
     sent = join(
         part_out[:1] + swap_plane(part_out[1:]), part_in[:1] + swap_plane(part_in[1:])
     )

time: 66.7 us -> 64.6 us (0.969)
  Pallas kernels: 30.6 us -> 24.6 us
  waiting for transfers between devices: 4.51 us -> 9.92 us
  starting transfers between devices: 30.5 us -> 29 us
    ppermute x4, waiting for transfers between devices: 1.48 us -> 6.45 us  [swap_section(): return lax.ppermute(rows, 'section', [(0, 1), (1, 0)])]
    pallas_call x2 -> x1, Pallas kernels: 7.42 us -> 2.95 us  [pin(): pl.pallas_call(pin_kernel, out_shape=[pltpu.VMEM(weight.shape, weight.dty...]
    ppermute x3, starting transfers between devices: 3.28 us -> 1.94 us  [swap_dp(): return lax.ppermute(rows, 'dp', [(0, 1), (1, 0)])]
    pallas_call x3 -> x2, Pallas kernels: 9.65 us -> 8.34 us  [outer(): pl.pallas_call(outer_kernel, out_shape=outs, in_specs=[INSIDE] * (1 + cou...]
  transfers between devices with their start and end apart: 23 -> 23, of which waited for: 5 -> 6; matrix products, arithmetic and copies ran while one was open for 0% -> 0% of each run, Pallas kernels for 42% -> 34%
where the time goes in v4:
time: 64.6 us; the launch traced here: 64.4 us
  starting transfers between devices  29 us (45%)
  Pallas kernels  24.6 us (38%)
  waiting for transfers between devices  9.92 us (15%)
  between operations  0.88 us (1%)
    ppermute x8, starting transfers between devices, turn(): got[k] = lax.ppermute(pieces[k], ('section', 'expert', 'dp'), pairs)  17.6 us
    pallas_call x2, Pallas kernels, outer(): pl.pallas_call(outer_kernel, out_shape=outs, in_specs=[INSIDE] * (1 + cou...  8.34 us
    ppermute x4, waiting for transfers between devices, swap_section(): return lax.ppermute(rows, 'section', [(0, 1), (1, 0)])  6.45 us
    pallas_call x1, Pallas kernels, backward(): pl.pallas_call(backward_kernel, out_shape=outs, in_specs=[INSIDE] * 6, ou...  3.67 us
    ppermute x4, starting transfers between devices, swap_section(): return lax.ppermute(rows, 'section', [(0, 1), (1, 0)])  3.52 us
    ppermute x4, starting transfers between devices, swap_plane(): far = lax.ppermute(pieces[2], ('section', 'expert'), both)  3.45 us
    pallas_call x1, Pallas kernels, pin(): pl.pallas_call(pin_kernel, out_shape=[pltpu.VMEM(weight.shape, weight.dty...  2.95 us
    ppermute x4, waiting for transfers between devices, swap_plane(): far = lax.ppermute(pieces[2], ('section', 'expert'), both)  2.83 us
  transfers between devices with their start and end apart: 23, of which 6 were waited for; matrix products, arithmetic and copies ran while one was open for 0% of the time, Pallas kernels for 34%

profile of v4, /device:TPU:1, one launch (start us, length us, event | category | flops | bytes accessed | tf_op | source)
XLA Modules:
  0.0 64.4 jit_solution(8070531191075145673)
XLA Ops:
  0.6 1.3 %shard_map.110 = (bf16[24,1536]{1,0:T(8,128)(2,1)S(1)}, bf16[24,1536]{1,0:T(8,128)(2,1)S(1)}, bf16[24,1536]{1,0:T(8,128)(2,1)S(1)}, bf16[24,1536]{1,0:T(8,128)(2,1)S(1)}) custom-call(bf16[16,3072]{1,0:T(8,128)(2,1)} %refs_0_.2, bf16[16,3072]{1,0:T(8,128)(2,1)} %refs_1_.1, s32[2,16]{1,0:T(2,128)} %bitcast.6, f32[2,16]{1,0:T(2,128)} %bitcast.8), custom_call_target="tpu_custom_call" | custom-call | bytes 491520 | tf_op jit(solution)/shard_map/pallas_call | solution.py:243
  1.9 5.7 %collective-permute-start = (bf16[24,1536]{1,0:T(8,128)(2,1)S(1)}, bf16[24,1536]{1,0:T(8,128)(2,1)S(1)}, u32[]{:S(2)}, u32[]{:S(2)}) collective-permute-start(bf16[24,1536]{1,0:T(8,128)(2,1)S(1)} %get-tuple-element.40), channel_id=1, source_target_pairs={{0,12},{1,28},{2,14},{3,30},{4,8},{5,24},{6,10},{7,26},{8,4},{9,20... | collective-permute-start | bytes 221192 | tf_op jit(solution)/shard_map/ppermute | solution.py:504
  7.7 0.0 collective-permute-start.1
  7.7 1.4 %collective-permute-start.2 = (bf16[24,1536]{1,0:T(8,128)(2,1)S(1)}, bf16[24,1536]{1,0:T(8,128)(2,1)S(1)}, u32[]{:S(2)}, u32[]{:S(2)}) collective-permute-start(bf16[24,1536]{1,0:T(8,128)(2,1)S(1)} %get-tuple-element.42), channel_id=1, source_target_pairs={{0,4},{1,20},{2,6},{3,22},{4,0},{5,16},{6,2},{7,18},{8,12},{9,28},... | collective-permute-start | bytes 221192 | tf_op jit(solution)/shard_map/ppermute | solution.py:504
  9.1 2.3 %collective-permute-start.3 = (bf16[24,1536]{1,0:T(8,128)(2,1)S(1)}, bf16[24,1536]{1,0:T(8,128)(2,1)S(1)}, u32[]{:S(2)}, u32[]{:S(2)}) collective-permute-start(bf16[24,1536]{1,0:T(8,128)(2,1)S(1)} %get-tuple-element.43.refs_1_), channel_id=1, source_target_pairs={{0,0},{1,16},{2,2},{3,18},{4,4},{5,20},{6,6},{7,22},{8,8},{9,24},{... | collective-permute-start | bytes 221192 | tf_op jit(solution)/shard_map/ppermute | solution.py:504
  11.4 0.0 slice-start.2
  11.4 2.9 %shard_map.111.refs_4_.wg_ref = bf16[1536,2048]{1,0:T(8,128)(2,1)S(1)} custom-call(bf16[1536,2048]{1,0:T(8,128)(2,1)} %refs_0_.3, bf16[24,1536]{1,0:T(8,128)(2,1)S(1)} %get-tuple-element.43.refs_1_), custom_call_target="tpu_custom_call" | custom-call | tf_op jit(solution)/shard_map/pallas_call | solution.py:150
  14.4 0.0 slice-start.3
  14.4 0.0 collective-permute-done.refs_0_
  14.4 0.0 collective-permute-done.1.refs_1_
  14.4 0.0 collective-permute-done.2.refs_2_
  14.4 0.3 collective-permute-done.3.refs_3_
  14.7 0.2 shard_map.112
  15.0 0.1 collective-permute-start.4
  15.0 1.3 %collective-permute-start.5 = (bf16[48,1536]{1,0:T(8,128)(2,1)S(1)}, bf16[48,1536]{1,0:T(8,128)(2,1)S(1)}, u32[]{:S(2)}, u32[]{:S(2)}) collective-permute-start(bf16[48,1536]{1,0:T(8,128)(2,1)S(1)} %get-tuple-element.44.refs_3_.refs_5_), channel_id=1, source_target_pairs={{0,2},{2,0},{4,6},{6,4},{8,10},{10,8},{12,14},{14,12},{1,3},{3,1},... | collective-permute-start | bytes 442376 | tf_op jit(solution)/shard_map/ppermute | solution.py:102
  16.3 1.4 %collective-permute-start.6 = (bf16[48,1536]{1,0:T(8,128)(2,1)S(1)}, bf16[48,1536]{1,0:T(8,128)(2,1)S(1)}, u32[]{:S(2)}, u32[]{:S(2)}) collective-permute-start(bf16[48,1536]{1,0:T(8,128)(2,1)S(1)} %get-tuple-element.44.refs_3_.refs_5_), channel_id=1, source_target_pairs={{0,16},{16,0},{1,17},{17,1},{2,18},{18,2},{3,19},{19,3},{4,20},{20... | collective-permute-start | bytes 442376 | tf_op jit(solution)/shard_map/ppermute | solution.py:106
  17.7 0.9 %collective-permute-start.9 = (bf16[48,1536]{1,0:T(8,128)(2,1)S(1)}, bf16[48,1536]{1,0:T(8,128)(2,1)S(1)}, u32[]{:S(2)}, u32[]{:S(2)}) collective-permute-start(bf16[48,1536]{1,0:T(8,128)(2,1)S(1)} %get-tuple-element.51.refs_3_), channel_id=1, source_target_pairs={{0,18},{2,16},{4,22},{6,20},{8,26},{10,24},{12,30},{14,28},{16,2},... | collective-permute-start | bytes 442376 | tf_op jit(solution)/shard_map/ppermute | solution.py:112
  18.6 0.4 collective-permute-start.10
  19.0 2.8 %collective-permute-done.4.refs_0_ = bf16[48,1536]{1,0:T(8,128)(2,1)S(1)} collective-permute-done((bf16[48,1536]{1,0:T(8,128)(2,1)S(1)}, bf16[48,1536]{1,0:T(8,128)(2,1)S(1)}, u32[]{:S(2)}, u32[]{:S(2)}) %collective-permute-start.4) | collective-permute-done | bytes 147488 | tf_op jit(solution)/shard_map/ppermute | solution.py:112
  21.8 0.0 collective-permute-start.11
  21.8 0.3 collective-permute-done.5.refs_1_
  22.1 2.8 %collective-permute-done.6.refs_2_ = bf16[48,1536]{1,0:T(8,128)(2,1)S(1)} collective-permute-done((bf16[48,1536]{1,0:T(8,128)(2,1)S(1)}, bf16[48,1536]{1,0:T(8,128)(2,1)S(1)}, u32[]{:S(2)}, u32[]{:S(2)}) %collective-permute-start.6) | collective-permute-done | bytes 147488 | tf_op jit(solution)/shard_map/ppermute | solution.py:106
  24.8 1.4 %shard_map.113 = (bf16[192,1536]{1,0:T(8,128)(2,1)S(1)}, bf16[192,2048]{1,0:T(8,128)(2,1)S(1)}) custom-call(bf16[48,1536]{1,0:T(8,128)(2,1)S(1)} %collective-permute-done.4.refs_0_, bf16[48,1536]{1,0:T(8,128)(2,1)S(1)} %collective-permute-done.5.refs_1_, bf16[48,1536]{1,0:T(8,128)(2,1)S(1)} %collective-permute-done.6.refs_2_, ...), custom_call_target="tpu_custom_call" | custom-call | tf_op jit(solution)/shard_map/pallas_call | solution.py:172
  26.2 1.2 %collective-permute-start.7 = (bf16[192,2048]{1,0:T(8,128)(2,1)S(1)}, bf16[192,2048]{1,0:T(8,128)(2,1)S(1)}, u32[]{:S(2)}, u32[]{:S(2)}) collective-permute-start(bf16[192,2048]{1,0:T(8,128)(2,1)S(1)} %get-tuple-element.45.g0_ref), channel_id=1, source_target_pairs={{0,1},{1,0},{2,3},{3,2},{4,5},{5,4},{6,7},{7,6},{8,9},{9,8},{10,11... | collective-permute-start | bytes 2359304 | tf_op jit(solution)/shard_map/ppermute | solution.py:491
  27.4 0.0 slice-done.2
  27.4 1.4 %shard_map.114.u0_ref.refs_5_ = bf16[192,2048]{1,0:T(8,128)(2,1)S(1)} custom-call(bf16[192,1536]{1,0:T(8,128)(2,1)S(1)} %get-tuple-element.46.x_ref.refs_0_, bf16[1536,2048]{1,0:T(8,128)(2,1)S(1)} %bitcast.5), custom_call_target="tpu_custom_call" | custom-call | tf_op jit(solution)/shard_map/pallas_call | solution.py:189
  28.8 0.1 collective-permute-start.8
  28.9 0.0 collective-permute-done.9.refs_0_
  28.9 0.0 collective-permute-done.10.refs_1_
  28.9 2.1 %collective-permute-done.11.refs_2_ = bf16[48,1536]{1,0:T(8,128)(2,1)S(1)} collective-permute-done((bf16[48,1536]{1,0:T(8,128)(2,1)S(1)}, bf16[48,1536]{1,0:T(8,128)(2,1)S(1)}, u32[]{:S(2)}, u32[]{:S(2)}) %collective-permute-start.11) | collective-permute-done | bytes 147488 | tf_op jit(solution)/shard_map/ppermute | solution.py:106
  31.0 0.0 slice-done
  31.1 1.4 %shard_map.116 = (bf16[192,1536]{1,0:T(8,128)(2,1)S(1)}, bf16[192,2048]{1,0:T(8,128)(2,1)S(1)}) custom-call(bf16[48,1536]{1,0:T(8,128)(2,1)S(1)} %collective-permute-done.9.refs_0_, bf16[48,1536]{1,0:T(8,128)(2,1)S(1)} %collective-permute-done.10.refs_1_, bf16[48,1536]{1,0:T(8,128)(2,1)S(1)} %collective-permute-done.11.refs_2_, ...), custom_call_target="tpu_custom_call" | custom-call | tf_op jit(solution)/shard_map/pallas_call | solution.py:172
  32.5 0.7 %collective-permute-start.15 = (bf16[192,2048]{1,0:T(8,128)(2,1)S(1)}, bf16[192,2048]{1,0:T(8,128)(2,1)S(1)}, u32[]{:S(2)}, u32[]{:S(2)}) collective-permute-start(bf16[192,2048]{1,0:T(8,128)(2,1)S(1)} %get-tuple-element.52.a0_ref), channel_id=1, source_target_pairs={{0,1},{1,0},{2,3},{3,2},{4,5},{5,4},{6,7},{7,6},{8,9},{9,8},{10,11... | collective-permute-start | bytes 2359304 | tf_op jit(solution)/shard_map/ppermute | solution.py:491
  33.1 0.0 collective-permute-done.7.g1_ref
  33.1 0.0 collective-permute-done.8.u1_ref
  33.1 2.6 %shard_map.115 = (bf16[192,2048]{1,0:T(8,128)(2,1)S(1)}, f32[192,2048]{1,0:T(8,128)S(1)}, f32[192,2048]{1,0:T(8,128)S(1)}, bf16[48,1536]{1,0:T(8,128)(2,1)S(1)},...) custom-call(bf16[192,2048]{1,0:T(8,128)(2,1)S(1)} %get-tuple-element.45.g0_ref, ...), custom_call_target="tpu_custom_call" | custom-call | tf_op jit(solution)/shard_map/pallas_call | solution.py:411
  35.7 1.2 %collective-permute-start.12 = (bf16[48,1536]{1,0:T(8,128)(2,1)S(1)}, bf16[48,1536]{1,0:T(8,128)(2,1)S(1)}, u32[]{:S(2)}, u32[]{:S(2)}) collective-permute-start(bf16[48,1536]{1,0:T(8,128)(2,1)S(1)} %get-tuple-element.53), channel_id=1, source_target_pairs={{0,18},{2,16},{4,22},{6,20},{8,26},{10,24},{12,30},{14,28},{16,2},... | collective-permute-start | bytes 442376 | tf_op jit(solution)/shard_map/ppermute | solution.py:112
  37.0 0.4 collective-permute-start.13
  37.4 1.1 %collective-permute-start.14 = (bf16[48,1536]{1,0:T(8,128)(2,1)S(1)}, bf16[48,1536]{1,0:T(8,128)(2,1)S(1)}, u32[]{:S(2)}, u32[]{:S(2)}) collective-permute-start(bf16[48,1536]{1,0:T(8,128)(2,1)S(1)} %get-tuple-element.55), channel_id=1, source_target_pairs={{0,16},{16,0},{1,17},{17,1},{2,18},{18,2},{3,19},{19,3},{4,20},{20... | collective-permute-start | bytes 442376 | tf_op jit(solution)/shard_map/ppermute | solution.py:106
  38.4 0.0 collective-permute-done.15.a1_ref
  38.4 3.7 %shard_map.117 = (bf16[192,2048]{1,0:T(8,128)(2,1)S(1)}, bf16[192,2048]{1,0:T(8,128)(2,1)S(1)}, bf16[48,1536]{1,0:T(8,128)(2,1)S(1)}, bf16[48,1536]{1,0:T(8,128)...) custom-call(bf16[192,2048]{1,0:T(8,128)(2,1)S(1)} %get-tuple-element.52.a0_ref, ...), custom_call_target="tpu_custom_call" | custom-call | flops 2415919104 | bytes 6881280 | tf_op jit(solution)/shard_map/pallas_call | solution.py:439
  42.1 1.2 %collective-permute-start.16 = (bf16[48,1536]{1,0:T(8,128)(2,1)S(1)}, bf16[48,1536]{1,0:T(8,128)(2,1)S(1)}, u32[]{:S(2)}, u32[]{:S(2)}) collective-permute-start(bf16[48,1536]{1,0:T(8,128)(2,1)S(1)} %get-tuple-element.59), channel_id=1, source_target_pairs={{0,18},{2,16},{4,22},{6,20},{8,26},{10,24},{12,30},{14,28},{16,2},... | collective-permute-start | bytes 442376 | tf_op jit(solution)/shard_map/ppermute | solution.py:112
  43.3 0.4 collective-permute-start.17
  43.8 0.0 collective-permute-done.12.refs_0_
  43.8 1.1 %collective-permute-start.18 = (bf16[48,1536]{1,0:T(8,128)(2,1)S(1)}, bf16[48,1536]{1,0:T(8,128)(2,1)S(1)}, u32[]{:S(2)}, u32[]{:S(2)}) collective-permute-start(bf16[48,1536]{1,0:T(8,128)(2,1)S(1)} %get-tuple-element.61), channel_id=1, source_target_pairs={{0,16},{16,0},{1,17},{17,1},{2,18},{18,2},{3,19},{19,3},{4,20},{20... | collective-permute-start | bytes 442376 | tf_op jit(solution)/shard_map/ppermute | solution.py:106
  44.8 5.1 %shard_map.120 = (bf16[1536,2048]{1,0:T(8,128)(2,1)}, bf16[1536,2048]{1,0:T(8,128)(2,1)}) custom-call(bf16[192,1536]{1,0:T(8,128)(2,1)S(1)} %get-tuple-element.46.x_ref.refs_0_, bf16[192,2048]{1,0:T(8,128)(2,1)S(1)} %get-tuple-element.69.refs_1_, bf16[192,2048]{1,0:T(8,128)(2,1)S(1)} %get-tuple-element.70.refs_2_), custom_call_target="tpu_custom_call" | custom-call | flops 2415919104 | bytes 14745600 | tf_op jit(solution)/shard_map/pallas_call | solution.py:475
  50.0 0.0 copy-start
  50.0 0.0 copy-start.1
  50.0 0.0 collective-permute-done.13.refs_1_
  50.0 0.0 collective-permute-done.14.refs_2_
  50.0 0.0 collective-permute-done.16.refs_4_
  50.0 0.0 collective-permute-done.17.refs_5_
  50.0 1.6 %collective-permute-done.18.refs_6_ = bf16[48,1536]{1,0:T(8,128)(2,1)S(1)} collective-permute-done((bf16[48,1536]{1,0:T(8,128)(2,1)S(1)}, bf16[48,1536]{1,0:T(8,128)(2,1)S(1)}, u32[]{:S(2)}, u32[]{:S(2)}) %collective-permute-start.18) | collective-permute-done | bytes 147488 | tf_op jit(solution)/shard_map/ppermute | solution.py:106
  51.6 0.3 shard_map.118
  51.9 4.1 %collective-permute-start.19 = (bf16[24,1536]{1,0:T(8,128)(2,1)S(1)}, bf16[24,1536]{1,0:T(8,128)(2,1)S(1)}, u32[]{:S(2)}, u32[]{:S(2)}) collective-permute-start(bf16[24,1536]{1,0:T(8,128)(2,1)S(1)} %get-tuple-element.63), channel_id=1, source_target_pairs={{0,12},{1,28},{2,14},{3,30},{4,8},{5,24},{6,10},{7,26},{8,4},{9,20... | collective-permute-start | bytes 221192 | tf_op jit(solution)/shard_map/ppermute | solution.py:504
  56.0 0.0 collective-permute-start.20
  56.0 1.6 %collective-permute-start.21 = (bf16[24,1536]{1,0:T(8,128)(2,1)S(1)}, bf16[24,1536]{1,0:T(8,128)(2,1)S(1)}, u32[]{:S(2)}, u32[]{:S(2)}) collective-permute-start(bf16[24,1536]{1,0:T(8,128)(2,1)S(1)} %get-tuple-element.65), channel_id=1, source_target_pairs={{0,4},{1,20},{2,6},{3,22},{4,0},{5,16},{6,2},{7,18},{8,12},{9,28},... | collective-permute-start | bytes 221192 | tf_op jit(solution)/shard_map/ppermute | solution.py:504
  57.6 2.5 %collective-permute-start.22 = (bf16[24,1536]{1,0:T(8,128)(2,1)S(1)}, bf16[24,1536]{1,0:T(8,128)(2,1)S(1)}, u32[]{:S(2)}, u32[]{:S(2)}) collective-permute-start(bf16[24,1536]{1,0:T(8,128)(2,1)S(1)} %get-tuple-element.66), channel_id=1, source_target_pairs={{0,0},{1,16},{2,2},{3,18},{4,4},{5,20},{6,6},{7,22},{8,8},{9,24},{... | collective-permute-start | bytes 221192 | tf_op jit(solution)/shard_map/ppermute | solution.py:504
  60.1 3.2 %shard_map.121 = bf16[1536,2048]{1,0:T(8,128)(2,1)} custom-call(bf16[192,1536]{1,0:T(8,128)(2,1)S(1)} %get-tuple-element.73.refs_0_, bf16[192,2048]{1,0:T(8,128)(2,1)S(1)} %get-tuple-element.74.refs_1_), custom_call_target="tpu_custom_call" | custom-call | flops 1207959552 | bytes 7667712 | tf_op jit(solution)/shard_map/pallas_call | solution.py:475
  63.3 0.0 collective-permute-done.19.refs_0_
  63.3 0.0 collective-permute-done.20.refs_1_
  63.3 0.0 collective-permute-done.21.refs_2_
  63.4 0.0 collective-permute-done.22.refs_3_
  63.4 1.0 %shard_map.119 = (bf16[16,1536]{1,0:T(8,128)(2,1)}, bf16[16,1536]{1,0:T(8,128)(2,1)}) custom-call(bf16[24,1536]{1,0:T(8,128)(2,1)S(1)} %collective-permute-done.19.refs_0_, bf16[24,1536]{1,0:T(8,128)(2,1)S(1)} %collective-permute-done.20.refs_1_, bf16[24,1536]{1,0:T(8,128)(2,1)S(1)} %collective-permute-done.21.refs_2_, ...), custom_call_target="tpu_custom_call" | custom-call | bytes 393216 | tf_op jit(solution)/shard_map/pallas_call | solution.py:349
  (8 shorter events, 0.0 us)
Async XLA Ops:
  1.9 12.4 %collective-permute-start = (bf16[24,1536]{1,0:T(8,128)(2,1)S(1)}, bf16[24,1536]{1,0:T(8,128)(2,1)S(1)}, u32[]{:S(2)}, u32[]{:S(2)}) collective-permute-start(bf16[24,1536]{1,0:T(8,128)(2,1)S(1)} %get-tuple-element.40), channel_id=1, source_target_pairs={{0,12},{1,28},{2,14},{3,30},{4,8},{5,24},{6,10},{7,26},{8,4},{9,20... | collective-permute-start | bytes 221192 | tf_op jit(solution)/shard_map/ppermute | solution.py:504
  7.7 6.7 %collective-permute-start.1 = (bf16[24,1536]{1,0:T(8,128)(2,1)S(1)}, bf16[24,1536]{1,0:T(8,128)(2,1)S(1)}, u32[]{:S(2)}, u32[]{:S(2)}) collective-permute-start(bf16[24,1536]{1,0:T(8,128)(2,1)S(1)} %get-tuple-element.41), channel_id=1, source_target_pairs={{0,8},{1,24},{2,10},{3,26},{4,12},{5,28},{6,14},{7,30},{8,0},{9,16... | collective-permute-start | bytes 221192 | tf_op jit(solution)/shard_map/ppermute | solution.py:504
  7.7 6.7 %collective-permute-start.2 = (bf16[24,1536]{1,0:T(8,128)(2,1)S(1)}, bf16[24,1536]{1,0:T(8,128)(2,1)S(1)}, u32[]{:S(2)}, u32[]{:S(2)}) collective-permute-start(bf16[24,1536]{1,0:T(8,128)(2,1)S(1)} %get-tuple-element.42), channel_id=1, source_target_pairs={{0,4},{1,20},{2,6},{3,22},{4,0},{5,16},{6,2},{7,18},{8,12},{9,28},... | collective-permute-start | bytes 221192 | tf_op jit(solution)/shard_map/ppermute | solution.py:504
  9.1 5.7 %collective-permute-start.3 = (bf16[24,1536]{1,0:T(8,128)(2,1)S(1)}, bf16[24,1536]{1,0:T(8,128)(2,1)S(1)}, u32[]{:S(2)}, u32[]{:S(2)}) collective-permute-start(bf16[24,1536]{1,0:T(8,128)(2,1)S(1)} %get-tuple-element.43.refs_1_), channel_id=1, source_target_pairs={{0,0},{1,16},{2,2},{3,18},{4,4},{5,20},{6,6},{7,22},{8,8},{9,24},{... | collective-permute-start | bytes 221192 | tf_op jit(solution)/shard_map/ppermute | solution.py:504
  11.4 16.0 %slice-start.2 = ((s8[6291456]{0:T(1024)(128)(4,1)}), s8[4194304]{0:T(1024)(128)(4,1)S(1)}, s32[]{:S(2)}) async-start(s8[6291456]{0:T(1024)(128)(4,1)} %bitcast.4), calls=%async_computation.2 | async-start | bytes 8388608
  14.4 13.0 %slice-start.3 = ((s8[6291456]{0:T(1024)(128)(4,1)}), s8[2097152]{0:T(1024)(128)(4,1)S(1)}, s32[]{:S(2)}) async-start(s8[6291456]{0:T(1024)(128)(4,1)} %bitcast.4), calls=%async_computation.3 | async-start | bytes 4194304
  15.0 6.8 %collective-permute-start.4 = (bf16[48,1536]{1,0:T(8,128)(2,1)S(1)}, bf16[48,1536]{1,0:T(8,128)(2,1)S(1)}, u32[]{:S(2)}, u32[]{:S(2)}) collective-permute-start(bf16[48,1536]{1,0:T(8,128)(2,1)S(1)} %get-tuple-element.44.refs_3_.refs_5_), channel_id=1, source_target_pairs={{0,18},{2,16},{4,22},{6,20},{8,26},{10,24},{12,30},{14,28},{16,2},... | collective-permute-start | bytes 442376 | tf_op jit(solution)/shard_map/ppermute | solution.py:112
  15.0 7.0 %collective-permute-start.5 = (bf16[48,1536]{1,0:T(8,128)(2,1)S(1)}, bf16[48,1536]{1,0:T(8,128)(2,1)S(1)}, u32[]{:S(2)}, u32[]{:S(2)}) collective-permute-start(bf16[48,1536]{1,0:T(8,128)(2,1)S(1)} %get-tuple-element.44.refs_3_.refs_5_), channel_id=1, source_target_pairs={{0,2},{2,0},{4,6},{6,4},{8,10},{10,8},{12,14},{14,12},{1,3},{3,1},... | collective-permute-start | bytes 442376 | tf_op jit(solution)/shard_map/ppermute | solution.py:102
  16.3 8.5 %collective-permute-start.6 = (bf16[48,1536]{1,0:T(8,128)(2,1)S(1)}, bf16[48,1536]{1,0:T(8,128)(2,1)S(1)}, u32[]{:S(2)}, u32[]{:S(2)}) collective-permute-start(bf16[48,1536]{1,0:T(8,128)(2,1)S(1)} %get-tuple-element.44.refs_3_.refs_5_), channel_id=1, source_target_pairs={{0,16},{16,0},{1,17},{17,1},{2,18},{18,2},{3,19},{19,3},{4,20},{20... | collective-permute-start | bytes 442376 | tf_op jit(solution)/shard_map/ppermute | solution.py:106
  17.7 13.4 %slice-start = ((s8[6291456]{0:T(1024)(128)(4,1)}), s8[4194304]{0:T(1024)(128)(4,1)S(1)}, s32[]{:S(2)}) async-start(s8[6291456]{0:T(1024)(128)(4,1)} %bitcast.2), calls=%async_computation | async-start | bytes 8388608
  17.7 11.3 %collective-permute-start.9 = (bf16[48,1536]{1,0:T(8,128)(2,1)S(1)}, bf16[48,1536]{1,0:T(8,128)(2,1)S(1)}, u32[]{:S(2)}, u32[]{:S(2)}) collective-permute-start(bf16[48,1536]{1,0:T(8,128)(2,1)S(1)} %get-tuple-element.51.refs_3_), channel_id=1, source_target_pairs={{0,18},{2,16},{4,22},{6,20},{8,26},{10,24},{12,30},{14,28},{16,2},... | collective-permute-start | bytes 442376 | tf_op jit(solution)/shard_map/ppermute | solution.py:112
  18.6 10.3 %collective-permute-start.10 = (bf16[48,1536]{1,0:T(8,128)(2,1)S(1)}, bf16[48,1536]{1,0:T(8,128)(2,1)S(1)}, u32[]{:S(2)}, u32[]{:S(2)}) collective-permute-start(bf16[48,1536]{1,0:T(8,128)(2,1)S(1)} %get-tuple-element.51.refs_3_), channel_id=1, source_target_pairs={{0,2},{2,0},{4,6},{6,4},{8,10},{10,8},{12,14},{14,12},{1,3},{3,1},... | collective-permute-start | bytes 442376 | tf_op jit(solution)/shard_map/ppermute | solution.py:102
  21.8 9.2 %collective-permute-start.11 = (bf16[48,1536]{1,0:T(8,128)(2,1)S(1)}, bf16[48,1536]{1,0:T(8,128)(2,1)S(1)}, u32[]{:S(2)}, u32[]{:S(2)}) collective-permute-start(bf16[48,1536]{1,0:T(8,128)(2,1)S(1)} %get-tuple-element.51.refs_3_), channel_id=1, source_target_pairs={{0,16},{16,0},{1,17},{17,1},{2,18},{18,2},{3,19},{19,3},{4,20},{20... | collective-permute-start | bytes 442376 | tf_op jit(solution)/shard_map/ppermute | solution.py:106
  26.2 6.9 %collective-permute-start.7 = (bf16[192,2048]{1,0:T(8,128)(2,1)S(1)}, bf16[192,2048]{1,0:T(8,128)(2,1)S(1)}, u32[]{:S(2)}, u32[]{:S(2)}) collective-permute-start(bf16[192,2048]{1,0:T(8,128)(2,1)S(1)} %get-tuple-element.45.g0_ref), channel_id=1, source_target_pairs={{0,1},{1,0},{2,3},{3,2},{4,5},{5,4},{6,7},{7,6},{8,9},{9,8},{10,11... | collective-permute-start | bytes 2359304 | tf_op jit(solution)/shard_map/ppermute | solution.py:491
  27.4 3.6 %slice-start.1 = ((s8[6291456]{0:T(1024)(128)(4,1)}), s8[2097152]{0:T(1024)(128)(4,1)S(1)}, s32[]{:S(2)}) async-start(s8[6291456]{0:T(1024)(128)(4,1)} %bitcast.2), calls=%async_computation.1 | async-start | bytes 4194304
  28.8 4.3 %collective-permute-start.8 = (bf16[192,2048]{1,0:T(8,128)(2,1)S(1)}, bf16[192,2048]{1,0:T(8,128)(2,1)S(1)}, u32[]{:S(2)}, u32[]{:S(2)}) collective-permute-start(bf16[192,2048]{1,0:T(8,128)(2,1)S(1)} %shard_map.114.u0_ref.refs_5_), channel_id=1, source_target_pairs={{0,1},{1,0},{2,3},{3,2},{4,5},{5,4},{6,7},{7,6},{8,9},{9,8},{10,11... | collective-permute-start | bytes 2359304 | tf_op jit(solution)/shard_map/ppermute | solution.py:491
  32.5 6.0 %collective-permute-start.15 = (bf16[192,2048]{1,0:T(8,128)(2,1)S(1)}, bf16[192,2048]{1,0:T(8,128)(2,1)S(1)}, u32[]{:S(2)}, u32[]{:S(2)}) collective-permute-start(bf16[192,2048]{1,0:T(8,128)(2,1)S(1)} %get-tuple-element.52.a0_ref), channel_id=1, source_target_pairs={{0,1},{1,0},{2,3},{3,2},{4,5},{5,4},{6,7},{7,6},{8,9},{9,8},{10,11... | collective-permute-start | bytes 2359304 | tf_op jit(solution)/shard_map/ppermute | solution.py:491
  35.7 8.0 %collective-permute-start.12 = (bf16[48,1536]{1,0:T(8,128)(2,1)S(1)}, bf16[48,1536]{1,0:T(8,128)(2,1)S(1)}, u32[]{:S(2)}, u32[]{:S(2)}) collective-permute-start(bf16[48,1536]{1,0:T(8,128)(2,1)S(1)} %get-tuple-element.53), channel_id=1, source_target_pairs={{0,18},{2,16},{4,22},{6,20},{8,26},{10,24},{12,30},{14,28},{16,2},... | collective-permute-start | bytes 442376 | tf_op jit(solution)/shard_map/ppermute | solution.py:112
  37.0 13.1 %collective-permute-start.13 = (bf16[48,1536]{1,0:T(8,128)(2,1)S(1)}, bf16[48,1536]{1,0:T(8,128)(2,1)S(1)}, u32[]{:S(2)}, u32[]{:S(2)}) collective-permute-start(bf16[48,1536]{1,0:T(8,128)(2,1)S(1)} %get-tuple-element.54), channel_id=1, source_target_pairs={{0,2},{2,0},{4,6},{6,4},{8,10},{10,8},{12,14},{14,12},{1,3},{3,1},... | collective-permute-start | bytes 442376 | tf_op jit(solution)/shard_map/ppermute | solution.py:102
  37.4 12.7 %collective-permute-start.14 = (bf16[48,1536]{1,0:T(8,128)(2,1)S(1)}, bf16[48,1536]{1,0:T(8,128)(2,1)S(1)}, u32[]{:S(2)}, u32[]{:S(2)}) collective-permute-start(bf16[48,1536]{1,0:T(8,128)(2,1)S(1)} %get-tuple-element.55), channel_id=1, source_target_pairs={{0,16},{16,0},{1,17},{17,1},{2,18},{18,2},{3,19},{19,3},{4,20},{20... | collective-permute-start | bytes 442376 | tf_op jit(solution)/shard_map/ppermute | solution.py:106
  42.1 7.9 %collective-permute-start.16 = (bf16[48,1536]{1,0:T(8,128)(2,1)S(1)}, bf16[48,1536]{1,0:T(8,128)(2,1)S(1)}, u32[]{:S(2)}, u32[]{:S(2)}) collective-permute-start(bf16[48,1536]{1,0:T(8,128)(2,1)S(1)} %get-tuple-element.59), channel_id=1, source_target_pairs={{0,18},{2,16},{4,22},{6,20},{8,26},{10,24},{12,30},{14,28},{16,2},... | collective-permute-start | bytes 442376 | tf_op jit(solution)/shard_map/ppermute | solution.py:112
  43.3 6.7 %collective-permute-start.17 = (bf16[48,1536]{1,0:T(8,128)(2,1)S(1)}, bf16[48,1536]{1,0:T(8,128)(2,1)S(1)}, u32[]{:S(2)}, u32[]{:S(2)}) collective-permute-start(bf16[48,1536]{1,0:T(8,128)(2,1)S(1)} %get-tuple-element.60), channel_id=1, source_target_pairs={{0,2},{2,0},{4,6},{6,4},{8,10},{10,8},{12,14},{14,12},{1,3},{3,1},... | collective-permute-start | bytes 442376 | tf_op jit(solution)/shard_map/ppermute | solution.py:102
  43.8 7.9 %collective-permute-start.18 = (bf16[48,1536]{1,0:T(8,128)(2,1)S(1)}, bf16[48,1536]{1,0:T(8,128)(2,1)S(1)}, u32[]{:S(2)}, u32[]{:S(2)}) collective-permute-start(bf16[48,1536]{1,0:T(8,128)(2,1)S(1)} %get-tuple-element.61), channel_id=1, source_target_pairs={{0,16},{16,0},{1,17},{17,1},{2,18},{18,2},{3,19},{19,3},{4,20},{20... | collective-permute-start | bytes 442376 | tf_op jit(solution)/shard_map/ppermute | solution.py:106
  50.0 13.4 %copy-start = (s32[16,2]{0,1:T(2,128)S(1)}, s32[16,2]{0,1:T(2,128)}, u32[]{:S(2)}) copy-start(s32[16,2]{0,1:T(2,128)} %param.9) | copy-start | bytes 388
  50.0 13.4 %copy-start.1 = (f32[16,2]{0,1:T(2,128)S(1)}, f32[16,2]{0,1:T(2,128)}, u32[]{:S(2)}) copy-start(f32[16,2]{0,1:T(2,128)} %param.10) | copy-start | bytes 388
  51.9 11.4 %collective-permute-start.19 = (bf16[24,1536]{1,0:T(8,128)(2,1)S(1)}, bf16[24,1536]{1,0:T(8,128)(2,1)S(1)}, u32[]{:S(2)}, u32[]{:S(2)}) collective-permute-start(bf16[24,1536]{1,0:T(8,128)(2,1)S(1)} %get-tuple-element.63), channel_id=1, source_target_pairs={{0,12},{1,28},{2,14},{3,30},{4,8},{5,24},{6,10},{7,26},{8,4},{9,20... | collective-permute-start | bytes 221192 | tf_op jit(solution)/shard_map/ppermute | solution.py:504
  56.0 7.3 %collective-permute-start.20 = (bf16[24,1536]{1,0:T(8,128)(2,1)S(1)}, bf16[24,1536]{1,0:T(8,128)(2,1)S(1)}, u32[]{:S(2)}, u32[]{:S(2)}) collective-permute-start(bf16[24,1536]{1,0:T(8,128)(2,1)S(1)} %get-tuple-element.64), channel_id=1, source_target_pairs={{0,8},{1,24},{2,10},{3,26},{4,12},{5,28},{6,14},{7,30},{8,0},{9,16... | collective-permute-start | bytes 221192 | tf_op jit(solution)/shard_map/ppermute | solution.py:504
  56.0 7.3 %collective-permute-start.21 = (bf16[24,1536]{1,0:T(8,128)(2,1)S(1)}, bf16[24,1536]{1,0:T(8,128)(2,1)S(1)}, u32[]{:S(2)}, u32[]{:S(2)}) collective-permute-start(bf16[24,1536]{1,0:T(8,128)(2,1)S(1)} %get-tuple-element.65), channel_id=1, source_target_pairs={{0,4},{1,20},{2,6},{3,22},{4,0},{5,16},{6,2},{7,18},{8,12},{9,28},... | collective-permute-start | bytes 221192 | tf_op jit(solution)/shard_map/ppermute | solution.py:504
  57.6 5.7 %collective-permute-start.22 = (bf16[24,1536]{1,0:T(8,128)(2,1)S(1)}, bf16[24,1536]{1,0:T(8,128)(2,1)S(1)}, u32[]{:S(2)}, u32[]{:S(2)}) collective-permute-start(bf16[24,1536]{1,0:T(8,128)(2,1)S(1)} %get-tuple-element.66), channel_id=1, source_target_pairs={{0,0},{1,16},{2,2},{3,18},{4,4},{5,20},{6,6},{7,22},{8,8},{9,24},{... | collective-permute-start | bytes 221192 | tf_op jit(solution)/shard_map/ppermute | solution.py:504

commit v5 on v4

--- a/solution.py
+++ b/solution.py
@@ -273,7 +273,7 @@
 
 
 def part_kernel(*refs):
-    refs, (_, tok_ref, grad_ref, held_ref) = refs[:EXP][::-1], refs[EXP:]
+    refs, (_, tok_ref, grad_ref, held_ref) = [refs[i] for i in (3, 2, 0, 1)], refs[EXP:]
     rows = jnp.dot(sorting(), stack(refs, held_ref), preferred_element_type=F32).astype(BF)
     n = EXP * CAP
     tok_ref[...] = rows[:n]
@@ -291,7 +291,7 @@
         scratch_shapes=[pltpu.VMEM((2 * EXP * CAP, width), F32)],
         cost_estimate=cost(0, *got, *outs),
         compiler_params=params(8),
-    )(*got[::-1], after)
+    )(*[got[i] for i in (2, 3, 1, 0)], after)
 
 
 def join_kernel(*refs):
@@ -332,15 +332,18 @@
         for j in range(2)
     ]
 
-    def found(where):
-        return contract_rows(jnp.logical_and(picks, where).astype(BF), rows)
-
     first = place < CAP
-    out_ref[...] = (
-        probs[0] * found(jnp.logical_and(first, match[0]))
-        + probs[1] * found(jnp.logical_and(first, match[1]))
-    ).astype(BF)
-    in_ref[...] = found(jnp.logical_not(first)).astype(BF)
+    masks = [
+        jnp.logical_and(picks, where).astype(BF)
+        for where in (
+            jnp.logical_and(first, match[0]),
+            jnp.logical_and(first, match[1]),
+            jnp.logical_not(first),
+        )
+    ]
+    found = contract_rows(jnp.concatenate(masks, axis=1), rows)
+    out_ref[...] = (probs[0] * found[:count] + probs[1] * found[count : 2 * count]).astype(BF)
+    in_ref[...] = found[2 * count :].astype(BF)
 
 
 def unpack(back, expert_ids, gate_probs):
@@ -508,8 +511,8 @@
 def paired(tokens, grad_out, expert_ids, gate_probs, gate_weight, up_weight, down_weight):
     payload = pack(tokens, grad_out, expert_ids, gate_probs, gate_weight.shape[0])
     got = turn(payload)
-    (gate_weight,) = pin((gate_weight,), payload[0])
-    own_t, own_g = part(got, gate_weight)
+    own_t, own_g = part(got, payload[0])
+    (gate_weight,) = pin((gate_weight,), own_t)
 
     slot_t, gate_part = gather_project([own_t] + swap_plane([own_t] * 3), gate_weight, own_t)
     gates = [gate_part, swap_dp(gate_part)]

time: 64.6 us -> 64.7 us (level)
  starting transfers between devices: 29 us -> 31.1 us
  waiting for transfers between devices: 9.92 us -> 7.89 us
    ppermute x4, waiting for transfers between devices: 6.45 us -> 2.56 us  [swap_section(): return lax.ppermute(rows, 'section', [(0, 1), (1, 0)])]
    ppermute x8, waiting for transfers between devices: 0.34 us -> 2.72 us  [turn(): got[k] = lax.ppermute(pieces[k], ('section', 'expert', 'dp'), pairs)]
    ppermute x3, starting transfers between devices: 1.94 us -> 4.19 us  [swap_dp(): return lax.ppermute(rows, 'dp', [(0, 1), (1, 0)])]
  transfers between devices with their start and end apart: 23 -> 23, of which waited for: 6 -> 7; matrix products, arithmetic and copies ran while one was open for 0% -> 0% of each run, Pallas kernels for 34% -> 33%
where the time goes in v5:
time: 64.7 us; the launch traced here: 64.5 us
  starting transfers between devices  31.1 us (48%)
  Pallas kernels  24.5 us (38%)
  waiting for transfers between devices  7.89 us (12%)
  between operations  0.87 us (1%)
    ppermute x8, starting transfers between devices, turn(): got[k] = lax.ppermute(pieces[k], ('section', 'expert', 'dp'), pairs)  17.5 us
    pallas_call x2, Pallas kernels, outer(): pl.pallas_call(outer_kernel, out_shape=outs, in_specs=[INSIDE] * (1 + cou...  8.33 us
    ppermute x3, starting transfers between devices, swap_dp(): return lax.ppermute(rows, 'dp', [(0, 1), (1, 0)])  4.19 us
    ppermute x4, starting transfers between devices, swap_section(): return lax.ppermute(rows, 'section', [(0, 1), (1, 0)])  4.03 us
    pallas_call x1, Pallas kernels, backward(): pl.pallas_call(backward_kernel, out_shape=outs, in_specs=[INSIDE] * 6, ou...  3.67 us
    ppermute x4, starting transfers between devices, swap_plane(): far = lax.ppermute(pieces[2], ('section', 'expert'), both)  2.89 us
    pallas_call x2, Pallas kernels, gather_project(): pl.pallas_call(gather_kernel, out_shape=outs, in_specs=[INSIDE] * (len(pi...  2.8 us
    pallas_call x1, Pallas kernels, pin(): pl.pallas_call(pin_kernel, out_shape=[pltpu.VMEM(weight.shape, weight.dty...  2.79 us
  transfers between devices with their start and end apart: 23, of which 7 were waited for; matrix products, arithmetic and copies ran while one was open for 0% of the time, Pallas kernels for 33%

profile of v5, /device:TPU:1, one launch (start us, length us, event | category | flops | bytes accessed | tf_op | source)
XLA Modules:
  0.0 64.5 jit_solution(11467892692753281265)
XLA Ops:
  0.6 1.3 %shard_map.110 = (bf16[24,1536]{1,0:T(8,128)(2,1)S(1)}, bf16[24,1536]{1,0:T(8,128)(2,1)S(1)}, bf16[24,1536]{1,0:T(8,128)(2,1)S(1)}, bf16[24,1536]{1,0:T(8,128)(2,1)S(1)}) custom-call(bf16[16,3072]{1,0:T(8,128)(2,1)} %refs_0_.2, bf16[16,3072]{1,0:T(8,128)(2,1)} %refs_1_.1, s32[2,16]{1,0:T(2,128)} %bitcast.6, f32[2,16]{1,0:T(2,128)} %bitcast.8), custom_call_target="tpu_custom_call" | custom-call | bytes 491520 | tf_op jit(solution)/shard_map/pallas_call | solution.py:243
  1.9 4.7 %collective-permute-start = (bf16[24,1536]{1,0:T(8,128)(2,1)S(1)}, bf16[24,1536]{1,0:T(8,128)(2,1)S(1)}, u32[]{:S(2)}, u32[]{:S(2)}) collective-permute-start(bf16[24,1536]{1,0:T(8,128)(2,1)S(1)} %get-tuple-element.40), channel_id=1, source_target_pairs={{0,8},{1,24},{2,10},{3,26},{4,12},{5,28},{6,14},{7,30},{8,0},{9,16... | collective-permute-start | bytes 221192 | tf_op jit(solution)/shard_map/ppermute | solution.py:507
  6.7 1.1 %collective-permute-start.1 = (bf16[24,1536]{1,0:T(8,128)(2,1)S(1)}, bf16[24,1536]{1,0:T(8,128)(2,1)S(1)}, u32[]{:S(2)}, u32[]{:S(2)}) collective-permute-start(bf16[24,1536]{1,0:T(8,128)(2,1)S(1)} %get-tuple-element.41), channel_id=1, source_target_pairs={{0,12},{1,28},{2,14},{3,30},{4,8},{5,24},{6,10},{7,26},{8,4},{9,20... | collective-permute-start | bytes 221192 | tf_op jit(solution)/shard_map/ppermute | solution.py:507
  7.7 0.4 collective-permute-start.2
  8.2 3.1 %collective-permute-start.3 = (bf16[24,1536]{1,0:T(8,128)(2,1)S(1)}, bf16[24,1536]{1,0:T(8,128)(2,1)S(1)}, u32[]{:S(2)}, u32[]{:S(2)}) collective-permute-start(bf16[24,1536]{1,0:T(8,128)(2,1)S(1)} %get-tuple-element.43.refs_4_), channel_id=1, source_target_pairs={{0,0},{1,16},{2,2},{3,18},{4,4},{5,20},{6,6},{7,22},{8,8},{9,24},{... | collective-permute-start | bytes 221192 | tf_op jit(solution)/shard_map/ppermute | solution.py:507
  11.3 0.5 collective-permute-done.refs_0_
  11.8 1.4 %collective-permute-done.1.refs_1_ = bf16[24,1536]{1,0:T(8,128)(2,1)S(1)} collective-permute-done((bf16[24,1536]{1,0:T(8,128)(2,1)S(1)}, bf16[24,1536]{1,0:T(8,128)(2,1)S(1)}, u32[]{:S(2)}, u32[]{:S(2)}) %collective-permute-start.1) | collective-permute-done | bytes 73760 | tf_op jit(solution)/shard_map/ppermute | solution.py:507
  13.2 0.0 collective-permute-done.2.refs_2_
  13.3 0.8 %collective-permute-done.3.refs_3_ = bf16[24,1536]{1,0:T(8,128)(2,1)S(1)} collective-permute-done((bf16[24,1536]{1,0:T(8,128)(2,1)S(1)}, bf16[24,1536]{1,0:T(8,128)(2,1)S(1)}, u32[]{:S(2)}, u32[]{:S(2)}) %collective-permute-start.3) | collective-permute-done | bytes 73760 | tf_op jit(solution)/shard_map/ppermute | solution.py:507
  14.0 0.2 shard_map.111
  14.3 0.1 collective-permute-start.4
  14.3 1.3 %collective-permute-start.5 = (bf16[48,1536]{1,0:T(8,128)(2,1)S(1)}, bf16[48,1536]{1,0:T(8,128)(2,1)S(1)}, u32[]{:S(2)}, u32[]{:S(2)}) collective-permute-start(bf16[48,1536]{1,0:T(8,128)(2,1)S(1)} %get-tuple-element.44.refs_1_.refs_3_.refs_5_), channel_id=1, source_target_pairs={{0,2},{2,0},{4,6},{6,4},{8,10},{10,8},{12,14},{14,12},{1,3},{3,1},... | collective-permute-start | bytes 442376 | tf_op jit(solution)/shard_map/ppermute | solution.py:102
  15.6 1.4 %collective-permute-start.6 = (bf16[48,1536]{1,0:T(8,128)(2,1)S(1)}, bf16[48,1536]{1,0:T(8,128)(2,1)S(1)}, u32[]{:S(2)}, u32[]{:S(2)}) collective-permute-start(bf16[48,1536]{1,0:T(8,128)(2,1)S(1)} %get-tuple-element.44.refs_1_.refs_3_.refs_5_), channel_id=1, source_target_pairs={{0,16},{16,0},{1,17},{17,1},{2,18},{18,2},{3,19},{19,3},{4,20},{20... | collective-permute-start | bytes 442376 | tf_op jit(solution)/shard_map/ppermute | solution.py:106
  17.0 0.9 %collective-permute-start.9 = (bf16[48,1536]{1,0:T(8,128)(2,1)S(1)}, bf16[48,1536]{1,0:T(8,128)(2,1)S(1)}, u32[]{:S(2)}, u32[]{:S(2)}) collective-permute-start(bf16[48,1536]{1,0:T(8,128)(2,1)S(1)} %get-tuple-element.51.refs_3_), channel_id=1, source_target_pairs={{0,18},{2,16},{4,22},{6,20},{8,26},{10,24},{12,30},{14,28},{16,2},... | collective-permute-start | bytes 442376 | tf_op jit(solution)/shard_map/ppermute | solution.py:112
  17.9 0.4 collective-permute-start.10
  18.3 2.3 %collective-permute-done.4.refs_0_ = bf16[48,1536]{1,0:T(8,128)(2,1)S(1)} collective-permute-done((bf16[48,1536]{1,0:T(8,128)(2,1)S(1)}, bf16[48,1536]{1,0:T(8,128)(2,1)S(1)}, u32[]{:S(2)}, u32[]{:S(2)}) %collective-permute-start.4) | collective-permute-done | bytes 147488 | tf_op jit(solution)/shard_map/ppermute | solution.py:112
  20.6 0.0 collective-permute-start.11
  20.6 2.8 %shard_map.112.refs_4_.wg_ref = bf16[1536,2048]{1,0:T(8,128)(2,1)S(1)} custom-call(bf16[1536,2048]{1,0:T(8,128)(2,1)} %refs_0_.3, bf16[48,1536]{1,0:T(8,128)(2,1)S(1)} %get-tuple-element.44.refs_1_.refs_3_.refs_5_), custom_call_target="tpu_custom_call" | custom-call | tf_op jit(solution)/shard_map/pallas_call | solution.py:150
  23.4 0.0 slice-start
  23.4 0.0 collective-permute-done.5.refs_1_
  23.4 0.8 %collective-permute-done.6.refs_2_ = bf16[48,1536]{1,0:T(8,128)(2,1)S(1)} collective-permute-done((bf16[48,1536]{1,0:T(8,128)(2,1)S(1)}, bf16[48,1536]{1,0:T(8,128)(2,1)S(1)}, u32[]{:S(2)}, u32[]{:S(2)}) %collective-permute-start.6) | collective-permute-done | bytes 147488 | tf_op jit(solution)/shard_map/ppermute | solution.py:106
  24.2 1.4 %shard_map.113 = (bf16[192,1536]{1,0:T(8,128)(2,1)S(1)}, bf16[192,2048]{1,0:T(8,128)(2,1)S(1)}) custom-call(bf16[48,1536]{1,0:T(8,128)(2,1)S(1)} %collective-permute-done.4.refs_0_, bf16[48,1536]{1,0:T(8,128)(2,1)S(1)} %collective-permute-done.5.refs_1_, bf16[48,1536]{1,0:T(8,128)(2,1)S(1)} %collective-permute-done.6.refs_2_, ...), custom_call_target="tpu_custom_call" | custom-call | tf_op jit(solution)/shard_map/pallas_call | solution.py:172
  25.6 3.6 %collective-permute-start.7 = (bf16[192,2048]{1,0:T(8,128)(2,1)S(1)}, bf16[192,2048]{1,0:T(8,128)(2,1)S(1)}, u32[]{:S(2)}, u32[]{:S(2)}) collective-permute-start(bf16[192,2048]{1,0:T(8,128)(2,1)S(1)} %get-tuple-element.45.g0_ref), channel_id=1, source_target_pairs={{0,1},{1,0},{2,3},{3,2},{4,5},{5,4},{6,7},{7,6},{8,9},{9,8},{10,11... | collective-permute-start | bytes 2359304 | tf_op jit(solution)/shard_map/ppermute | solution.py:494
  29.2 0.0 slice-done.3
  29.2 1.4 %shard_map.114.u0_ref.refs_5_ = bf16[192,2048]{1,0:T(8,128)(2,1)S(1)} custom-call(bf16[192,1536]{1,0:T(8,128)(2,1)S(1)} %get-tuple-element.46.x_ref.refs_0_, bf16[1536,2048]{1,0:T(8,128)(2,1)S(1)} %bitcast.5), custom_call_target="tpu_custom_call" | custom-call | tf_op jit(solution)/shard_map/pallas_call | solution.py:189
  30.6 0.1 collective-permute-start.8
  30.7 0.0 collective-permute-done.9.refs_0_
  30.7 0.0 collective-permute-done.10.refs_1_
  30.7 0.0 collective-permute-done.11.refs_2_
  30.7 0.0 slice-done
  30.7 0.1 slice-done.1
  30.8 1.4 %shard_map.116 = (bf16[192,1536]{1,0:T(8,128)(2,1)S(1)}, bf16[192,2048]{1,0:T(8,128)(2,1)S(1)}) custom-call(bf16[48,1536]{1,0:T(8,128)(2,1)S(1)} %collective-permute-done.9.refs_0_, bf16[48,1536]{1,0:T(8,128)(2,1)S(1)} %collective-permute-done.10.refs_1_, bf16[48,1536]{1,0:T(8,128)(2,1)S(1)} %collective-permute-done.11.refs_2_, ...), custom_call_target="tpu_custom_call" | custom-call | tf_op jit(solution)/shard_map/pallas_call | solution.py:172
  32.2 0.5 collective-permute-start.15
  32.7 0.0 collective-permute-done.7.g1_ref
  32.7 0.3 collective-permute-done.8.u1_ref
  33.0 2.6 %shard_map.115 = (bf16[192,2048]{1,0:T(8,128)(2,1)S(1)}, f32[192,2048]{1,0:T(8,128)S(1)}, f32[192,2048]{1,0:T(8,128)S(1)}, bf16[48,1536]{1,0:T(8,128)(2,1)S(1)},...) custom-call(bf16[192,2048]{1,0:T(8,128)(2,1)S(1)} %get-tuple-element.45.g0_ref, ...), custom_call_target="tpu_custom_call" | custom-call | tf_op jit(solution)/shard_map/pallas_call | solution.py:414
  35.5 0.9 %collective-permute-start.12 = (bf16[48,1536]{1,0:T(8,128)(2,1)S(1)}, bf16[48,1536]{1,0:T(8,128)(2,1)S(1)}, u32[]{:S(2)}, u32[]{:S(2)}) collective-permute-start(bf16[48,1536]{1,0:T(8,128)(2,1)S(1)} %get-tuple-element.53), channel_id=1, source_target_pairs={{0,18},{2,16},{4,22},{6,20},{8,26},{10,24},{12,30},{14,28},{16,2},... | collective-permute-start | bytes 442376 | tf_op jit(solution)/shard_map/ppermute | solution.py:112
  36.4 0.5 collective-permute-start.13
  36.9 1.3 %collective-permute-start.14 = (bf16[48,1536]{1,0:T(8,128)(2,1)S(1)}, bf16[48,1536]{1,0:T(8,128)(2,1)S(1)}, u32[]{:S(2)}, u32[]{:S(2)}) collective-permute-start(bf16[48,1536]{1,0:T(8,128)(2,1)S(1)} %get-tuple-element.55), channel_id=1, source_target_pairs={{0,16},{16,0},{1,17},{17,1},{2,18},{18,2},{3,19},{19,3},{4,20},{20... | collective-permute-start | bytes 442376 | tf_op jit(solution)/shard_map/ppermute | solution.py:106
  38.3 0.0 collective-permute-done.15.a1_ref
  38.3 3.7 %shard_map.117 = (bf16[192,2048]{1,0:T(8,128)(2,1)S(1)}, bf16[192,2048]{1,0:T(8,128)(2,1)S(1)}, bf16[48,1536]{1,0:T(8,128)(2,1)S(1)}, bf16[48,1536]{1,0:T(8,128)...) custom-call(bf16[192,2048]{1,0:T(8,128)(2,1)S(1)} %get-tuple-element.52.a0_ref, ...), custom_call_target="tpu_custom_call" | custom-call | flops 2415919104 | bytes 6881280 | tf_op jit(solution)/shard_map/pallas_call | solution.py:442
  41.9 1.0 %collective-permute-start.16 = (bf16[48,1536]{1,0:T(8,128)(2,1)S(1)}, bf16[48,1536]{1,0:T(8,128)(2,1)S(1)}, u32[]{:S(2)}, u32[]{:S(2)}) collective-permute-start(bf16[48,1536]{1,0:T(8,128)(2,1)S(1)} %get-tuple-element.59), channel_id=1, source_target_pairs={{0,18},{2,16},{4,22},{6,20},{8,26},{10,24},{12,30},{14,28},{16,2},... | collective-permute-start | bytes 442376 | tf_op jit(solution)/shard_map/ppermute | solution.py:112
  43.0 0.4 collective-permute-start.17
  43.3 0.0 collective-permute-done.12.refs_0_
  43.3 1.3 %collective-permute-start.18 = (bf16[48,1536]{1,0:T(8,128)(2,1)S(1)}, bf16[48,1536]{1,0:T(8,128)(2,1)S(1)}, u32[]{:S(2)}, u32[]{:S(2)}) collective-permute-start(bf16[48,1536]{1,0:T(8,128)(2,1)S(1)} %get-tuple-element.61), channel_id=1, source_target_pairs={{0,16},{16,0},{1,17},{17,1},{2,18},{18,2},{3,19},{19,3},{4,20},{20... | collective-permute-start | bytes 442376 | tf_op jit(solution)/shard_map/ppermute | solution.py:106
  44.7 5.1 %shard_map.120 = (bf16[1536,2048]{1,0:T(8,128)(2,1)}, bf16[1536,2048]{1,0:T(8,128)(2,1)}) custom-call(bf16[192,1536]{1,0:T(8,128)(2,1)S(1)} %get-tuple-element.46.x_ref.refs_0_, bf16[192,2048]{1,0:T(8,128)(2,1)S(1)} %get-tuple-element.69.refs_1_, bf16[192,2048]{1,0:T(8,128)(2,1)S(1)} %get-tuple-element.70.refs_2_), custom_call_target="tpu_custom_call" | custom-call | flops 2415919104 | bytes 14745600 | tf_op jit(solution)/shard_map/pallas_call | solution.py:478
  49.8 0.0 copy-start
  49.8 0.0 copy-start.1
  49.8 0.0 collective-permute-done.13.refs_1_
  49.8 0.0 collective-permute-done.14.refs_2_
  49.8 0.0 collective-permute-done.16.refs_4_
  49.9 0.0 collective-permute-done.17.refs_5_
  49.9 1.8 %collective-permute-done.18.refs_6_ = bf16[48,1536]{1,0:T(8,128)(2,1)S(1)} collective-permute-done((bf16[48,1536]{1,0:T(8,128)(2,1)S(1)}, bf16[48,1536]{1,0:T(8,128)(2,1)S(1)}, u32[]{:S(2)}, u32[]{:S(2)}) %collective-permute-start.18) | collective-permute-done | bytes 147488 | tf_op jit(solution)/shard_map/ppermute | solution.py:106
  51.6 0.3 shard_map.118
  52.0 3.5 %collective-permute-start.19 = (bf16[24,1536]{1,0:T(8,128)(2,1)S(1)}, bf16[24,1536]{1,0:T(8,128)(2,1)S(1)}, u32[]{:S(2)}, u32[]{:S(2)}) collective-permute-start(bf16[24,1536]{1,0:T(8,128)(2,1)S(1)} %get-tuple-element.63), channel_id=1, source_target_pairs={{0,12},{1,28},{2,14},{3,30},{4,8},{5,24},{6,10},{7,26},{8,4},{9,20... | collective-permute-start | bytes 221192 | tf_op jit(solution)/shard_map/ppermute | solution.py:507
  55.4 0.0 collective-permute-start.20
  55.4 1.9 %collective-permute-start.21 = (bf16[24,1536]{1,0:T(8,128)(2,1)S(1)}, bf16[24,1536]{1,0:T(8,128)(2,1)S(1)}, u32[]{:S(2)}, u32[]{:S(2)}) collective-permute-start(bf16[24,1536]{1,0:T(8,128)(2,1)S(1)} %get-tuple-element.65), channel_id=1, source_target_pairs={{0,4},{1,20},{2,6},{3,22},{4,0},{5,16},{6,2},{7,18},{8,12},{9,28},... | collective-permute-start | bytes 221192 | tf_op jit(solution)/shard_map/ppermute | solution.py:507
  57.3 2.8 %collective-permute-start.22 = (bf16[24,1536]{1,0:T(8,128)(2,1)S(1)}, bf16[24,1536]{1,0:T(8,128)(2,1)S(1)}, u32[]{:S(2)}, u32[]{:S(2)}) collective-permute-start(bf16[24,1536]{1,0:T(8,128)(2,1)S(1)} %get-tuple-element.66), channel_id=1, source_target_pairs={{0,0},{1,16},{2,2},{3,18},{4,4},{5,20},{6,6},{7,22},{8,8},{9,24},{... | collective-permute-start | bytes 221192 | tf_op jit(solution)/shard_map/ppermute | solution.py:507
  60.1 3.2 %shard_map.121 = bf16[1536,2048]{1,0:T(8,128)(2,1)} custom-call(bf16[192,1536]{1,0:T(8,128)(2,1)S(1)} %get-tuple-element.73.refs_0_, bf16[192,2048]{1,0:T(8,128)(2,1)S(1)} %get-tuple-element.74.refs_1_), custom_call_target="tpu_custom_call" | custom-call | flops 1207959552 | bytes 7667712 | tf_op jit(solution)/shard_map/pallas_call | solution.py:478
  63.3 0.0 collective-permute-done.19.refs_0_
  63.3 0.0 collective-permute-done.20.refs_1_
  63.4 0.0 collective-permute-done.21.refs_2_
  63.4 0.0 collective-permute-done.22.refs_3_
  63.4 1.1 %shard_map.119 = (bf16[16,1536]{1,0:T(8,128)(2,1)}, bf16[16,1536]{1,0:T(8,128)(2,1)}) custom-call(bf16[24,1536]{1,0:T(8,128)(2,1)S(1)} %collective-permute-done.19.refs_0_, bf16[24,1536]{1,0:T(8,128)(2,1)S(1)} %collective-permute-done.20.refs_1_, bf16[24,1536]{1,0:T(8,128)(2,1)S(1)} %collective-permute-done.21.refs_2_, ...), custom_call_target="tpu_custom_call" | custom-call | bytes 393216 | tf_op jit(solution)/shard_map/pallas_call | solution.py:352
  (8 shorter events, 0.0 us)
Async XLA Ops:
  1.9 9.9 %collective-permute-start = (bf16[24,1536]{1,0:T(8,128)(2,1)S(1)}, bf16[24,1536]{1,0:T(8,128)(2,1)S(1)}, u32[]{:S(2)}, u32[]{:S(2)}) collective-permute-start(bf16[24,1536]{1,0:T(8,128)(2,1)S(1)} %get-tuple-element.40), channel_id=1, source_target_pairs={{0,8},{1,24},{2,10},{3,26},{4,12},{5,28},{6,14},{7,30},{8,0},{9,16... | collective-permute-start | bytes 221192 | tf_op jit(solution)/shard_map/ppermute | solution.py:507
  6.7 6.6 %collective-permute-start.1 = (bf16[24,1536]{1,0:T(8,128)(2,1)S(1)}, bf16[24,1536]{1,0:T(8,128)(2,1)S(1)}, u32[]{:S(2)}, u32[]{:S(2)}) collective-permute-start(bf16[24,1536]{1,0:T(8,128)(2,1)S(1)} %get-tuple-element.41), channel_id=1, source_target_pairs={{0,12},{1,28},{2,14},{3,30},{4,8},{5,24},{6,10},{7,26},{8,4},{9,20... | collective-permute-start | bytes 221192 | tf_op jit(solution)/shard_map/ppermute | solution.py:507
  7.7 5.5 %collective-permute-start.2 = (bf16[24,1536]{1,0:T(8,128)(2,1)S(1)}, bf16[24,1536]{1,0:T(8,128)(2,1)S(1)}, u32[]{:S(2)}, u32[]{:S(2)}) collective-permute-start(bf16[24,1536]{1,0:T(8,128)(2,1)S(1)} %get-tuple-element.42), channel_id=1, source_target_pairs={{0,4},{1,20},{2,6},{3,22},{4,0},{5,16},{6,2},{7,18},{8,12},{9,28},... | collective-permute-start | bytes 221192 | tf_op jit(solution)/shard_map/ppermute | solution.py:507
  8.2 5.9 %collective-permute-start.3 = (bf16[24,1536]{1,0:T(8,128)(2,1)S(1)}, bf16[24,1536]{1,0:T(8,128)(2,1)S(1)}, u32[]{:S(2)}, u32[]{:S(2)}) collective-permute-start(bf16[24,1536]{1,0:T(8,128)(2,1)S(1)} %get-tuple-element.43.refs_4_), channel_id=1, source_target_pairs={{0,0},{1,16},{2,2},{3,18},{4,4},{5,20},{6,6},{7,22},{8,8},{9,24},{... | collective-permute-start | bytes 221192 | tf_op jit(solution)/shard_map/ppermute | solution.py:507
  14.0 15.2 %slice-start.2 = ((s8[6291456]{0:T(1024)(128)(4,1)}), s8[4194304]{0:T(1024)(128)(4,1)S(1)}, s32[]{:S(2)}) async-start(s8[6291456]{0:T(1024)(128)(4,1)} %bitcast.4), calls=%async_computation.2 | async-start | bytes 8388608
  14.3 6.3 %collective-permute-start.4 = (bf16[48,1536]{1,0:T(8,128)(2,1)S(1)}, bf16[48,1536]{1,0:T(8,128)(2,1)S(1)}, u32[]{:S(2)}, u32[]{:S(2)}) collective-permute-start(bf16[48,1536]{1,0:T(8,128)(2,1)S(1)} %get-tuple-element.44.refs_1_.refs_3_.refs_5_), channel_id=1, source_target_pairs={{0,18},{2,16},{4,22},{6,20},{8,26},{10,24},{12,30},{14,28},{16,2},... | collective-permute-start | bytes 442376 | tf_op jit(solution)/shard_map/ppermute | solution.py:112
  14.3 9.1 %collective-permute-start.5 = (bf16[48,1536]{1,0:T(8,128)(2,1)S(1)}, bf16[48,1536]{1,0:T(8,128)(2,1)S(1)}, u32[]{:S(2)}, u32[]{:S(2)}) collective-permute-start(bf16[48,1536]{1,0:T(8,128)(2,1)S(1)} %get-tuple-element.44.refs_1_.refs_3_.refs_5_), channel_id=1, source_target_pairs={{0,2},{2,0},{4,6},{6,4},{8,10},{10,8},{12,14},{14,12},{1,3},{3,1},... | collective-permute-start | bytes 442376 | tf_op jit(solution)/shard_map/ppermute | solution.py:102
  15.6 8.6 %collective-permute-start.6 = (bf16[48,1536]{1,0:T(8,128)(2,1)S(1)}, bf16[48,1536]{1,0:T(8,128)(2,1)S(1)}, u32[]{:S(2)}, u32[]{:S(2)}) collective-permute-start(bf16[48,1536]{1,0:T(8,128)(2,1)S(1)} %get-tuple-element.44.refs_1_.refs_3_.refs_5_), channel_id=1, source_target_pairs={{0,16},{16,0},{1,17},{17,1},{2,18},{18,2},{3,19},{19,3},{4,20},{20... | collective-permute-start | bytes 442376 | tf_op jit(solution)/shard_map/ppermute | solution.py:106
  17.0 12.2 %slice-start.3 = ((s8[6291456]{0:T(1024)(128)(4,1)}), s8[2097152]{0:T(1024)(128)(4,1)S(1)}, s32[]{:S(2)}) async-start(s8[6291456]{0:T(1024)(128)(4,1)} %bitcast.4), calls=%async_computation.3 | async-start | bytes 4194304
  17.0 13.7 %collective-permute-start.9 = (bf16[48,1536]{1,0:T(8,128)(2,1)S(1)}, bf16[48,1536]{1,0:T(8,128)(2,1)S(1)}, u32[]{:S(2)}, u32[]{:S(2)}) collective-permute-start(bf16[48,1536]{1,0:T(8,128)(2,1)S(1)} %get-tuple-element.51.refs_3_), channel_id=1, source_target_pairs={{0,18},{2,16},{4,22},{6,20},{8,26},{10,24},{12,30},{14,28},{16,2},... | collective-permute-start | bytes 442376 | tf_op jit(solution)/shard_map/ppermute | solution.py:112
  17.9 12.8 %collective-permute-start.10 = (bf16[48,1536]{1,0:T(8,128)(2,1)S(1)}, bf16[48,1536]{1,0:T(8,128)(2,1)S(1)}, u32[]{:S(2)}, u32[]{:S(2)}) collective-permute-start(bf16[48,1536]{1,0:T(8,128)(2,1)S(1)} %get-tuple-element.51.refs_3_), channel_id=1, source_target_pairs={{0,2},{2,0},{4,6},{6,4},{8,10},{10,8},{12,14},{14,12},{1,3},{3,1},... | collective-permute-start | bytes 442376 | tf_op jit(solution)/shard_map/ppermute | solution.py:102
  20.6 10.1 %collective-permute-start.11 = (bf16[48,1536]{1,0:T(8,128)(2,1)S(1)}, bf16[48,1536]{1,0:T(8,128)(2,1)S(1)}, u32[]{:S(2)}, u32[]{:S(2)}) collective-permute-start(bf16[48,1536]{1,0:T(8,128)(2,1)S(1)} %get-tuple-element.51.refs_3_), channel_id=1, source_target_pairs={{0,16},{16,0},{1,17},{17,1},{2,18},{18,2},{3,19},{19,3},{4,20},{20... | collective-permute-start | bytes 442376 | tf_op jit(solution)/shard_map/ppermute | solution.py:106
  23.4 7.3 %slice-start = ((s8[6291456]{0:T(1024)(128)(4,1)}), s8[4194304]{0:T(1024)(128)(4,1)S(1)}, s32[]{:S(2)}) async-start(s8[6291456]{0:T(1024)(128)(4,1)} %bitcast.2), calls=%async_computation | async-start | bytes 8388608
  25.6 7.1 %collective-permute-start.7 = (bf16[192,2048]{1,0:T(8,128)(2,1)S(1)}, bf16[192,2048]{1,0:T(8,128)(2,1)S(1)}, u32[]{:S(2)}, u32[]{:S(2)}) collective-permute-start(bf16[192,2048]{1,0:T(8,128)(2,1)S(1)} %get-tuple-element.45.g0_ref), channel_id=1, source_target_pairs={{0,1},{1,0},{2,3},{3,2},{4,5},{5,4},{6,7},{7,6},{8,9},{9,8},{10,11... | collective-permute-start | bytes 2359304 | tf_op jit(solution)/shard_map/ppermute | solution.py:494
  29.2 1.6 %slice-start.1 = ((s8[6291456]{0:T(1024)(128)(4,1)}), s8[2097152]{0:T(1024)(128)(4,1)S(1)}, s32[]{:S(2)}) async-start(s8[6291456]{0:T(1024)(128)(4,1)} %bitcast.2), calls=%async_computation.1 | async-start | bytes 4194304
  30.6 2.4 %collective-permute-start.8 = (bf16[192,2048]{1,0:T(8,128)(2,1)S(1)}, bf16[192,2048]{1,0:T(8,128)(2,1)S(1)}, u32[]{:S(2)}, u32[]{:S(2)}) collective-permute-start(bf16[192,2048]{1,0:T(8,128)(2,1)S(1)} %shard_map.114.u0_ref.refs_5_), channel_id=1, source_target_pairs={{0,1},{1,0},{2,3},{3,2},{4,5},{5,4},{6,7},{7,6},{8,9},{9,8},{10,11... | collective-permute-start | bytes 2359304 | tf_op jit(solution)/shard_map/ppermute | solution.py:494
  32.2 6.1 %collective-permute-start.15 = (bf16[192,2048]{1,0:T(8,128)(2,1)S(1)}, bf16[192,2048]{1,0:T(8,128)(2,1)S(1)}, u32[]{:S(2)}, u32[]{:S(2)}) collective-permute-start(bf16[192,2048]{1,0:T(8,128)(2,1)S(1)} %get-tuple-element.52.a0_ref), channel_id=1, source_target_pairs={{0,1},{1,0},{2,3},{3,2},{4,5},{5,4},{6,7},{7,6},{8,9},{9,8},{10,11... | collective-permute-start | bytes 2359304 | tf_op jit(solution)/shard_map/ppermute | solution.py:494
  35.5 7.8 %collective-permute-start.12 = (bf16[48,1536]{1,0:T(8,128)(2,1)S(1)}, bf16[48,1536]{1,0:T(8,128)(2,1)S(1)}, u32[]{:S(2)}, u32[]{:S(2)}) collective-permute-start(bf16[48,1536]{1,0:T(8,128)(2,1)S(1)} %get-tuple-element.53), channel_id=1, source_target_pairs={{0,18},{2,16},{4,22},{6,20},{8,26},{10,24},{12,30},{14,28},{16,2},... | collective-permute-start | bytes 442376 | tf_op jit(solution)/shard_map/ppermute | solution.py:112
  36.4 13.4 %collective-permute-start.13 = (bf16[48,1536]{1,0:T(8,128)(2,1)S(1)}, bf16[48,1536]{1,0:T(8,128)(2,1)S(1)}, u32[]{:S(2)}, u32[]{:S(2)}) collective-permute-start(bf16[48,1536]{1,0:T(8,128)(2,1)S(1)} %get-tuple-element.54), channel_id=1, source_target_pairs={{0,2},{2,0},{4,6},{6,4},{8,10},{10,8},{12,14},{14,12},{1,3},{3,1},... | collective-permute-start | bytes 442376 | tf_op jit(solution)/shard_map/ppermute | solution.py:102
  36.9 12.9 %collective-permute-start.14 = (bf16[48,1536]{1,0:T(8,128)(2,1)S(1)}, bf16[48,1536]{1,0:T(8,128)(2,1)S(1)}, u32[]{:S(2)}, u32[]{:S(2)}) collective-permute-start(bf16[48,1536]{1,0:T(8,128)(2,1)S(1)} %get-tuple-element.55), channel_id=1, source_target_pairs={{0,16},{16,0},{1,17},{17,1},{2,18},{18,2},{3,19},{19,3},{4,20},{20... | collective-permute-start | bytes 442376 | tf_op jit(solution)/shard_map/ppermute | solution.py:106
  41.9 7.9 %collective-permute-start.16 = (bf16[48,1536]{1,0:T(8,128)(2,1)S(1)}, bf16[48,1536]{1,0:T(8,128)(2,1)S(1)}, u32[]{:S(2)}, u32[]{:S(2)}) collective-permute-start(bf16[48,1536]{1,0:T(8,128)(2,1)S(1)} %get-tuple-element.59), channel_id=1, source_target_pairs={{0,18},{2,16},{4,22},{6,20},{8,26},{10,24},{12,30},{14,28},{16,2},... | collective-permute-start | bytes 442376 | tf_op jit(solution)/shard_map/ppermute | solution.py:112
  43.0 6.9 %collective-permute-start.17 = (bf16[48,1536]{1,0:T(8,128)(2,1)S(1)}, bf16[48,1536]{1,0:T(8,128)(2,1)S(1)}, u32[]{:S(2)}, u32[]{:S(2)}) collective-permute-start(bf16[48,1536]{1,0:T(8,128)(2,1)S(1)} %get-tuple-element.60), channel_id=1, source_target_pairs={{0,2},{2,0},{4,6},{6,4},{8,10},{10,8},{12,14},{14,12},{1,3},{3,1},... | collective-permute-start | bytes 442376 | tf_op jit(solution)/shard_map/ppermute | solution.py:102
  43.3 8.3 %collective-permute-start.18 = (bf16[48,1536]{1,0:T(8,128)(2,1)S(1)}, bf16[48,1536]{1,0:T(8,128)(2,1)S(1)}, u32[]{:S(2)}, u32[]{:S(2)}) collective-permute-start(bf16[48,1536]{1,0:T(8,128)(2,1)S(1)} %get-tuple-element.61), channel_id=1, source_target_pairs={{0,16},{16,0},{1,17},{17,1},{2,18},{18,2},{3,19},{19,3},{4,20},{20... | collective-permute-start | bytes 442376 | tf_op jit(solution)/shard_map/ppermute | solution.py:106
  49.8 13.6 %copy-start = (s32[16,2]{0,1:T(2,128)S(1)}, s32[16,2]{0,1:T(2,128)}, u32[]{:S(2)}) copy-start(s32[16,2]{0,1:T(2,128)} %param.9) | copy-start | bytes 388
  49.8 13.6 %copy-start.1 = (f32[16,2]{0,1:T(2,128)S(1)}, f32[16,2]{0,1:T(2,128)}, u32[]{:S(2)}) copy-start(f32[16,2]{0,1:T(2,128)} %param.10) | copy-start | bytes 388
  52.0 11.4 %collective-permute-start.19 = (bf16[24,1536]{1,0:T(8,128)(2,1)S(1)}, bf16[24,1536]{1,0:T(8,128)(2,1)S(1)}, u32[]{:S(2)}, u32[]{:S(2)}) collective-permute-start(bf16[24,1536]{1,0:T(8,128)(2,1)S(1)} %get-tuple-element.63), channel_id=1, source_target_pairs={{0,12},{1,28},{2,14},{3,30},{4,8},{5,24},{6,10},{7,26},{8,4},{9,20... | collective-permute-start | bytes 221192 | tf_op jit(solution)/shard_map/ppermute | solution.py:507
  55.4 7.9 %collective-permute-start.20 = (bf16[24,1536]{1,0:T(8,128)(2,1)S(1)}, bf16[24,1536]{1,0:T(8,128)(2,1)S(1)}, u32[]{:S(2)}, u32[]{:S(2)}) collective-permute-start(bf16[24,1536]{1,0:T(8,128)(2,1)S(1)} %get-tuple-element.64), channel_id=1, source_target_pairs={{0,8},{1,24},{2,10},{3,26},{4,12},{5,28},{6,14},{7,30},{8,0},{9,16... | collective-permute-start | bytes 221192 | tf_op jit(solution)/shard_map/ppermute | solution.py:507
  55.4 7.9 %collective-permute-start.21 = (bf16[24,1536]{1,0:T(8,128)(2,1)S(1)}, bf16[24,1536]{1,0:T(8,128)(2,1)S(1)}, u32[]{:S(2)}, u32[]{:S(2)}) collective-permute-start(bf16[24,1536]{1,0:T(8,128)(2,1)S(1)} %get-tuple-element.65), channel_id=1, source_target_pairs={{0,4},{1,20},{2,6},{3,22},{4,0},{5,16},{6,2},{7,18},{8,12},{9,28},... | collective-permute-start | bytes 221192 | tf_op jit(solution)/shard_map/ppermute | solution.py:507
  57.3 6.0 %collective-permute-start.22 = (bf16[24,1536]{1,0:T(8,128)(2,1)S(1)}, bf16[24,1536]{1,0:T(8,128)(2,1)S(1)}, u32[]{:S(2)}, u32[]{:S(2)}) collective-permute-start(bf16[24,1536]{1,0:T(8,128)(2,1)S(1)} %get-tuple-element.66), channel_id=1, source_target_pairs={{0,0},{1,16},{2,2},{3,18},{4,4},{5,20},{6,6},{7,22},{8,8},{9,24},{... | collective-permute-start | bytes 221192 | tf_op jit(solution)/shard_map/ppermute | solution.py:507
